TPU v7x, 128 devices: a whole 4x4x4 slice. The times are simulated.
128 devices in a mesh: gx: 16 (over z, x), gy: 8 (over y, core).
Axes of the slice: x: 4, y: 4, z: 4, core: 2. Of those that a mesh axis runs over, the one named last changes fastest.
Arguments:
- initial_head: float32 [10, 512, 1024], P(None, 'gx', 'gy'), may hold values from -6 to 6
- conductivity: float32 [10, 512, 1024], P(None, 'gx', 'gy'), may hold values from 0.3 to 3
- source_rate: float32 [10, 512, 1024], P(None, 'gx', 'gy'), may hold values from -6 to 6
- storage_term: float32 [10, 512, 1024], P(None, 'gx', 'gy'), may hold values from 0.05 to 0.5
- bed_conduct: float32 [512, 1024], P('gx', 'gy'), may hold values from 0.001 to 0.01
- row_cells: int32 [128, 256, 128], P(('gx', 'gy')), may hold values from 0 to 4096, as said below
- row_reach: int32 [128, 256], P(('gx', 'gy')), may hold values from 0 to 255
- river_section: float32 [128, 256], P(('gx', 'gy')), may hold values from -6 to 6
- bed_depth: float32 [128, 256], P(('gx', 'gy')), may hold values from 0.5 to 2
- route_inverse: float32 [128, 256, 256], P(('gx', 'gy')), as said below
- retention: float32 [128], P(('gx', 'gy')), may hold values from 0.9 to 1
- chain_heads: int32 [128], P(('gx', 'gy')), may hold values 0 or 1
Outputs:
- head_field: float32 [10, 512, 1024], P(None, 'gx', 'gy')
- reach_flow: float32 [128, 256], P(('gx', 'gy'))
Inputs may be any that keep to these rules, and one draw needn't show every extreme that they name: `row_cells`: each row lists 1 to 128 cells of the sender's tile followed by the empty index 4096; row 0 of every sender is full. `route_inverse`: each block's matrix is lower triangular with a unit diagonal.
All inputs are finite; a program needn't handle non-finite values. No bound on the sum of `chain_heads` on one device may be relied on, other than what follows from the above.
Results may differ from a plain program's by a relative error of at most 0.00018.
Values sent between devices are 32-bit elements; how exact they have to be, the bound alone decides.
No kernel may reach another device: no remote copies, remote signals or barrier semaphores. Data moves between devices by JAX's collectives and lax.ppermute only.
A program may use at most 64 MiB of HBM per device.

v0:
```python
import jax
import jax.numpy as jnp
from jax import lax
from jax.sharding import PartitionSpec as P

SWEEPS = 8


def extended(block, sides, width):
    for axis, dim in sides:
        count = lax.axis_size(axis)
        forward = [(i, i + 1) for i in range(count - 1)]
        backward = [(target, source) for source, target in forward]
        low = lax.ppermute(
            lax.slice_in_dim(block, block.shape[dim] - width, None, axis=dim), axis, forward
        )
        high = lax.ppermute(lax.slice_in_dim(block, 0, width, axis=dim), axis, backward)
        block = jnp.concatenate([low, block, high], axis=dim)
    return block


def entering(value, axis, join, neutral):
    count, mine = (lax.axis_size(axis), lax.axis_index(axis))
    pieces = jax.tree.map(lambda part: lax.all_gather(part, axis), value)
    so_far = jax.tree.map(
        lambda part, zero: jnp.full_like(part, 0) + jnp.asarray(zero, part.dtype), value, neutral
    )

    def hop(position, so_far):
        longer = join(so_far, jax.tree.map(lambda part: part[position], pieces))
        return jax.tree.map(lambda new, old: jnp.where(position < mine, new, old), longer, so_far)

    return lax.fori_loop(0, count - 1, hop, so_far)


def relax(head_pad, cond_pad, mask_pad, source, storage):
    height = head_pad.shape[1] - 2
    breadth = head_pad.shape[2] - 2
    cond_mid = cond_pad[:, 1:-1, 1:-1]
    head_mid = head_pad[:, 1:-1, 1:-1]
    mask_mid = mask_pad[:, 1:-1, 1:-1]
    numerator = source
    denominator = storage
    for offset_x, offset_y in ((0, 1), (2, 1), (1, 0), (1, 2)):
        cond_near = cond_pad[:, offset_x : offset_x + height, offset_y : offset_y + breadth]
        head_near = head_pad[:, offset_x : offset_x + height, offset_y : offset_y + breadth]
        mask_near = mask_pad[:, offset_x : offset_x + height, offset_y : offset_y + breadth]
        face = 0.5 * (cond_mid + cond_near) * mask_near
        numerator = numerator + face * head_near
        denominator = denominator + face
    vertical = 0.5 * (cond_mid[1:] + cond_mid[:-1])
    nothing = jnp.zeros_like(cond_mid[:1])
    numerator = (
        numerator
        + jnp.concatenate([nothing, vertical * head_mid[:-1]], 0)
        + jnp.concatenate([vertical * head_mid[1:], nothing], 0)
    )
    denominator = (
        denominator
        + jnp.concatenate([nothing, vertical], 0)
        + jnp.concatenate([vertical, nothing], 0)
    )
    return numerator / (denominator + (1.0 - mask_mid)) * mask_mid


def inside_mask(margin, tile_x, tile_y):
    global_x = lax.axis_index("gx") * tile_x + jnp.arange(tile_x + 2 * margin) - margin
    global_y = lax.axis_index("gy") * tile_y + jnp.arange(tile_y + 2 * margin) - margin
    inside_x = (global_x >= 0) & (global_x < tile_x * lax.axis_size("gx"))
    inside_y = (global_y >= 0) & (global_y < tile_y * lax.axis_size("gy"))
    return (inside_x[:, None] & inside_y[None, :]).astype(jnp.float32)[None]


def compose(earlier, later):
    return (later[0] * earlier[0], later[0] * earlier[1] + later[1])


def pick_cells(cells, head_top, bed_top):
    tile_x = head_top.shape[0]
    tile_y = head_top.shape[1]
    cell_total = tile_x * tile_y
    layout = cells.shape
    blocks = cells.reshape(8, -1)

    def one_block(indices):
        usable = indices < cell_total
        row_index = jnp.minimum(indices // tile_y, tile_x - 1)
        column = indices % tile_y
        select = ((column[:, None] == jnp.arange(tile_y)[None, :]) & usable[:, None]).astype(
            jnp.float32
        )
        head_vals = jnp.sum(head_top[row_index] * select, -1)
        bed_vals = jnp.sum(bed_top[row_index] * select, -1)
        return (head_vals, bed_vals)

    head_vals, bed_vals = lax.map(one_block, blocks)
    return (head_vals.reshape(layout), bed_vals.reshape(layout))


def per_device(
    initial_head,
    conductivity,
    source_rate,
    storage_term,
    bed_conduct,
    row_cells,
    row_reach,
    river_section,
    bed_depth,
    route_inverse,
    retention,
    chain_heads,
):
    tile_x = initial_head.shape[1]
    tile_y = initial_head.shape[2]
    mask_pad = inside_mask(1, tile_x, tile_y)
    cond_pad = extended(conductivity, (("gx", 1), ("gy", 2)), 1)
    head_now = initial_head
    for sweep_index in range(SWEEPS):
        head_pad = extended(head_now, (("gx", 1), ("gy", 2)), 1)
        head_now = relax(head_pad, cond_pad, mask_pad, source_rate, storage_term)
    devices = lax.axis_size("gx") * lax.axis_size("gy")
    slot_count = row_cells.shape[2]
    row_total = row_cells.shape[1]
    per_peer = row_total // devices
    reach_count = river_section.shape[1]
    cells = row_cells[0].reshape(devices, per_peer, slot_count)
    head_rows, bed_rows = pick_cells(cells, head_now[0], bed_conduct)
    one_hot = (row_reach[0][:, None] == jnp.arange(reach_count)[None, :]).astype(jnp.float32)
    levels = jnp.dot(
        one_hot, jnp.stack([river_section[0], bed_depth[0]], 1), precision=lax.Precision.HIGHEST
    )
    section_row = levels[:, 0]
    bottom_row = section_row - levels[:, 1]
    heads_in, beds_in = (
        lax.all_to_all(head_rows, ("gx", "gy"), split_axis=0, concat_axis=0, tiled=True),
        lax.all_to_all(bed_rows, ("gx", "gy"), split_axis=0, concat_axis=0, tiled=True),
    )
    heads_in = heads_in.reshape(row_total, slot_count)
    beds_in = beds_in.reshape(row_total, slot_count)
    leak = beds_in * (jnp.maximum(heads_in, bottom_row[:, None]) - section_row[:, None])
    row_leak = jnp.sum(leak, -1)
    reach_leak = jnp.dot(row_leak, one_hot, precision=lax.Precision.HIGHEST)
    local_flow = jnp.dot(route_inverse[0], reach_leak, precision=lax.Precision.HIGHEST)
    carry = retention * (1.0 - chain_heads.astype(jnp.float32))
    last_flow = local_flow[-1:]
    prefix = entering(
        (carry, last_flow),
        ("gx", "gy"),
        compose,
        (jnp.ones((1,), jnp.float32), jnp.zeros((1,), jnp.float32)),
    )
    outlet_before = prefix[1]
    inflow = carry * outlet_before
    reach_flow = (local_flow + inflow)[None]
    return (head_now, reach_flow)


def solution(mesh):
    placed = (
        P(None, "gx", "gy"),
        P(None, "gx", "gy"),
        P(None, "gx", "gy"),
        P(None, "gx", "gy"),
        P("gx", "gy"),
        P(("gx", "gy"), None, None),
        P(("gx", "gy"), None),
        P(("gx", "gy"), None),
        P(("gx", "gy"), None),
        P(("gx", "gy"), None, None),
        P(("gx", "gy")),
        P(("gx", "gy")),
    )
    return jax.shard_map(
        per_device,
        mesh=mesh,
        in_specs=placed,
        out_specs=(P(None, "gx", "gy"), P(("gx", "gy"), None)),
        check_vma=False,
    )
```

profile of v0, /device:TPU:1, one launch (start us, length us, event | category | flops | bytes accessed | tf_op | source)
XLA Modules:
  0.0 765.1 jit_solution(9597967608266066180)
XLA Ops:
  16.2 4.6 collective-permute-start.4
  29.2 4.4 collective-permute-done.7
  48.8 4.4 collective-permute-done.11
  59.0 5.4 collective-permute-done.13
  70.2 4.4 collective-permute-done.15
  74.9 5.7 collective-permute-start.16
  91.0 4.4 collective-permute-done.19
  109.8 4.4 collective-permute-done.23
  128.7 4.4 collective-permute-done.27
  166.5 4.4 collective-permute-done.35
  171.8 240.3 %while.27 = (s32[]{:T(128)}, f32[8,4096]{1,0:T(8,128)S(1)}, f32[8,4096]{1,0:T(8,128)S(1)}, s32[8,4096]{1,0:T(8,128)S(1)}, f32[32,128]{1,0:T(8,128)S(1)}, /*index=5*/f32[32,128]{1,0:T(8,128)S(1)}, s32[]{:T(128)}, s32[]{:T(128)}) while((s32[]{:T(128)}, f32[8,4096]{1,0:T(8,128)S(1)}, f32[8,4096]{1,0:T(8,128)S(1)}, s32[8,4096]{1,0:T(8,128)S(1)}, ...), condition=%wide.region_3.4_spmd, body=%wide.region_0.3_spmd.sunk | while | flops 3268610 | bytes 12869729 | solution.py:96
  171.9 10.8 %gather_fusion = f32[4096,128]{1,0:T(8,128)S(1)} fusion(f32[32,128]{1,0:T(8,128)S(1)} %get-tuple-element.375, s32[4096]{0:T(1024)S(1)} %broadcast_clamp_fusion.2), kind=kCustom, calls=%fused_computation.1.clone.1 | custom fusion | bytes 4210688 | tf_op jit(solution)/shard_map/while/body/eval_jaxpr/gather | solution.py:93
  182.7 14.2 %gather_fusion.1 = f32[4096,128]{1,0:T(8,128)} fusion(f32[32,128]{1,0:T(8,128)S(1)} %get-tuple-element.374, s32[4096]{0:T(1024)S(1)} %broadcast_clamp_fusion.2), kind=kCustom, calls=%fused_computation.clone.1 | custom fusion | bytes 4210688 | tf_op jit(solution)/shard_map/while/body/eval_jaxpr/gather | solution.py:92
  201.9 10.8 %gather_fusion = f32[4096,128]{1,0:T(8,128)S(1)} fusion(f32[32,128]{1,0:T(8,128)S(1)} %get-tuple-element.375, s32[4096]{0:T(1024)S(1)} %broadcast_clamp_fusion.2), kind=kCustom, calls=%fused_computation.1.clone.1 | custom fusion | bytes 4210688 | tf_op jit(solution)/shard_map/while/body/eval_jaxpr/gather | solution.py:93
  212.7 14.2 %gather_fusion.1 = f32[4096,128]{1,0:T(8,128)} fusion(f32[32,128]{1,0:T(8,128)S(1)} %get-tuple-element.374, s32[4096]{0:T(1024)S(1)} %broadcast_clamp_fusion.2), kind=kCustom, calls=%fused_computation.clone.1 | custom fusion | bytes 4210688 | tf_op jit(solution)/shard_map/while/body/eval_jaxpr/gather | solution.py:92
  232.0 10.8 %gather_fusion = f32[4096,128]{1,0:T(8,128)S(1)} fusion(f32[32,128]{1,0:T(8,128)S(1)} %get-tuple-element.375, s32[4096]{0:T(1024)S(1)} %broadcast_clamp_fusion.2), kind=kCustom, calls=%fused_computation.1.clone.1 | custom fusion | bytes 4210688 | tf_op jit(solution)/shard_map/while/body/eval_jaxpr/gather | solution.py:93
  242.8 14.2 %gather_fusion.1 = f32[4096,128]{1,0:T(8,128)} fusion(f32[32,128]{1,0:T(8,128)S(1)} %get-tuple-element.374, s32[4096]{0:T(1024)S(1)} %broadcast_clamp_fusion.2), kind=kCustom, calls=%fused_computation.clone.1 | custom fusion | bytes 4210688 | tf_op jit(solution)/shard_map/while/body/eval_jaxpr/gather | solution.py:92
  262.0 10.8 %gather_fusion = f32[4096,128]{1,0:T(8,128)S(1)} fusion(f32[32,128]{1,0:T(8,128)S(1)} %get-tuple-element.375, s32[4096]{0:T(1024)S(1)} %broadcast_clamp_fusion.2), kind=kCustom, calls=%fused_computation.1.clone.1 | custom fusion | bytes 4210688 | tf_op jit(solution)/shard_map/while/body/eval_jaxpr/gather | solution.py:93
  272.8 14.2 %gather_fusion.1 = f32[4096,128]{1,0:T(8,128)} fusion(f32[32,128]{1,0:T(8,128)S(1)} %get-tuple-element.374, s32[4096]{0:T(1024)S(1)} %broadcast_clamp_fusion.2), kind=kCustom, calls=%fused_computation.clone.1 | custom fusion | bytes 4210688 | tf_op jit(solution)/shard_map/while/body/eval_jaxpr/gather | solution.py:92
  292.1 10.8 %gather_fusion = f32[4096,128]{1,0:T(8,128)S(1)} fusion(f32[32,128]{1,0:T(8,128)S(1)} %get-tuple-element.375, s32[4096]{0:T(1024)S(1)} %broadcast_clamp_fusion.2), kind=kCustom, calls=%fused_computation.1.clone.1 | custom fusion | bytes 4210688 | tf_op jit(solution)/shard_map/while/body/eval_jaxpr/gather | solution.py:93
  302.9 14.2 %gather_fusion.1 = f32[4096,128]{1,0:T(8,128)} fusion(f32[32,128]{1,0:T(8,128)S(1)} %get-tuple-element.374, s32[4096]{0:T(1024)S(1)} %broadcast_clamp_fusion.2), kind=kCustom, calls=%fused_computation.clone.1 | custom fusion | bytes 4210688 | tf_op jit(solution)/shard_map/while/body/eval_jaxpr/gather | solution.py:92
  322.1 10.8 %gather_fusion = f32[4096,128]{1,0:T(8,128)S(1)} fusion(f32[32,128]{1,0:T(8,128)S(1)} %get-tuple-element.375, s32[4096]{0:T(1024)S(1)} %broadcast_clamp_fusion.2), kind=kCustom, calls=%fused_computation.1.clone.1 | custom fusion | bytes 4210688 | tf_op jit(solution)/shard_map/while/body/eval_jaxpr/gather | solution.py:93
  332.9 14.2 %gather_fusion.1 = f32[4096,128]{1,0:T(8,128)} fusion(f32[32,128]{1,0:T(8,128)S(1)} %get-tuple-element.374, s32[4096]{0:T(1024)S(1)} %broadcast_clamp_fusion.2), kind=kCustom, calls=%fused_computation.clone.1 | custom fusion | bytes 4210688 | tf_op jit(solution)/shard_map/while/body/eval_jaxpr/gather | solution.py:92
  352.1 10.8 %gather_fusion = f32[4096,128]{1,0:T(8,128)S(1)} fusion(f32[32,128]{1,0:T(8,128)S(1)} %get-tuple-element.375, s32[4096]{0:T(1024)S(1)} %broadcast_clamp_fusion.2), kind=kCustom, calls=%fused_computation.1.clone.1 | custom fusion | bytes 4210688 | tf_op jit(solution)/shard_map/while/body/eval_jaxpr/gather | solution.py:93
  362.9 14.2 %gather_fusion.1 = f32[4096,128]{1,0:T(8,128)} fusion(f32[32,128]{1,0:T(8,128)S(1)} %get-tuple-element.374, s32[4096]{0:T(1024)S(1)} %broadcast_clamp_fusion.2), kind=kCustom, calls=%fused_computation.clone.1 | custom fusion | bytes 4210688 | tf_op jit(solution)/shard_map/while/body/eval_jaxpr/gather | solution.py:92
  382.2 10.8 %gather_fusion = f32[4096,128]{1,0:T(8,128)S(1)} fusion(f32[32,128]{1,0:T(8,128)S(1)} %get-tuple-element.375, s32[4096]{0:T(1024)S(1)} %broadcast_clamp_fusion.2), kind=kCustom, calls=%fused_computation.1.clone.1 | custom fusion | bytes 4210688 | tf_op jit(solution)/shard_map/while/body/eval_jaxpr/gather | solution.py:93
  393.0 14.2 %gather_fusion.1 = f32[4096,128]{1,0:T(8,128)} fusion(f32[32,128]{1,0:T(8,128)S(1)} %get-tuple-element.374, s32[4096]{0:T(1024)S(1)} %broadcast_clamp_fusion.2), kind=kCustom, calls=%fused_computation.clone.1 | custom fusion | bytes 4210688 | tf_op jit(solution)/shard_map/while/body/eval_jaxpr/gather | solution.py:92
  412.9 11.2 %all-to-all-start = ((f32[128,2,128]{2,1,0:T(2,128)}), f32[128,2,128]{2,1,0:T(2,128)S(1)}, u32[]{:S(2)}, u32[]{:S(2)}) async-start(f32[128,2,128]{2,1,0:T(2,128)} %reshape.209), calls=%async_computation | async-start | bytes 262144 | tf_op jit(solution)/shard_map/all_to_all | solution.py:137
  424.8 9.2 %all-to-all-done = f32[128,2,128]{2,1,0:T(2,128)S(1)} async-done(((f32[128,2,128]{2,1,0:T(2,128)}), f32[128,2,128]{2,1,0:T(2,128)S(1)}, u32[]{:S(2)}, u32[]{:S(2)}) %all-to-all-start) | async-done | bytes 131104 | tf_op jit(solution)/shard_map/all_to_all | solution.py:137
  441.5 6.7 all-to-all-done.1
  449.6 62.6 %all-reduce.20 = (f32[128]{0:T(128)S(1)}, f32[128]{0:T(128)S(1)}) all-reduce(f32[128]{0:T(128)S(1)} %dynamic-update-slice, f32[128]{0:T(128)S(1)} %slice_dynamic-update-slice_fusion), channel_id=2, replica_groups=mesh['gx'=16,'gy'=8] {'gx','gy'}, use_global_device_ids=true, to_apply=%add.18 | all-reduce | flops 256 | bytes 2048
  512.2 251.6 %while.28 = (s32[]{:T(128)}, f32[1]{0:T(128)}, s32[]{:T(128)}, f32[128,1]{0,1:T(1,128)S(1)}, f32[128,1]{0,1:T(1,128)S(1)}, /*index=5*/s32[]{:T(128)}) while((s32[]{:T(128)}, f32[1]{0:T(128)}, s32[]{:T(128)}, f32[128,1]{0,1:T(1,128)S(1)}, f32[128,1]{0,1:T(1,128)S(1)}, /*index=5*/s32[]{:T(128)}) %tuple.105), condition=%wide.region_6.7_spmd, body=%wide.region_5.6_spmd.sunk | while | flops 6 | bytes 135 | solution.py:33
  (335 shorter events, 256.2 us)
Async XLA Ops:
  1.6 13.5 %collective-permute-start = (f32[10,1,128]{2,1,0:T(1,128)S(1)}, f32[10,1,128]{2,1,0:T(1,128)S(1)}, u32[]{:S(2)}, u32[]{:S(2)}) collective-permute-start(f32[10,1,128]{2,1,0:T(1,128)S(1)} %get-tuple-element.265), channel_id=1, source_target_pairs={{0,8},{8,16},{16,24},{24,32},{32,40},{40,48},{48,56},{56,64},{64,7... | collective-permute-start | bytes 15368 | tf_op jit(solution)/shard_map/ppermute | solution.py:14
  5.6 9.6 %collective-permute-start.2 = (f32[10,1,128]{2,1,0:T(1,128)S(1)}, f32[10,1,128]{2,1,0:T(1,128)S(1)}, u32[]{:S(2)}, u32[]{:S(2)}) collective-permute-start(f32[10,1,128]{2,1,0:T(1,128)S(1)} %get-tuple-element.264), channel_id=1, source_target_pairs={{8,0},{16,8},{24,16},{32,24},{40,32},{48,40},{56,48},{64,56},{72,6... | collective-permute-start | bytes 15368 | tf_op jit(solution)/shard_map/ppermute | solution.py:17
  7.7 15.1 %collective-permute-start.1 = (f32[10,1,128]{2,1,0:T(1,128)S(1)}, f32[10,1,128]{2,1,0:T(1,128)S(1)}, u32[]{:S(2)}, u32[]{:S(2)}) collective-permute-start(f32[10,1,128]{2,1,0:T(1,128)S(1)} %get-tuple-element.266), channel_id=1, source_target_pairs={{0,8},{8,16},{16,24},{24,32},{32,40},{40,48},{48,56},{56,64},{64,7... | collective-permute-start | bytes 15368 | tf_op jit(solution)/shard_map/ppermute | solution.py:14
  11.7 11.1 %collective-permute-start.3 = (f32[10,1,128]{2,1,0:T(1,128)S(1)}, f32[10,1,128]{2,1,0:T(1,128)S(1)}, u32[]{:S(2)}, u32[]{:S(2)}) collective-permute-start(f32[10,1,128]{2,1,0:T(1,128)S(1)} %get-tuple-element.267), channel_id=1, source_target_pairs={{8,0},{16,8},{24,16},{32,24},{40,32},{48,40},{56,48},{64,56},{72,6... | collective-permute-start | bytes 15368 | tf_op jit(solution)/shard_map/ppermute | solution.py:17
  16.2 12.4 %collective-permute-start.4 = (f32[10,34,1]{2,1,0:T(8,128)S(1)}, f32[10,34,1]{2,1,0:T(8,128)S(1)}, u32[]{:S(2)}, u32[]{:S(2)}) collective-permute-start(f32[10,34,1]{2,1,0:T(8,128)S(1)} %get-tuple-element.247), channel_id=1, source_target_pairs={{0,1},{1,2},{2,3},{3,4},{4,5},{5,6},{6,7},{8,9},{9,10},{10,11},{11... | collective-permute-start | bytes 4088 | tf_op jit(solution)/shard_map/ppermute | solution.py:14
  20.8 7.8 %collective-permute-start.6 = (f32[10,34,1]{2,1,0:T(8,128)S(1)}, f32[10,34,1]{2,1,0:T(8,128)S(1)}, u32[]{:S(2)}, u32[]{:S(2)}) collective-permute-start(f32[10,34,1]{2,1,0:T(8,128)S(1)} %get-tuple-element.246), channel_id=1, source_target_pairs={{1,0},{2,1},{3,2},{4,3},{5,4},{6,5},{7,6},{9,8},{10,9},{11,10},{12... | collective-permute-start | bytes 4088 | tf_op jit(solution)/shard_map/ppermute | solution.py:17
  22.9 6.3 collective-permute-start.5
  26.6 7.1 collective-permute-start.7
  34.1 5.6 collective-permute-start.8
  42.9 5.9 collective-permute-start.10
  46.1 7.1 collective-permute-start.11
  53.5 5.5 collective-permute-start.12
  57.7 6.8 collective-permute-start.13
  64.6 5.6 collective-permute-start.14
  67.5 7.1 collective-permute-start.15
  74.9 7.1 collective-permute-start.16
  85.4 5.6 collective-permute-start.18
  88.3 7.1 collective-permute-start.19
  95.7 5.1 collective-permute-start.20
  104.3 5.6 collective-permute-start.22
  107.2 7.1 collective-permute-start.23
  114.5 5.1 collective-permute-start.24
  123.1 5.6 collective-permute-start.26
  126.0 7.1 collective-permute-start.27
  133.4 5.2 collective-permute-start.28
  142.0 5.6 collective-permute-start.30
  144.9 7.1 collective-permute-start.31
  152.3 5.1 collective-permute-start.32
  160.9 5.6 collective-permute-start.34
  163.8 7.1 collective-permute-start.35
  412.9 21.2 %all-to-all-start = ((f32[128,2,128]{2,1,0:T(2,128)}), f32[128,2,128]{2,1,0:T(2,128)S(1)}, u32[]{:S(2)}, u32[]{:S(2)}) async-start(f32[128,2,128]{2,1,0:T(2,128)} %reshape.209), calls=%async_computation | async-start | bytes 262144 | tf_op jit(solution)/shard_map/all_to_all | solution.py:137
  434.1 14.1 %all-to-all-start.1 = ((f32[128,2,128]{2,1,0:T(2,128)}), f32[128,2,128]{2,1,0:T(2,128)S(1)}, u32[]{:S(2)}, u32[]{:S(2)}) async-start(f32[128,2,128]{2,1,0:T(2,128)} %reshape.210), calls=%async_computation.1 | async-start | bytes 262144 | tf_op jit(solution)/shard_map/all_to_all | solution.py:136
  (17 other events, 1441.8 us)
where the time goes:
time: 769 us; the launch traced here: 765 us
  local copies, waits for them, and re-layouts  296 us (38%)
  loops' own time  169 us (22%)
  starting transfers between devices  110 us (14%)
  waiting for transfers between devices  81.9 us (11%)
  blocking collectives  62.6 us (8%)
  other arithmetic  40.9 us (5%)
    another operation x1, loops' own time, entering(): return lax.fori_loop(0, count - 1, hop, so_far)  168 us
    gather x8, local copies, waits for them, and re-layouts, one_block(): head_vals = jnp.sum(head_top[row_index] * select, -1)  113 us
    gather x8, local copies, waits for them, and re-layouts, one_block(): bed_vals = jnp.sum(bed_top[row_index] * select, -1)  86.2 us
    dynamic_slice x127, local copies, waits for them, and re-layouts, hop(): longer = join(so_far, jax.tree.map(lambda part: part[position], pieces))  83.2 us
    ppermute x18, starting transfers between devices, extended(): lax.ppermute(lax.slice_in_dim(block, block.shape[dim] - width, None, axis...  66.1 us
    unnamed x1, blocking collectives  62.6 us
    ppermute x18, waiting for transfers between devices, extended(): lax.ppermute(lax.slice_in_dim(block, 0, width, axis=dim), axis, backward)  60.3 us
    reduce_sum x8, other arithmetic, one_block(): bed_vals = jnp.sum(bed_top[row_index] * select, -1)  32.8 us
  transfers between devices with their start and end apart: 38, of which 25 were waited for; matrix products, arithmetic and copies ran while one was open for 1% of the time, Pallas kernels for 0%

commit v1 on v0

v1 whole, which is shorter than its diff:
```python
import jax
import jax.numpy as jnp
from jax import lax
from jax.experimental import pallas as pl
from jax.experimental.pallas import tpu as pltpu
from jax.sharding import PartitionSpec as P

SWEEPS = 8
HALO = 8
LANES = 128
GROUPS = LANES // HALO
AXES = ("gx", "gy")
VMEM = pl.BlockSpec(memory_space=pltpu.VMEM)
SMEM = pl.BlockSpec(memory_space=pltpu.SMEM)


def call(body, out, count, scratch=(), smem=(), cost=None):
    return pl.pallas_call(
        body,
        out_shape=out,
        in_specs=[SMEM if i in smem else VMEM for i in range(count)],
        out_specs=jax.tree.map(lambda _: VMEM, out),
        scratch_shapes=list(scratch),
        compiler_params=pltpu.CompilerParams(vmem_limit_bytes=40 * 1024 * 1024),
        cost_estimate=cost,
    )


def f32(*shape):
    return jax.ShapeDtypeStruct(shape, jnp.float32)


def pack_x(head, cond, source, storage, last_out, first_out):
    rows = head.shape[1]
    for k, ref in enumerate((head, cond, source, storage)):
        last_out[k] = ref[:, rows - HALO :, :]
        first_out[k] = ref[:, :HALO, :]


def pack_y(head, cond, source, storage, low, high, last_out, first_out):
    layers, rows, width = head.shape
    lane = lax.broadcasted_iota(jnp.int32, (rows + 2 * HALO, LANES), 1)
    first_sum = [None] * last_out.shape[0]
    last_sum = [None] * last_out.shape[0]
    for k, ref in enumerate((head, cond, source, storage)):
        for l in range(layers):
            plane, group = divmod(k * layers + l, GROUPS)
            whole = jnp.concatenate([ref[l], high[k, l], low[k, l]], 0)
            mine = (lane >= group * HALO) & (lane < (group + 1) * HALO)
            first = pltpu.roll(whole, group * HALO, 1) if group else whole
            turn = (group + 1) * HALO % LANES
            last = pltpu.roll(whole, turn, 1) if turn else whole
            if first_sum[plane] is None:
                first_sum[plane], last_sum[plane] = first, last
            else:
                first_sum[plane] = jnp.where(mine, first, first_sum[plane])
                last_sum[plane] = jnp.where(mine, last, last_sum[plane])
    for plane in range(last_out.shape[0]):
        first_out[plane] = first_sum[plane]
        last_out[plane] = last_sum[plane]


def row_info(reach, section, depth, route, retention, heads, info_out, routed_out):
    rows = reach.shape[1]
    reaches = section.shape[1]
    carry = retention[0] * (1.0 - heads[0].astype(jnp.float32))
    sec = section[...]
    bottom = sec - depth[...]
    weight = route[reaches - 1 : reaches, :]
    stacked = jnp.concatenate(
        [sec, bottom, weight, jnp.zeros((LANES - 3, reaches), jnp.float32)], 0
    )
    line = lax.broadcasted_iota(jnp.int32, (reaches, rows), 0)
    one_hot = (line == reach[...]).astype(jnp.float32)
    picked = jnp.dot(
        stacked[:8], one_hot, precision=lax.Precision.HIGHEST, preferred_element_type=jnp.float32
    )
    kind = lax.broadcasted_iota(jnp.int32, (8, rows), 0)
    picked = jnp.where(kind == 3, carry, picked)
    picked = jnp.concatenate([picked, jnp.zeros((LANES - 8, rows), jnp.float32)], 0)
    for part in range(rows // LANES):
        info_out[part * LANES : (part + 1) * LANES, :] = jnp.transpose(
            picked[:, part * LANES : (part + 1) * LANES]
        )
    routed_out[...] = lax.dot_general(
        one_hot,
        route[...],
        (((0,), (1,)), ((), ())),
        precision=lax.Precision.HIGHEST,
        preferred_element_type=jnp.float32,
    )


def select_cells(cells_ref, table, per_group, finish):
    table_rows = table.shape[0]
    blocks = cells_ref.shape[0] // 8
    for start in range(0, blocks, per_group):
        cells = [cells_ref[(start + b) * 8 : (start + b + 1) * 8, :] for b in range(per_group)]
        column = [c & (LANES - 1) for c in cells]
        line = [c // LANES for c in cells]
        found = [jnp.zeros((8, LANES), jnp.float32) for _ in cells]
        for r in range(table_rows):
            spread = jnp.broadcast_to(table[r : r + 1, :], (8, LANES))
            for b in range(per_group):
                value = jnp.take_along_axis(spread, column[b], axis=1, mode="promise_in_bounds")
                found[b] = jnp.where(line[b] == r, value, found[b])
        for b in range(per_group):
            finish(start + b, found[b])


def pick_beds(cells, bed, out):
    table = bed[...]

    def finish(b, value):
        out[b * 8 : (b + 1) * 8, :] = value

    select_cells(cells, table, 8, finish)


def main(
    head, cond, source, storage, low, high, left, right, cells, beds, info, field_out, send_out,
    now, before, coef, weights,
):
    layers, rows, width = head.shape
    tall = rows + 2 * HALO
    blocks = cells.shape[0] // 8
    peers = cells.shape[0] // 2

    lane1 = lax.broadcasted_iota(jnp.int32, (tall, LANES), 1)

    def extended(k, ref, l):
        plane, group = divmod(k * layers + l, GROUPS)
        whole = jnp.concatenate([ref[l], high[k, l], low[k, l]], 0)
        after = right[plane]
        if group:
            after = pltpu.roll(after, LANES - group * HALO, 1)
        ahead = left[plane]
        turn = (LANES - HALO - group * HALO) % LANES
        if turn:
            ahead = pltpu.roll(ahead, turn, 1)
        side = jnp.where(lane1 < HALO, after, jnp.where(lane1 >= LANES - HALO, ahead, 0.0))
        return jnp.concatenate([whole, side], 1)

    wide = 2 * LANES
    conds = [None, extended(1, cond, 0), None]
    for l in range(layers):
        conds[0], conds[1] = (conds[1], conds[2]) if l else (None, conds[1])
        conds[2] = extended(1, cond, l + 1) if l + 1 < layers else None
        mid = conds[1]
        inside = mid > 0.0

        def face(near):
            return jnp.where(inside & (near > 0.0), 0.5 * (mid + near), 0.0)

        faces = [
            face(pltpu.roll(mid, wide - 1, 1)),
            face(pltpu.roll(mid, 1, 1)),
            face(pltpu.roll(mid, tall - 1, 0)),
            face(pltpu.roll(mid, 1, 0)),
        ]
        faces.append(0.5 * (mid + conds[0]) if l else None)
        faces.append(0.5 * (mid + conds[2]) if l + 1 < layers else None)
        total = extended(3, storage, l)
        for one in faces:
            if one is not None:
                total = total + one
        inverse = jnp.where(inside, 1.0 / jnp.where(inside, total, 1.0), 0.0)
        for k, one in enumerate(faces):
            if one is not None:
                coef[k, l] = one * inverse
        coef[6, l] = extended(2, source, l) * inverse
        now[l] = extended(0, head, l)

    sub = lax.broadcasted_iota(jnp.int32, (peers, LANES), 0)
    lane = lax.broadcasted_iota(jnp.int32, (peers, LANES), 1)
    carry_column = info[pl.ds(0, peers, stride=2), :][:, 3:4]
    carry_row = jnp.sum(jnp.where(sub == lane, carry_column, 0.0), 0, keepdims=True)
    product = jnp.where(lane > sub, carry_row, 1.0)
    step = 1
    while step < LANES:
        product = product * jnp.where(lane >= step, pltpu.roll(product, step, 1), 1.0)
        step *= 2
    product = jnp.where(lane > sub, product, 0.0)
    for c in range(2):
        weights[c] = product * info[pl.ds(c, peers, stride=2), :][:, 2:3]

    def sweep(src, dst):
        for l in range(layers):
            mid = src[l]
            out = coef[6, l] + coef[0, l] * pltpu.roll(mid, wide - 1, 1)
            out = out + coef[1, l] * pltpu.roll(mid, 1, 1)
            out = out + coef[2, l] * pltpu.roll(mid, tall - 1, 0)
            out = out + coef[3, l] * pltpu.roll(mid, 1, 0)
            if l:
                out = out + coef[4, l] * src[l - 1]
            if l + 1 < layers:
                out = out + coef[5, l] * src[l + 1]
            dst[l] = out

    def two_sweeps(_, carry):
        sweep(now, before)
        sweep(before, now)
        return carry

    lax.fori_loop(0, SWEEPS // 2, two_sweeps, 0)
    for l in range(layers):
        field_out[l] = now[l, :rows, :width]

    table = now[0, :rows, :width]
    leaks = [None] * blocks

    def finish(b, value):
        span = pl.ds(b * 8, 8)
        detail = info[span, :]
        leak = beds[span, :] * (jnp.maximum(value, detail[:, 1:2]) - detail[:, 0:1])
        leaks[b] = jnp.sum(leak, 1, keepdims=True)

    select_cells(cells, table, 8, finish)
    row_leak = jnp.concatenate(leaks, 0)
    lane2 = lax.broadcasted_iota(jnp.int32, (2 * peers, LANES), 1)
    send_out[...] = jnp.where(lane2 == 0, row_leak, 0.0)
    flow = jnp.zeros((peers, LANES), jnp.float32)
    for c in range(2):
        flow = flow + weights[c] * send_out[pl.ds(c, peers, stride=2), :][:, 0:1]
    flow = jnp.sum(flow, 0, keepdims=True)
    column = jnp.sum(jnp.where(sub == lane, flow, 0.0), 1, keepdims=True)
    even = send_out[pl.ds(0, peers, stride=2), :]
    send_out[pl.ds(0, peers, stride=2), :] = jnp.where(lane == 1, column, even)


def finish_flow(arrived, routed, out):
    parts = arrived[...]
    flow = jnp.sum(parts[:, 0:1] * routed[...], 0, keepdims=True)
    inflow = jnp.sum(parts[:, 1:2], 0, keepdims=True)
    out[...] = flow + inflow


def shifted(value, axis, by):
    count = lax.axis_size(axis)
    pairs = [(i, i + by) for i in range(count) if 0 <= i + by < count]
    return lax.ppermute(value, axis, pairs)


def per_device(
    initial_head, conductivity, source_rate, storage_term, bed_conduct, row_cells, row_reach,
    river_section, bed_depth, route_inverse, retention, chain_heads,
):
    layers, rows, width = initial_head.shape
    fields = (initial_head, conductivity, source_rate, storage_term)
    edge = f32(4, layers, HALO, width)
    planes = -(-4 * layers // GROUPS)
    side = f32(planes, rows + 2 * HALO, LANES)
    tall = rows + 2 * HALO
    row_total = row_cells.shape[1]
    cells = row_cells[0]

    info, routed = call(
        row_info, (f32(row_total, LANES), f32(row_total, river_section.shape[1])), 6, smem=(4, 5)
    )(row_reach, river_section, bed_depth, route_inverse[0], retention, chain_heads)
    last, first = call(pack_x, (edge, edge), 4)(*fields)
    low = shifted(last, "gx", 1)
    high = shifted(first, "gx", -1)
    info = lax.all_to_all(info, AXES, split_axis=0, concat_axis=0, tiled=True)
    beds = call(pick_beds, f32(row_total, LANES), 2)(cells, bed_conduct)
    last, first = call(pack_y, (side, side), 6)(*fields, low, high)
    left = shifted(last, "gy", 1)
    right = shifted(first, "gy", -1)
    wide = pltpu.VMEM((layers, tall, 2 * LANES), jnp.float32)
    head_field, sent = call(
        main,
        (f32(layers, rows, width), f32(row_total, LANES)),
        11,
        scratch=(
            wide,
            wide,
            pltpu.VMEM((7, layers, tall, 2 * LANES), jnp.float32),
            pltpu.VMEM((2, row_total // 2, LANES), jnp.float32),
        ),
    )(*fields, low, high, left, right, cells, beds, info)
    arrived = lax.all_to_all(sent, AXES, split_axis=0, concat_axis=0, tiled=True)
    reach_flow = call(finish_flow, f32(1, river_section.shape[1]), 2)(arrived, routed)
    return (head_field, reach_flow)


def solution(mesh):
    placed = (
        P(None, "gx", "gy"),
        P(None, "gx", "gy"),
        P(None, "gx", "gy"),
        P(None, "gx", "gy"),
        P("gx", "gy"),
        P(AXES, None, None),
        P(AXES, None),
        P(AXES, None),
        P(AXES, None),
        P(AXES, None, None),
        P(AXES),
        P(AXES),
    )
    return jax.shard_map(
        per_device,
        mesh=mesh,
        in_specs=placed,
        out_specs=(P(None, "gx", "gy"), P(AXES, None)),
        check_vma=False,
    )
```

time: 769 us -> 65.3 us (0.08)
  local copies, waits for them, and re-layouts: 296 us -> 4.34 us
  loops' own time: 169 us -> 0 us
  starting transfers between devices: 110 us -> 22.9 us
  waiting for transfers between devices: 81.9 us -> 1.04 us
  blocking collectives: 62.6 us -> 18.8 us
  other arithmetic: 40.9 us -> 0 us
  Pallas kernels: 0 us -> 15.6 us
    gather x16 -> x0, local copies, waits for them, and re-layouts: 200 us -> none  [the longest x8 113 us: one_block(): head_vals = jnp.sum(head_top[row_index] * select, -1)]
    another operation x2 -> x0, loops' own time: 169 us -> none  [the longest x1 168 us: entering(): return lax.fori_loop(0, count - 1, hop, so_far)]
    ppermute x36 -> x4, starting transfers between devices: 95 us -> 10.8 us  [shifted(): return lax.ppermute(value, axis, pairs)]
    dynamic_slice x127 -> x0, local copies, waits for them, and re-layouts: 83.2 us -> none  [hop(): longer = join(so_far, jax.tree.map(lambda part: part[position], pieces))]
    ppermute x36 -> x4, waiting for transfers between devices: 66 us -> 0.08 us  [shifted(): return lax.ppermute(value, axis, pairs)]
    unnamed x1 -> x0, blocking collectives: 62.6 us -> none
    reduce_sum x9 -> x0, other arithmetic: 33.3 us -> none  [the longest x8 32.8 us: one_block(): bed_vals = jnp.sum(bed_top[row_index] * select, -1)]
    all_to_all x0 -> x1, blocking collectives: none -> 18.8 us  [per_device(): lax.all_to_all(sent, AXES, split_axis=0, concat_axis=0, tiled=True)]
  transfers between devices with their start and end apart: 38 -> 5, of which waited for: 25 -> 2; matrix products, arithmetic and copies ran while one was open for 1% -> 0% of each run, Pallas kernels for 0% -> 7%
where the time goes in v1:
time: 65.3 us; the launch traced here: 64.9 us
  starting transfers between devices  22.9 us (35%)
  blocking collectives  18.8 us (29%)
  Pallas kernels  15.6 us (24%)
  local copies, waits for them, and re-layouts  4.34 us (7%)
  between operations  2.12 us (3%)
  waiting for transfers between devices  1.04 us (2%)
    all_to_all x1, blocking collectives, per_device(): lax.all_to_all(sent, AXES, split_axis=0, concat_axis=0, tiled=True)  18.8 us
    all_to_all x1, starting transfers between devices, per_device(): info = lax.all_to_all(info, AXES, split_axis=0, concat_axis=0, tiled=True)  12.1 us
    ppermute x4, starting transfers between devices, shifted(): return lax.ppermute(value, axis, pairs)  10.8 us
    pallas_call x1, Pallas kernels, per_device(): call(main, (f32(layers, rows, width), f32(row_total, LANES)), 11, scratch...  10.3 us
    unnamed x28, local copies, waits for them, and re-layouts  4.34 us
    pallas_call x1, Pallas kernels, per_device(): beds = call(pick_beds, f32(row_total, LANES), 2)(cells, bed_conduct)  2.93 us
  transfers between devices with their start and end apart: 5, of which 2 were waited for; matrix products, arithmetic and copies ran while one was open for 0% of the time, Pallas kernels for 7%

profile of v1, /device:TPU:1, one launch (start us, length us, event | category | flops | bytes accessed | tf_op | source)
XLA Modules:
  0.0 64.9 jit_solution(12175437738477718257)
XLA Ops:
  0.6 0.0 copy-start
  0.6 0.9 %copy-done = f32[10,32,128]{2,1,0:T(8,128)S(1)} copy-done((f32[10,32,128]{2,1,0:T(8,128)S(1)}, f32[10,32,128]{2,1,0:T(8,128)}, u32[]{:S(2)}) %copy-start) | copy-done | bytes 163864
  1.6 0.9 %copy-done.2 = f32[10,32,128]{2,1,0:T(8,128)S(1)} copy-done((f32[10,32,128]{2,1,0:T(8,128)S(1)}, f32[10,32,128]{2,1,0:T(8,128)}, u32[]{:S(2)}) %copy-start.2) | copy-done | bytes 163864
  2.5 0.9 %copy-done.4 = f32[10,32,128]{2,1,0:T(8,128)S(1)} copy-done((f32[10,32,128]{2,1,0:T(8,128)S(1)}, f32[10,32,128]{2,1,0:T(8,128)}, u32[]{:S(2)}) %copy-start.4) | copy-done | bytes 163864
  3.4 0.9 %copy-done.6 = f32[10,32,128]{2,1,0:T(8,128)S(1)} copy-done((f32[10,32,128]{2,1,0:T(8,128)S(1)}, f32[10,32,128]{2,1,0:T(8,128)}, u32[]{:S(2)}) %copy-start.6) | copy-done | bytes 163864
  4.3 0.0 copy-start.12
  4.3 0.0 copy-start.13
  4.4 4.1 %collective-permute-start = (f32[4,10,8,128]{3,2,1,0:T(8,128)S(1)}, f32[4,10,8,128]{3,2,1,0:T(8,128)S(1)}, u32[]{:S(2)}, u32[]{:S(2)}) collective-permute-start(f32[4,10,8,128]{3,2,1,0:T(8,128)S(1)} %get-tuple-element.10), channel_id=1, source_target_pairs={{0,8},{8,16},{16,24},{24,32},{32,40},{40,48},{48,56},{56,64},{64,7... | collective-permute-start | bytes 491528 | tf_op jit(solution)/shard_map/ppermute | solution.py:241
  8.4 1.3 %collective-permute-start.1 = (f32[4,10,8,128]{3,2,1,0:T(8,128)S(1)}, f32[4,10,8,128]{3,2,1,0:T(8,128)S(1)}, u32[]{:S(2)}, u32[]{:S(2)}) collective-permute-start(f32[4,10,8,128]{3,2,1,0:T(8,128)S(1)} %get-tuple-element.11), channel_id=1, source_target_pairs={{8,0},{16,8},{24,16},{32,24},{40,32},{48,40},{56,48},{64,56},{72,6... | collective-permute-start | bytes 491528 | tf_op jit(solution)/shard_map/ppermute | solution.py:241
  11.0 0.0 copy-start.11
  11.1 0.0 copy-done.9
  11.1 0.6 copy-done.11
  11.7 1.1 %shard_map.134 = (f32[256,128]{1,0:T(8,128)}, f32[256,256]{1,0:T(8,128)S(1)}) custom-call(s32[1,256]{1,0:T(1,128)S(1)} %copy-done.11, f32[1,256]{1,0:T(1,128)S(1)} %copy-done.12, f32[1,256]{1,0:T(1,128)S(1)} %copy-done.13, f32[256,256]{1,0:T(8,128)S(1)} %bitcast.10, f32[1]{0:T(128)S(6)} %copy.14.retention, s32[1]{0:T(128)S(6)} %copy.15.heads), custom_call_target="tpu_custom_call" | custom-call | tf_op jit(solution)/shard_map/pallas_call | solution.py:257
  12.9 12.1 %all-to-all-start = ((f32[128,2,128]{2,1,0:T(2,128)}), f32[128,2,128]{2,1,0:T(2,128)S(1)}, u32[]{:S(2)}, u32[]{:S(2)}) async-start(f32[128,2,128]{2,1,0:T(2,128)} %bitcast.2), calls=%async_computation | async-start | bytes 262144 | tf_op jit(solution)/shard_map/all_to_all | solution.py:263
  25.0 0.0 copy-start.8
  25.0 0.0 collective-permute-done.low
  25.0 0.0 collective-permute-done.1.high
  25.0 0.0 copy-done.7
  25.0 0.0 copy-done.3
  25.0 0.0 copy-done.5
  25.0 0.0 copy-done.1
  25.0 0.0 copy-start.10
  25.0 0.5 shard_map.132
  25.6 3.5 %collective-permute-start.2 = (f32[3,48,128]{2,1,0:T(8,128)S(1)}, f32[3,48,128]{2,1,0:T(8,128)S(1)}, u32[]{:S(2)}, u32[]{:S(2)}) collective-permute-start(f32[3,48,128]{2,1,0:T(8,128)S(1)} %get-tuple-element.12), channel_id=1, source_target_pairs={{0,1},{1,2},{2,3},{3,4},{4,5},{5,6},{6,7},{8,9},{9,10},{10,11},{11... | collective-permute-start | bytes 221192 | tf_op jit(solution)/shard_map/ppermute | solution.py:241
  29.1 1.9 %collective-permute-start.3 = (f32[3,48,128]{2,1,0:T(8,128)S(1)}, f32[3,48,128]{2,1,0:T(8,128)S(1)}, u32[]{:S(2)}, u32[]{:S(2)}) collective-permute-start(f32[3,48,128]{2,1,0:T(8,128)S(1)} %get-tuple-element.13), channel_id=1, source_target_pairs={{1,0},{2,1},{3,2},{4,3},{5,4},{6,5},{7,6},{9,8},{10,9},{11,10},{12... | collective-permute-start | bytes 221192 | tf_op jit(solution)/shard_map/ppermute | solution.py:241
  31.1 2.9 %shard_map.133.beds = f32[256,128]{1,0:T(8,128)S(1)} custom-call(s32[256,128]{1,0:T(8,128)S(1)} %bitcast.6, f32[32,128]{1,0:T(8,128)S(1)} %copy-done.10), custom_call_target="tpu_custom_call" | custom-call | tf_op jit(solution)/shard_map/pallas_call | solution.py:264
  34.0 1.0 %all-to-all-done = f32[128,2,128]{2,1,0:T(2,128)S(1)} async-done(((f32[128,2,128]{2,1,0:T(2,128)}), f32[128,2,128]{2,1,0:T(2,128)S(1)}, u32[]{:S(2)}, u32[]{:S(2)}) %all-to-all-start) | async-done | bytes 131104 | tf_op jit(solution)/shard_map/all_to_all | solution.py:263
  35.0 0.0 collective-permute-done.2.left
  35.0 0.1 collective-permute-done.3.right
  35.1 10.3 %shard_map.135 = (f32[10,32,128]{2,1,0:T(8,128)}, f32[256,128]{1,0:T(8,128)S(1)}) custom-call(f32[10,32,128]{2,1,0:T(8,128)S(1)} %copy-done.1, f32[10,32,128]{2,1,0:T(8,128)S(1)} %copy-done.3, f32[10,32,128]{2,1,0:T(8,128)S(1)} %copy-done.5, f32[10,32,128]{2,1,0:T(8,128)S(1)} %copy-done.7, f32[4,10,8,128]{3,2,1,0:T(8,128)S(1)} %collective-permute-done.low, ...), custom_call_target="tpu_custom_call" | custom-call | tf_op jit(solution)/shard_map/pallas_call | solution.py:269
  45.4 18.8 %all_to_all.22 = f32[128,2,128]{2,1,0:T(2,128)S(1)} all-to-all(f32[128,2,128]{2,1,0:T(2,128)S(1)} %bitcast.11), channel_id=1, replica_groups=mesh['gx'=16,'gy'=8] {'gx','gy'}, dimensions={0} | all-to-all | bytes 262144 | tf_op jit(solution)/shard_map/all_to_all | solution.py:280
  64.2 0.7 %shard_map.136 = f32[1,256]{1,0:T(1,128)} custom-call(f32[256,128]{1,0:T(8,128)S(1)} %bitcast.9, f32[256,256]{1,0:T(8,128)S(1)} %get-tuple-element.17.routed), custom_call_target="tpu_custom_call" | custom-call | tf_op jit(solution)/shard_map/pallas_call | solution.py:281
  (13 shorter events, 0.0 us)
Async XLA Ops:
  0.6 0.9 %copy-start = (f32[10,32,128]{2,1,0:T(8,128)S(1)}, f32[10,32,128]{2,1,0:T(8,128)}, u32[]{:S(2)}) copy-start(f32[10,32,128]{2,1,0:T(8,128)} %head.5) | copy-start | bytes 491524
  1.5 0.9 %copy-start.2 = (f32[10,32,128]{2,1,0:T(8,128)S(1)}, f32[10,32,128]{2,1,0:T(8,128)}, u32[]{:S(2)}) copy-start(f32[10,32,128]{2,1,0:T(8,128)} %cond.5) | copy-start | bytes 491524
  2.5 0.9 %copy-start.4 = (f32[10,32,128]{2,1,0:T(8,128)S(1)}, f32[10,32,128]{2,1,0:T(8,128)}, u32[]{:S(2)}) copy-start(f32[10,32,128]{2,1,0:T(8,128)} %source.5) | copy-start | bytes 491524
  3.4 0.9 %copy-start.6 = (f32[10,32,128]{2,1,0:T(8,128)S(1)}, f32[10,32,128]{2,1,0:T(8,128)}, u32[]{:S(2)}) copy-start(f32[10,32,128]{2,1,0:T(8,128)} %storage.5) | copy-start | bytes 491524
  4.3 6.8 %copy-start.9 = (f32[1,256,256]{2,1,0:T(8,128)S(1)}, f32[1,256,256]{2,1,0:T(8,128)}, u32[]{:S(2)}) copy-start(f32[1,256,256]{2,1,0:T(8,128)} %param.21) | copy-start | bytes 786436
  4.3 20.7 %copy-start.7 = (f32[10,32,128]{2,1,0:T(8,128)S(1)}, f32[10,32,128]{2,1,0:T(8,128)}, u32[]{:S(2)}) copy-start(f32[10,32,128]{2,1,0:T(8,128)} %storage.5) | copy-start | bytes 491524
  4.3 6.7 %copy-start.12 = (f32[1,256]{1,0:T(1,128)S(1)}, f32[1,256]{1,0:T(1,128)}, u32[]{:S(2)}) copy-start(f32[1,256]{1,0:T(1,128)} %section.1) | copy-start | bytes 3076
  4.3 6.7 %copy-start.13 = (f32[1,256]{1,0:T(1,128)S(1)}, f32[1,256]{1,0:T(1,128)}, u32[]{:S(2)}) copy-start(f32[1,256]{1,0:T(1,128)} %depth.1) | copy-start | bytes 3076
  4.4 20.6 %collective-permute-start = (f32[4,10,8,128]{3,2,1,0:T(8,128)S(1)}, f32[4,10,8,128]{3,2,1,0:T(8,128)S(1)}, u32[]{:S(2)}, u32[]{:S(2)}) collective-permute-start(f32[4,10,8,128]{3,2,1,0:T(8,128)S(1)} %get-tuple-element.10), channel_id=1, source_target_pairs={{0,8},{8,16},{16,24},{24,32},{32,40},{40,48},{48,56},{56,64},{64,7... | collective-permute-start | bytes 491528 | tf_op jit(solution)/shard_map/ppermute | solution.py:241
  8.4 16.5 %collective-permute-start.1 = (f32[4,10,8,128]{3,2,1,0:T(8,128)S(1)}, f32[4,10,8,128]{3,2,1,0:T(8,128)S(1)}, u32[]{:S(2)}, u32[]{:S(2)}) collective-permute-start(f32[4,10,8,128]{3,2,1,0:T(8,128)S(1)} %get-tuple-element.11), channel_id=1, source_target_pairs={{8,0},{16,8},{24,16},{32,24},{40,32},{48,40},{56,48},{64,56},{72,6... | collective-permute-start | bytes 491528 | tf_op jit(solution)/shard_map/ppermute | solution.py:241
  11.0 0.7 %copy-start.11 = (s32[1,256]{1,0:T(1,128)S(1)}, s32[1,256]{1,0:T(1,128)}, u32[]{:S(2)}) copy-start(s32[1,256]{1,0:T(1,128)} %reach.1) | copy-start | bytes 3076
  11.7 13.3 %copy-start.3 = (f32[10,32,128]{2,1,0:T(8,128)S(1)}, f32[10,32,128]{2,1,0:T(8,128)}, u32[]{:S(2)}) copy-start(f32[10,32,128]{2,1,0:T(8,128)} %cond.5) | copy-start | bytes 491524
  11.7 13.3 %copy-start.5 = (f32[10,32,128]{2,1,0:T(8,128)S(1)}, f32[10,32,128]{2,1,0:T(8,128)}, u32[]{:S(2)}) copy-start(f32[10,32,128]{2,1,0:T(8,128)} %source.5) | copy-start | bytes 491524
  12.9 12.2 %copy-start.1 = (f32[10,32,128]{2,1,0:T(8,128)S(1)}, f32[10,32,128]{2,1,0:T(8,128)}, u32[]{:S(2)}) copy-start(f32[10,32,128]{2,1,0:T(8,128)} %head.5) | copy-start | bytes 491524
  12.9 22.1 %all-to-all-start = ((f32[128,2,128]{2,1,0:T(2,128)}), f32[128,2,128]{2,1,0:T(2,128)S(1)}, u32[]{:S(2)}, u32[]{:S(2)}) async-start(f32[128,2,128]{2,1,0:T(2,128)} %bitcast.2), calls=%async_computation | async-start | bytes 262144 | tf_op jit(solution)/shard_map/all_to_all | solution.py:263
  25.0 6.1 %copy-start.8 = (s32[1,256,128]{2,1,0:T(8,128)S(1)}, s32[1,256,128]{2,1,0:T(8,128)}, u32[]{:S(2)}) copy-start(s32[1,256,128]{2,1,0:T(8,128)} %param.17) | copy-start | bytes 393220
  25.0 6.1 %copy-start.10 = (f32[32,128]{1,0:T(8,128)S(1)}, f32[32,128]{1,0:T(8,128)}, u32[]{:S(2)}) copy-start(f32[32,128]{1,0:T(8,128)} %bed.1) | copy-start | bytes 49156
  25.6 9.4 %collective-permute-start.2 = (f32[3,48,128]{2,1,0:T(8,128)S(1)}, f32[3,48,128]{2,1,0:T(8,128)S(1)}, u32[]{:S(2)}, u32[]{:S(2)}) collective-permute-start(f32[3,48,128]{2,1,0:T(8,128)S(1)} %get-tuple-element.12), channel_id=1, source_target_pairs={{0,1},{1,2},{2,3},{3,4},{4,5},{5,6},{6,7},{8,9},{9,10},{10,11},{11... | collective-permute-start | bytes 221192 | tf_op jit(solution)/shard_map/ppermute | solution.py:241
  29.1 5.9 %collective-permute-start.3 = (f32[3,48,128]{2,1,0:T(8,128)S(1)}, f32[3,48,128]{2,1,0:T(8,128)S(1)}, u32[]{:S(2)}, u32[]{:S(2)}) collective-permute-start(f32[3,48,128]{2,1,0:T(8,128)S(1)} %get-tuple-element.13), channel_id=1, source_target_pairs={{1,0},{2,1},{3,2},{4,3},{5,4},{6,5},{7,6},{9,8},{10,9},{11,10},{12... | collective-permute-start | bytes 221192 | tf_op jit(solution)/shard_map/ppermute | solution.py:241

commit v2 on v1

v2 whole, which is shorter than its diff:
```python
import jax
import jax.numpy as jnp
from jax import lax
from jax.experimental import pallas as pl
from jax.experimental.pallas import tpu as pltpu
from jax.sharding import PartitionSpec as P

SWEEPS = 8
HALO = 8
LANES = 128
GROUPS = LANES // HALO
AXES = ("gx", "gy")
VMEM = pl.BlockSpec(memory_space=pltpu.VMEM)
ANY = pl.BlockSpec(memory_space=pl.ANY)
TOP, BOTTOM = HALO, 2 * HALO


def call(body, out, count, scratch=(), anywhere=False, mib=8, micros=1):
    return pl.pallas_call(
        body,
        out_shape=out,
        in_specs=[ANY if anywhere else VMEM] * count,
        out_specs=jax.tree.map(lambda _: VMEM, out),
        scratch_shapes=list(scratch),
        compiler_params=pltpu.CompilerParams(vmem_limit_bytes=mib * 1024 * 1024),
        cost_estimate=pl.CostEstimate(
            flops=0, transcendentals=0, bytes_accessed=micros * 3_000_000
        ),
    )


def f32(*shape):
    return jax.ShapeDtypeStruct(shape, jnp.float32)


def front(
    head, cond, source, storage, reach, section, depth, route, retention, heads,
    last_out, first_out, info_out,
    reach_here, section_here, depth_here, weight_here, retention_here, heads_here, sems,
):
    rows = head.shape[1]
    reaches = section.shape[1]
    edges = []
    for k, ref in enumerate((head, cond, source, storage)):
        edges.append((ref.at[:, rows - HALO :, :], last_out.at[k]))
        edges.append((ref.at[:, :HALO, :], first_out.at[k]))
    small = [
        (reach, reach_here),
        (section, section_here),
        (depth, depth_here),
        (route.at[0, reaches - 8 :, :], weight_here),
        (retention, retention_here),
        (heads, heads_here),
    ]
    copies = [pltpu.make_async_copy(a, b, sems.at[i]) for i, (a, b) in enumerate(small + edges)]
    for copy in copies:
        copy.start()
    for copy in copies[: len(small)]:
        copy.wait()
    carry = retention_here[0] * (1.0 - heads_here[0].astype(jnp.float32))
    sec = section_here[...]
    table = jnp.concatenate(
        [sec, sec - depth_here[...], weight_here[7:8, :], jnp.full((5, reaches), carry)], 0
    )
    count = reach.shape[1]
    for part in range(count // LANES):
        spots = jnp.broadcast_to(reach_here[:, part * LANES : (part + 1) * LANES], (8, LANES))
        picked = jnp.zeros((8, LANES), jnp.float32)
        for block in range(reaches // LANES):
            value = jnp.take_along_axis(
                table[:, block * LANES : (block + 1) * LANES],
                spots & (LANES - 1),
                axis=1,
                mode="promise_in_bounds",
            )
            picked = jnp.where(spots // LANES == block, value, picked)
        tall = jnp.concatenate([picked, jnp.zeros((LANES - 8, LANES), jnp.float32)], 0)
        info_out[part * LANES : (part + 1) * LANES, :] = jnp.transpose(tall)
    for copy in copies[len(small) :]:
        copy.wait()


def pack_y(head, cond, source, storage, low, high, last_out, first_out):
    layers, rows, width = head.shape
    lane = lax.broadcasted_iota(jnp.int32, (rows + 2 * HALO, LANES), 1)
    first_sum = [None] * last_out.shape[0]
    last_sum = [None] * last_out.shape[0]
    for k, ref in enumerate((head, cond, source, storage)):
        for l in range(layers):
            plane, group = divmod(k * layers + l, GROUPS)
            whole = jnp.concatenate([low[k, l], ref[l], high[k, l]], 0)
            mine = (lane >= group * HALO) & (lane < (group + 1) * HALO)
            first = pltpu.roll(whole, group * HALO, 1) if group else whole
            turn = (group + 1) * HALO % LANES
            last = pltpu.roll(whole, turn, 1) if turn else whole
            if first_sum[plane] is None:
                first_sum[plane], last_sum[plane] = first, last
            else:
                first_sum[plane] = jnp.where(mine, first, first_sum[plane])
                last_sum[plane] = jnp.where(mine, last, last_sum[plane])
    for plane in range(last_out.shape[0]):
        first_out[plane] = first_sum[plane]
        last_out[plane] = last_sum[plane]


def select_cells(cells_ref, table, finish):
    for b in range(cells_ref.shape[0] // 8):
        cells = cells_ref[b * 8 : (b + 1) * 8, :]
        column, line = cells & (LANES - 1), cells // LANES
        found = jnp.zeros((8, LANES), jnp.float32)
        for r, spread in enumerate(table):
            value = jnp.take_along_axis(spread, column, axis=1, mode="promise_in_bounds")
            found = jnp.where(line == r, value, found)
        finish(b, found)


def spread_rows(table):
    return [jnp.broadcast_to(table[r : r + 1, :], (8, LANES)) for r in range(table.shape[0])]


def pick_beds(cells, bed, out):
    def finish(b, value):
        out[b * 8 : (b + 1) * 8, :] = value

    select_cells(cells, spread_rows(bed[...]), finish)


def extended(fields, halos, k, l):
    low, high, left, right = halos
    layers, rows, width = fields[k].shape
    lane = lax.broadcasted_iota(jnp.int32, (rows + 2 * HALO, LANES), 1)
    plane, group = divmod(k * layers + l, GROUPS)
    whole = jnp.concatenate([low[k, l], fields[k][l], high[k, l]], 0)
    after = right[plane]
    if group:
        after = pltpu.roll(after, LANES - group * HALO, 1)
    ahead = left[plane]
    turn = (LANES - HALO - group * HALO) % LANES
    if turn:
        ahead = pltpu.roll(ahead, turn, 1)
    side = jnp.where(lane < HALO, after, jnp.where(lane >= LANES - HALO, ahead, 0.0))
    return whole, side


def beside(pair):
    lane = lax.broadcasted_iota(jnp.int32, pair[0].shape, 1)
    ahead = [pltpu.roll(one, LANES - 1, 1) for one in pair]
    behind = [pltpu.roll(one, 1, 1) for one in pair]
    east = [jnp.where(lane == LANES - 1, ahead[1 - t], ahead[t]) for t in range(2)]
    west = [jnp.where(lane == 0, behind[1 - t], behind[t]) for t in range(2)]
    return east, west


def set_conduct(fields, halos, conds, l, slot):
    rows = conds.shape[2]
    for t, value in enumerate(extended(fields, halos, 1, l)):
        conds[t, slot, TOP : rows - TOP, :] = value
        conds[t, slot, :TOP, :] = jnp.zeros((TOP, LANES), jnp.float32)
        conds[t, slot, rows - TOP :, :] = jnp.zeros((TOP, LANES), jnp.float32)


def set_coefs(fields, halos, conds, slots, coef, l, at):
    rows = conds.shape[2]
    above, here, below = slots
    mids = [conds[t, here, TOP : rows - TOP, :] for t in range(2)]
    east, west = beside(mids)
    storage = extended(fields, halos, 3, l)
    source = extended(fields, halos, 2, l)
    for t in range(2):
        mid = mids[t]
        inside = mid > 0.0

        def face(near):
            return jnp.where(inside & (near > 0.0), 0.5 * (mid + near), 0.0)

        faces = [
            face(east[t]),
            face(west[t]),
            face(conds[t, here, TOP + 1 : rows - TOP + 1, :]),
            face(conds[t, here, TOP - 1 : rows - TOP - 1, :]),
            None if above is None else 0.5 * (mid + conds[t, above, TOP : rows - TOP, :]),
            None if below is None else 0.5 * (mid + conds[t, below, TOP : rows - TOP, :]),
        ]
        total = storage[t]
        for one in faces:
            if one is not None:
                total = total + one
        inverse = jnp.where(inside, 1.0 / jnp.where(inside, total, 1.0), 0.0)
        for k, one in enumerate(faces):
            if one is not None:
                coef[k, t, at] = one * inverse
        coef[6, t, at] = source[t] * inverse


def sweep(place, coef_of, time, first, last, top, only_main, store):
    for start in range(BOTTOM if only_main else TOP, top - (BOTTOM if only_main else TOP), 8):
        span = slice(start, start + 8)
        mids = {}
        for l in range(max(first - 1, 0), last + 2):
            if place(time, l) is not None:
                ref, at = place(time, l)
                mids[l] = [
                    ref[(*at, t, l, span, slice(None))] for t in range(2)
                ]
        for l in range(first, last + 1):
            ref, at = place(time, l)
            east, west = beside(mids[l])
            coef, c = coef_of(l)
            for t in range(1 if only_main else 2):
                rows = slice(start - TOP, start - TOP + 8)
                out = coef[6, t, c, rows, :] + coef[0, t, c, rows, :] * east[t]
                out = out + coef[1, t, c, rows, :] * west[t]
                out = out + coef[2, t, c, rows, :] * ref[(*at, t, l, slice(start + 1, start + 9), slice(None))]
                out = out + coef[3, t, c, rows, :] * ref[(*at, t, l, slice(start - 1, start + 7), slice(None))]
                if l - 1 in mids:
                    out = out + coef[4, t, c, rows, :] * mids[l - 1][t]
                if l + 1 in mids:
                    out = out + coef[5, t, c, rows, :] * mids[l + 1][t]
                store(l, t, start, out)


def set_heads(fields, halos, heads, l):
    rows = heads.shape[3]
    for t, value in enumerate(extended(fields, halos, 0, l)):
        heads[0, t, l, TOP : rows - TOP, :] = value
        for parity in range(2):
            heads[parity, t, l, :TOP, :] = jnp.zeros((TOP, LANES), jnp.float32)
            heads[parity, t, l, rows - TOP :, :] = jnp.zeros((TOP, LANES), jnp.float32)


def upper(
    head, cond, source, storage, low, high, left, right, cells, beds, info,
    send_out, heads, coef, conds, weights,
):
    fields, halos = (head, cond, source, storage), (low, high, left, right)
    layers, rows, width = head.shape
    peers = cells.shape[0] // 2
    for l in range(SWEEPS + 1):
        set_heads(fields, halos, heads, l)
        set_conduct(fields, halos, conds, l, l)
    for l in range(SWEEPS):
        set_coefs(fields, halos, conds, (l - 1 if l else None, l, l + 1), coef, l, l)

    sub = lax.broadcasted_iota(jnp.int32, (peers, LANES), 0)
    lane = lax.broadcasted_iota(jnp.int32, (peers, LANES), 1)
    carry_column = info[pl.ds(0, peers, stride=2), :][:, 3:4]
    carry_row = jnp.sum(jnp.where(sub == lane, carry_column, 0.0), 0, keepdims=True)
    product = jnp.where(lane > sub, carry_row, 1.0)
    step = 1
    while step < LANES:
        product = product * jnp.where(lane >= step, pltpu.roll(product, step, 1), 1.0)
        step *= 2
    product = jnp.where(lane > sub, product, 0.0)
    for c in range(2):
        weights[c] = product * info[pl.ds(c, peers, stride=2), :][:, 2:3]

    for time in range(SWEEPS):

        def store(l, t, start, value):
            heads[(time + 1) % 2, t, l, start : start + 8, :] = value

        sweep(
            lambda when, l: (heads, (when % 2,)),
            lambda l: (coef, l),
            time, 0, SWEEPS - 1 - time, heads.shape[3], time == SWEEPS - 1, store,
        )

    table = heads[SWEEPS % 2, 0, 0, BOTTOM : BOTTOM + rows, :]
    leaks = []

    def finish(b, value):
        span = pl.ds(b * 8, 8)
        detail = info[span, :]
        leak = beds[span, :] * (jnp.maximum(value, detail[:, 1:2]) - detail[:, 0:1])
        leaks.append(jnp.sum(leak, 1, keepdims=True))

    select_cells(cells, spread_rows(table), finish)
    row_leak = jnp.concatenate(leaks, 0)
    lane2 = lax.broadcasted_iota(jnp.int32, (2 * peers, LANES), 1)
    send_out[...] = jnp.where(lane2 == 0, row_leak, 0.0)
    flow = jnp.zeros((peers, LANES), jnp.float32)
    for c in range(2):
        flow = flow + weights[c] * send_out[pl.ds(c, peers, stride=2), :][:, 0:1]
    flow = jnp.sum(flow, 0, keepdims=True)
    column = jnp.sum(jnp.where(sub == lane, flow, 0.0), 1, keepdims=True)
    even = send_out[pl.ds(0, peers, stride=2), :]
    send_out[pl.ds(0, peers, stride=2), :] = jnp.where(lane == 1, column, even)


def lower(
    head, cond, source, storage, low, high, left, right, heads, reach, route,
    field_out, routed_out, mine, coef, conds,
):
    fields, halos = (head, cond, source, storage), (low, high, left, right)
    layers, rows, width = head.shape
    for l in range(SWEEPS + 1, layers):
        set_heads(fields, halos, mine, l)
    for l in range(1, SWEEPS + 1):
        for t in range(2):
            for parity in range(2):
                mine[parity, t, l, :TOP, :] = jnp.zeros((TOP, LANES), jnp.float32)
                mine[parity, t, l, mine.shape[3] - TOP :, :] = jnp.zeros((TOP, LANES), jnp.float32)
    for l in range(layers):
        set_conduct(fields, halos, conds, l, l)
    for l in range(1, layers):
        set_coefs(
            fields, halos, conds, (l - 1, l, l + 1 if l + 1 < layers else None), coef, l, l
        )

    def place(when, l):
        if l >= layers:
            return None
        return (heads if l <= SWEEPS and when <= SWEEPS - l else mine), (when % 2,)

    for time in range(SWEEPS):
        final = time == SWEEPS - 1

        def store(l, t, start, value):
            if final:
                field_out[l, start - BOTTOM : start - BOTTOM + 8, :] = value
            else:
                mine[(time + 1) % 2, t, l, start : start + 8, :] = value

        sweep(
            place,
            lambda l: (coef, l),
            time, SWEEPS - time, layers - 1, heads.shape[3], final, store,
        )
    field_out[0] = heads[SWEEPS % 2, 0, 0, BOTTOM : BOTTOM + rows, :]
    count, reaches = routed_out.shape
    line = lax.broadcasted_iota(jnp.int32, (reaches, count), 0)
    routed_out[...] = lax.dot_general(
        (line == reach[...]).astype(jnp.float32),
        route[...],
        (((0,), (1,)), ((), ())),
        precision=lax.Precision.HIGHEST,
        preferred_element_type=jnp.float32,
    )


def finish_flow(arrived, routed, out):
    parts = arrived[...]
    flow = jnp.sum(parts[:, 0:1] * routed[...], 0, keepdims=True)
    inflow = jnp.sum(parts[:, 1:2], 0, keepdims=True)
    out[...] = flow + inflow


def shifted(value, axis, by):
    count = lax.axis_size(axis)
    pairs = [(i, i + by) for i in range(count) if 0 <= i + by < count]
    return lax.ppermute(value, axis, pairs)


def per_device(
    initial_head, conductivity, source_rate, storage_term, bed_conduct, row_cells, row_reach,
    river_section, bed_depth, route_inverse, retention, chain_heads,
):
    layers, rows, width = initial_head.shape
    fields = (initial_head, conductivity, source_rate, storage_term)
    edge = f32(4, layers, HALO, width)
    planes = -(-4 * layers // GROUPS)
    tall = rows + 2 * HALO
    side = f32(planes, tall, LANES)
    row_total = row_cells.shape[1]
    reaches = river_section.shape[1]
    cells = row_cells[0]

    def scratch(*shape):
        return pltpu.VMEM(shape, jnp.float32)

    last, first, info = call(
        front,
        (edge, edge, f32(row_total, LANES)),
        10,
        scratch=(
            pltpu.VMEM((1, row_total), jnp.int32),
            scratch(1, reaches),
            scratch(1, reaches),
            scratch(8, reaches),
            pltpu.SMEM((1,), jnp.float32),
            pltpu.SMEM((1,), jnp.int32),
            pltpu.SemaphoreType.DMA((14,)),
        ),
        anywhere=True,
        mib=60,
    )(*fields, row_reach, river_section, bed_depth, route_inverse, retention, chain_heads)
    low = shifted(last, "gx", 1)
    high = shifted(first, "gx", -1)
    info = lax.all_to_all(info, AXES, split_axis=0, concat_axis=0, tiled=True)
    beds = call(pick_beds, f32(row_total, LANES), 2, micros=2)(cells, bed_conduct)
    last, first = call(pack_y, (side, side), 6)(*fields, low, high)
    left = shifted(last, "gy", 1)
    right = shifted(first, "gy", -1)
    pads = tall + 2 * TOP
    sent, heads = call(
        upper,
        (
            f32(row_total, LANES),
            f32(2, 2, SWEEPS + 1, pads, LANES),
        ),
        11,
        scratch=(
            scratch(7, 2, SWEEPS, tall, LANES),
            scratch(2, SWEEPS + 1, pads, LANES),
            scratch(2, row_total // 2, LANES),
        ),
        mib=16,
        micros=5,
    )(*fields, low, high, left, right, cells, beds, info)
    arrived = lax.all_to_all(sent, AXES, split_axis=0, concat_axis=0, tiled=True)
    head_field, routed = call(
        lower,
        (f32(layers, rows, width), f32(row_total, reaches)),
        11,
        scratch=(
            scratch(2, 2, layers, pads, LANES),
            scratch(7, 2, layers, tall, LANES),
            scratch(2, layers, pads, LANES),
        ),
        mib=16,
        micros=5,
    )(*fields, low, high, left, right, heads, row_reach, route_inverse[0])
    reach_flow = call(finish_flow, f32(1, reaches), 2)(arrived, routed)
    return (head_field, reach_flow)


def solution(mesh):
    placed = (
        P(None, "gx", "gy"),
        P(None, "gx", "gy"),
        P(None, "gx", "gy"),
        P(None, "gx", "gy"),
        P("gx", "gy"),
        P(AXES, None, None),
        P(AXES, None),
        P(AXES, None),
        P(AXES, None),
        P(AXES, None, None),
        P(AXES),
        P(AXES),
    )
    return jax.shard_map(
        per_device,
        mesh=mesh,
        in_specs=placed,
        out_specs=(P(None, "gx", "gy"), P(AXES, None)),
        check_vma=False,
    )
```

time: 65.3 us -> 58.6 us (0.90)
  blocking collectives: 18.8 us -> 0 us
  starting transfers between devices: 22.9 us -> 31.9 us
  waiting for transfers between devices: 1.04 us -> 9.63 us
  local copies, waits for them, and re-layouts: 4.34 us -> 0.04 us
  Pallas kernels: 15.6 us -> 14.4 us
    all_to_all x1 -> x0, blocking collectives: 18.8 us -> none  [per_device(): lax.all_to_all(sent, AXES, split_axis=0, concat_axis=0, tiled=True)]
    all_to_all x0 -> x1, starting transfers between devices: none -> 8.96 us  [per_device(): lax.all_to_all(sent, AXES, split_axis=0, concat_axis=0, tiled=True)]
    all_to_all x0 -> x1, waiting for transfers between devices: none -> 7.03 us  [per_device(): lax.all_to_all(sent, AXES, split_axis=0, concat_axis=0, tiled=True)]
    unnamed x28 -> x16, local copies, waits for them, and re-layouts: 4.34 us -> 0.04 us
    all_to_all x1, waiting for transfers between devices: 0.96 us -> 2.51 us  [per_device(): info = lax.all_to_all(info, AXES, split_axis=0, concat_axis=0, tiled=True)]
    pallas_call x5, Pallas kernels: 15.1 us -> 13.9 us  [the longest x1 7.07 us: per_device(): call(upper, (f32(row_total, LANES), f32(2, 2, SWEEPS + 1, pads, LANES)),...]
  transfers between devices with their start and end apart: 5 -> 6, of which waited for: 2 -> 3; matrix products, arithmetic and copies ran while one was open for 0% -> 0% of each run, Pallas kernels for 7% -> 8%
where the time goes in v2:
time: 58.6 us; the launch traced here: 58.2 us
  starting transfers between devices  31.9 us (54%)
  Pallas kernels  14.4 us (25%)
  waiting for transfers between devices  9.63 us (16%)
  between operations  2.21 us (4%)
    all_to_all x1, starting transfers between devices, per_device(): info = lax.all_to_all(info, AXES, split_axis=0, concat_axis=0, tiled=True)  12.1 us
    ppermute x4, starting transfers between devices, shifted(): return lax.ppermute(value, axis, pairs)  10.8 us
    all_to_all x1, starting transfers between devices, per_device(): lax.all_to_all(sent, AXES, split_axis=0, concat_axis=0, tiled=True)  8.96 us
    pallas_call x1, Pallas kernels, per_device(): call(upper, (f32(row_total, LANES), f32(2, 2, SWEEPS + 1, pads, LANES)),...  7.07 us
    all_to_all x1, waiting for transfers between devices, per_device(): lax.all_to_all(sent, AXES, split_axis=0, concat_axis=0, tiled=True)  7.03 us
    pallas_call x1, Pallas kernels, per_device(): call(lower, (f32(layers, rows, width), f32(row_total, reaches)), 11, scra...  3.03 us
    all_to_all x1, waiting for transfers between devices, per_device(): info = lax.all_to_all(info, AXES, split_axis=0, concat_axis=0, tiled=True)  2.51 us
    pallas_call x1, Pallas kernels, per_device(): call(front, (edge, edge, f32(row_total, LANES)), 10, scratch=(pltpu.VMEM(...  1.87 us
  transfers between devices with their start and end apart: 6, of which 3 were waited for; matrix products, arithmetic and copies ran while one was open for 0% of the time, Pallas kernels for 8%

profile of v2, /device:TPU:1, one launch (start us, length us, event | category | flops | bytes accessed | tf_op | source)
XLA Modules:
  0.0 58.2 jit_solution(11133031281871820695)
XLA Ops:
  0.6 0.0 copy-start.3
  0.6 0.0 copy-start.2
  0.7 0.0 copy-start.1
  0.7 0.0 copy-start
  0.7 0.0 copy-start.5
  0.7 0.0 copy-start.6
  2.1 1.9 %shard_map.131 = (f32[4,10,8,128]{3,2,1,0:T(8,128)}, f32[4,10,8,128]{3,2,1,0:T(8,128)}, f32[256,128]{1,0:T(8,128)}) custom-call(f32[10,32,128]{2,1,0:T(8,128)} %head.7, f32[10,32,128]{2,1,0:T(8,128)} %cond.7, f32[10,32,128]{2,1,0:T(8,128)} %source.7, f32[10,32,128]{2,1,0:T(8,128)} %storage.7, s32[1,256]{1,0:T(1,128)} %reach.3, f32[1,256]{1,0:T(1,128)} %section.1, ...), custom_call_target="tpu_custom_call" | custom-call | bytes 3000000 | tf_op jit(solution)/shard_map/pallas_call | solution.py:371
  3.9 4.0 %collective-permute-start = (f32[4,10,8,128]{3,2,1,0:T(8,128)}, f32[4,10,8,128]{3,2,1,0:T(8,128)S(1)}, u32[]{:S(2)}, u32[]{:S(2)}) collective-permute-start(f32[4,10,8,128]{3,2,1,0:T(8,128)} %get-tuple-element.11), channel_id=1, source_target_pairs={{0,8},{8,16},{16,24},{24,32},{32,40},{40,48},{48,56},{56,64},{64,7... | collective-permute-start | bytes 491528 | tf_op jit(solution)/shard_map/ppermute | solution.py:351
  7.9 1.3 %collective-permute-start.1 = (f32[4,10,8,128]{3,2,1,0:T(8,128)}, f32[4,10,8,128]{3,2,1,0:T(8,128)S(1)}, u32[]{:S(2)}, u32[]{:S(2)}) collective-permute-start(f32[4,10,8,128]{3,2,1,0:T(8,128)} %get-tuple-element.12), channel_id=1, source_target_pairs={{8,0},{16,8},{24,16},{32,24},{40,32},{48,40},{56,48},{64,56},{72,6... | collective-permute-start | bytes 491528 | tf_op jit(solution)/shard_map/ppermute | solution.py:351
  9.2 12.1 %all-to-all-start = ((f32[128,2,128]{2,1,0:T(2,128)}), f32[128,2,128]{2,1,0:T(2,128)S(1)}, u32[]{:S(2)}, u32[]{:S(2)}) async-start(f32[128,2,128]{2,1,0:T(2,128)} %bitcast.11), calls=%async_computation | async-start | bytes 262144 | tf_op jit(solution)/shard_map/all_to_all | solution.py:389
  21.3 0.0 collective-permute-done.low
  21.3 0.0 collective-permute-done.1.high
  21.3 0.0 copy-done.3
  21.3 0.0 copy-done.2
  21.3 0.0 copy-done.1
  21.4 0.0 copy-done
  21.4 0.5 shard_map.132
  21.9 0.0 copy-start.4
  21.9 0.0 copy-start.7
  21.9 3.7 %collective-permute-start.2 = (f32[3,48,128]{2,1,0:T(8,128)S(1)}, f32[3,48,128]{2,1,0:T(8,128)S(1)}, u32[]{:S(2)}, u32[]{:S(2)}) collective-permute-start(f32[3,48,128]{2,1,0:T(8,128)S(1)} %get-tuple-element.13), channel_id=1, source_target_pairs={{0,1},{1,2},{2,3},{3,4},{4,5},{5,6},{6,7},{8,9},{9,10},{10,11},{11... | collective-permute-start | bytes 221192 | tf_op jit(solution)/shard_map/ppermute | solution.py:351
  25.6 1.9 %collective-permute-start.3 = (f32[3,48,128]{2,1,0:T(8,128)S(1)}, f32[3,48,128]{2,1,0:T(8,128)S(1)}, u32[]{:S(2)}, u32[]{:S(2)}) collective-permute-start(f32[3,48,128]{2,1,0:T(8,128)S(1)} %get-tuple-element.14), channel_id=1, source_target_pairs={{1,0},{2,1},{3,2},{4,3},{5,4},{6,5},{7,6},{9,8},{10,9},{11,10},{12... | collective-permute-start | bytes 221192 | tf_op jit(solution)/shard_map/ppermute | solution.py:351
  27.6 1.2 %shard_map.133.beds = f32[256,128]{1,0:T(8,128)S(1)} custom-call(s32[256,128]{1,0:T(8,128)S(1)} %bitcast.7, f32[32,128]{1,0:T(8,128)S(1)} %copy-done.6), custom_call_target="tpu_custom_call" | custom-call | bytes 6000000 | tf_op jit(solution)/shard_map/pallas_call | solution.py:390
  28.8 2.5 %all-to-all-done = f32[128,2,128]{2,1,0:T(2,128)S(1)} async-done(((f32[128,2,128]{2,1,0:T(2,128)}), f32[128,2,128]{2,1,0:T(2,128)S(1)}, u32[]{:S(2)}, u32[]{:S(2)}) %all-to-all-start) | async-done | bytes 131104 | tf_op jit(solution)/shard_map/all_to_all | solution.py:389
  31.3 0.0 collective-permute-done.2.left
  31.3 0.1 collective-permute-done.3.right
  31.4 7.1 %shard_map.134 = (f32[256,128]{1,0:T(8,128)}, f32[2,2,9,64,128]{4,3,2,1,0:T(8,128)S(1)}) custom-call(f32[10,32,128]{2,1,0:T(8,128)S(1)} %copy-done, f32[10,32,128]{2,1,0:T(8,128)S(1)} %copy-done.1, f32[10,32,128]{2,1,0:T(8,128)S(1)} %copy-done.2, f32[10,32,128]{2,1,0:T(8,128)S(1)} %copy-done.3, f32[4,10,8,128]{3,2,1,0:T(8,128)S(1)} %collective-permute-done.low, ...), custom_call_target="tpu_custom_call" | custom-call | bytes 15000000 | tf_op jit(solution)/shard_map/pallas_call | solution.py:395
  38.5 9.0 %all-to-all-start.1 = ((f32[128,2,128]{2,1,0:T(2,128)}), f32[128,2,128]{2,1,0:T(2,128)S(1)}, u32[]{:S(2)}, u32[]{:S(2)}) async-start(f32[128,2,128]{2,1,0:T(2,128)} %bitcast.4), calls=%async_computation.1 | async-start | bytes 262144 | tf_op jit(solution)/shard_map/all_to_all | solution.py:410
  47.4 0.0 copy-done.4
  47.5 0.0 copy-done.7
  47.5 3.0 %shard_map.135 = (f32[10,32,128]{2,1,0:T(8,128)}, f32[256,256]{1,0:T(8,128)S(1)}) custom-call(f32[10,32,128]{2,1,0:T(8,128)S(1)} %copy-done, f32[10,32,128]{2,1,0:T(8,128)S(1)} %copy-done.1, f32[10,32,128]{2,1,0:T(8,128)S(1)} %copy-done.2, f32[10,32,128]{2,1,0:T(8,128)S(1)} %copy-done.3, f32[4,10,8,128]{3,2,1,0:T(8,128)S(1)} %collective-permute-done.low, ...), custom_call_target="tpu_custom_call" | custom-call | bytes 15000000 | tf_op jit(solution)/shard_map/pallas_call | solution.py:411
  50.5 7.0 %all-to-all-done.1 = f32[128,2,128]{2,1,0:T(2,128)S(1)} async-done(((f32[128,2,128]{2,1,0:T(2,128)}), f32[128,2,128]{2,1,0:T(2,128)S(1)}, u32[]{:S(2)}, u32[]{:S(2)}) %all-to-all-start.1) | async-done | bytes 131104 | tf_op jit(solution)/shard_map/all_to_all | solution.py:410
  57.5 0.7 %shard_map.136 = f32[1,256]{1,0:T(1,128)} custom-call(f32[256,128]{1,0:T(8,128)S(1)} %bitcast.10, f32[256,256]{1,0:T(8,128)S(1)} %get-tuple-element.19.routed), custom_call_target="tpu_custom_call" | custom-call | bytes 3000000 | tf_op jit(solution)/shard_map/pallas_call | solution.py:423
  (2 shorter events, 0.0 us)
Async XLA Ops:
  0.6 20.7 %copy-start.3 = (f32[10,32,128]{2,1,0:T(8,128)S(1)}, f32[10,32,128]{2,1,0:T(8,128)}, u32[]{:S(2)}) copy-start(f32[10,32,128]{2,1,0:T(8,128)} %storage.7) | copy-start | bytes 491524
  0.6 20.7 %copy-start.2 = (f32[10,32,128]{2,1,0:T(8,128)S(1)}, f32[10,32,128]{2,1,0:T(8,128)}, u32[]{:S(2)}) copy-start(f32[10,32,128]{2,1,0:T(8,128)} %source.7) | copy-start | bytes 491524
  0.7 20.7 %copy-start.1 = (f32[10,32,128]{2,1,0:T(8,128)S(1)}, f32[10,32,128]{2,1,0:T(8,128)}, u32[]{:S(2)}) copy-start(f32[10,32,128]{2,1,0:T(8,128)} %cond.7) | copy-start | bytes 491524
  0.7 20.7 %copy-start = (f32[10,32,128]{2,1,0:T(8,128)S(1)}, f32[10,32,128]{2,1,0:T(8,128)}, u32[]{:S(2)}) copy-start(f32[10,32,128]{2,1,0:T(8,128)} %head.7) | copy-start | bytes 491524
  0.7 26.9 %copy-start.5 = (s32[1,256,128]{2,1,0:T(8,128)S(1)}, s32[1,256,128]{2,1,0:T(8,128)}, u32[]{:S(2)}) copy-start(s32[1,256,128]{2,1,0:T(8,128)} %param.17) | copy-start | bytes 393220
  0.7 26.9 %copy-start.6 = (f32[32,128]{1,0:T(8,128)S(1)}, f32[32,128]{1,0:T(8,128)}, u32[]{:S(2)}) copy-start(f32[32,128]{1,0:T(8,128)} %bed.1) | copy-start | bytes 49156
  3.9 17.4 %collective-permute-start = (f32[4,10,8,128]{3,2,1,0:T(8,128)}, f32[4,10,8,128]{3,2,1,0:T(8,128)S(1)}, u32[]{:S(2)}, u32[]{:S(2)}) collective-permute-start(f32[4,10,8,128]{3,2,1,0:T(8,128)} %get-tuple-element.11), channel_id=1, source_target_pairs={{0,8},{8,16},{16,24},{24,32},{32,40},{40,48},{48,56},{56,64},{64,7... | collective-permute-start | bytes 491528 | tf_op jit(solution)/shard_map/ppermute | solution.py:351
  7.9 13.4 %collective-permute-start.1 = (f32[4,10,8,128]{3,2,1,0:T(8,128)}, f32[4,10,8,128]{3,2,1,0:T(8,128)S(1)}, u32[]{:S(2)}, u32[]{:S(2)}) collective-permute-start(f32[4,10,8,128]{3,2,1,0:T(8,128)} %get-tuple-element.12), channel_id=1, source_target_pairs={{8,0},{16,8},{24,16},{32,24},{40,32},{48,40},{56,48},{64,56},{72,6... | collective-permute-start | bytes 491528 | tf_op jit(solution)/shard_map/ppermute | solution.py:351
  9.2 22.1 %all-to-all-start = ((f32[128,2,128]{2,1,0:T(2,128)}), f32[128,2,128]{2,1,0:T(2,128)S(1)}, u32[]{:S(2)}, u32[]{:S(2)}) async-start(f32[128,2,128]{2,1,0:T(2,128)} %bitcast.11), calls=%async_computation | async-start | bytes 262144 | tf_op jit(solution)/shard_map/all_to_all | solution.py:389
  21.9 25.5 %copy-start.4 = (f32[1,256,256]{2,1,0:T(8,128)S(1)}, f32[1,256,256]{2,1,0:T(8,128)}, u32[]{:S(2)}) copy-start(f32[1,256,256]{2,1,0:T(8,128)} %route.1) | copy-start | bytes 786436
  21.9 25.5 %copy-start.7 = (s32[1,256]{1,0:T(1,128)S(1)}, s32[1,256]{1,0:T(1,128)}, u32[]{:S(2)}) copy-start(s32[1,256]{1,0:T(1,128)} %reach.3) | copy-start | bytes 3076
  21.9 9.4 %collective-permute-start.2 = (f32[3,48,128]{2,1,0:T(8,128)S(1)}, f32[3,48,128]{2,1,0:T(8,128)S(1)}, u32[]{:S(2)}, u32[]{:S(2)}) collective-permute-start(f32[3,48,128]{2,1,0:T(8,128)S(1)} %get-tuple-element.13), channel_id=1, source_target_pairs={{0,1},{1,2},{2,3},{3,4},{4,5},{5,6},{6,7},{8,9},{9,10},{10,11},{11... | collective-permute-start | bytes 221192 | tf_op jit(solution)/shard_map/ppermute | solution.py:351
  25.6 5.8 %collective-permute-start.3 = (f32[3,48,128]{2,1,0:T(8,128)S(1)}, f32[3,48,128]{2,1,0:T(8,128)S(1)}, u32[]{:S(2)}, u32[]{:S(2)}) collective-permute-start(f32[3,48,128]{2,1,0:T(8,128)S(1)} %get-tuple-element.14), channel_id=1, source_target_pairs={{1,0},{2,1},{3,2},{4,3},{5,4},{6,5},{7,6},{9,8},{10,9},{11,10},{12... | collective-permute-start | bytes 221192 | tf_op jit(solution)/shard_map/ppermute | solution.py:351
  38.5 19.1 %all-to-all-start.1 = ((f32[128,2,128]{2,1,0:T(2,128)}), f32[128,2,128]{2,1,0:T(2,128)S(1)}, u32[]{:S(2)}, u32[]{:S(2)}) async-start(f32[128,2,128]{2,1,0:T(2,128)} %bitcast.4), calls=%async_computation.1 | async-start | bytes 262144 | tf_op jit(solution)/shard_map/all_to_all | solution.py:410

commit v3 on v2

--- a/solution.py
+++ b/solution.py
@@ -151,10 +151,22 @@
     return east, west
 
 
-def set_conduct(fields, halos, conds, l, slot):
+def grid_mask(rows):
+    row = lax.broadcasted_iota(jnp.int32, (rows, LANES), 0)
+    lane = lax.broadcasted_iota(jnp.int32, (rows, LANES), 1)
+    at_x, at_y = lax.axis_index("gx"), lax.axis_index("gy")
+    first_row = jnp.where(at_x == 0, HALO, 0)
+    last_row = jnp.where(at_x == lax.axis_size("gx") - 1, rows - HALO, rows)
+    after = jnp.where(at_y == lax.axis_size("gy") - 1, 0, HALO)
+    ahead = jnp.where(at_y == 0, LANES, LANES - HALO)
+    tall = (row >= first_row) & (row < last_row)
+    return [tall, tall & ((lane < after) | (lane >= ahead))]
+
+
+def set_conduct(fields, halos, mask, conds, l, slot):
     rows = conds.shape[2]
     for t, value in enumerate(extended(fields, halos, 1, l)):
-        conds[t, slot, TOP : rows - TOP, :] = value
+        conds[t, slot, TOP : rows - TOP, :] = jnp.where(mask[t], value, 0.0)
         conds[t, slot, :TOP, :] = jnp.zeros((TOP, LANES), jnp.float32)
         conds[t, slot, rows - TOP :, :] = jnp.zeros((TOP, LANES), jnp.float32)
 
@@ -235,9 +247,10 @@
     fields, halos = (head, cond, source, storage), (low, high, left, right)
     layers, rows, width = head.shape
     peers = cells.shape[0] // 2
+    mask = grid_mask(rows + 2 * HALO)
     for l in range(SWEEPS + 1):
         set_heads(fields, halos, heads, l)
-        set_conduct(fields, halos, conds, l, l)
+        set_conduct(fields, halos, mask, conds, l, l)
     for l in range(SWEEPS):
         set_coefs(fields, halos, conds, (l - 1 if l else None, l, l + 1), coef, l, l)
 
@@ -293,6 +306,7 @@
 ):
     fields, halos = (head, cond, source, storage), (low, high, left, right)
     layers, rows, width = head.shape
+    mask = grid_mask(rows + 2 * HALO)
     for l in range(SWEEPS + 1, layers):
         set_heads(fields, halos, mine, l)
     for l in range(1, SWEEPS + 1):
@@ -301,7 +315,7 @@
                 mine[parity, t, l, :TOP, :] = jnp.zeros((TOP, LANES), jnp.float32)
                 mine[parity, t, l, mine.shape[3] - TOP :, :] = jnp.zeros((TOP, LANES), jnp.float32)
     for l in range(layers):
-        set_conduct(fields, halos, conds, l, l)
+        set_conduct(fields, halos, mask, conds, l, l)
     for l in range(1, layers):
         set_coefs(
             fields, halos, conds, (l - 1, l, l + 1 if l + 1 < layers else None), coef, l, l
@@ -347,8 +361,7 @@
 
 def shifted(value, axis, by):
     count = lax.axis_size(axis)
-    pairs = [(i, i + by) for i in range(count) if 0 <= i + by < count]
-    return lax.ppermute(value, axis, pairs)
+    return lax.ppermute(value, axis, [(i, (i + by) % count) for i in range(count)])
 
 
 def per_device(

time: 58.6 us -> 50.9 us (0.87)
  starting transfers between devices: 31.9 us -> 20.5 us
  waiting for transfers between devices: 9.63 us -> 13.5 us
    all_to_all x1, starting transfers between devices: 12.1 us -> 6.66 us  [per_device(): info = lax.all_to_all(info, AXES, split_axis=0, concat_axis=0, tiled=True)]
    all_to_all x1, waiting for transfers between devices: 2.51 us -> 6.48 us  [per_device(): info = lax.all_to_all(info, AXES, split_axis=0, concat_axis=0, tiled=True)]
    all_to_all x1, starting transfers between devices: 8.96 us -> 5.22 us  [per_device(): lax.all_to_all(sent, AXES, split_axis=0, concat_axis=0, tiled=True)]
    ppermute x4, starting transfers between devices: 10.8 us -> 8.58 us  [shifted(): lax.ppermute(value, axis, [(i, (i + by) % count) for i in range(count)])]
  transfers between devices with their start and end apart: 6 -> 6, of which waited for: 3 -> 2; matrix products, arithmetic and copies ran while one was open for 0% -> 0% of each run, Pallas kernels for 8% -> 10%
where the time goes in v3:
time: 50.9 us; the launch traced here: 50.6 us
  starting transfers between devices  20.5 us (40%)
  Pallas kernels  14.5 us (28%)
  waiting for transfers between devices  13.5 us (27%)
  between operations  2.17 us (4%)
    ppermute x4, starting transfers between devices, shifted(): lax.ppermute(value, axis, [(i, (i + by) % count) for i in range(count)])  8.58 us
    pallas_call x1, Pallas kernels, per_device(): call(upper, (f32(row_total, LANES), f32(2, 2, SWEEPS + 1, pads, LANES)),...  7.1 us
    all_to_all x1, waiting for transfers between devices, per_device(): lax.all_to_all(sent, AXES, split_axis=0, concat_axis=0, tiled=True)  6.98 us
    all_to_all x1, starting transfers between devices, per_device(): info = lax.all_to_all(info, AXES, split_axis=0, concat_axis=0, tiled=True)  6.66 us
    all_to_all x1, waiting for transfers between devices, per_device(): info = lax.all_to_all(info, AXES, split_axis=0, concat_axis=0, tiled=True)  6.48 us
    all_to_all x1, starting transfers between devices, per_device(): lax.all_to_all(sent, AXES, split_axis=0, concat_axis=0, tiled=True)  5.22 us
    pallas_call x1, Pallas kernels, per_device(): call(lower, (f32(layers, rows, width), f32(row_total, reaches)), 11, scra...  3.08 us
    pallas_call x1, Pallas kernels, per_device(): call(front, (edge, edge, f32(row_total, LANES)), 10, scratch=(pltpu.VMEM(...  1.87 us
  transfers between devices with their start and end apart: 6, of which 2 were waited for; matrix products, arithmetic and copies ran while one was open for 0% of the time, Pallas kernels for 10%

profile of v3, /device:TPU:1, one launch (start us, length us, event | category | flops | bytes accessed | tf_op | source)
XLA Modules:
  0.0 50.6 jit_solution(13215880058841769842)
XLA Ops:
  0.6 0.0 copy-start.3
  0.6 0.0 copy-start.2
  0.7 0.0 copy-start.1
  0.7 0.0 copy-start
  0.7 0.0 copy-start.5
  0.7 0.0 copy-start.6
  2.1 1.9 %shard_map.131 = (f32[4,10,8,128]{3,2,1,0:T(8,128)}, f32[4,10,8,128]{3,2,1,0:T(8,128)}, f32[256,128]{1,0:T(8,128)}) custom-call(f32[10,32,128]{2,1,0:T(8,128)} %head.7, f32[10,32,128]{2,1,0:T(8,128)} %cond.7, f32[10,32,128]{2,1,0:T(8,128)} %source.7, f32[10,32,128]{2,1,0:T(8,128)} %storage.7, s32[1,256]{1,0:T(1,128)} %reach.3, f32[1,256]{1,0:T(1,128)} %section.1, ...), custom_call_target="tpu_custom_call" | custom-call | bytes 3000000 | tf_op jit(solution)/shard_map/pallas_call | solution.py:384
  3.9 2.1 %collective-permute-start = (f32[4,10,8,128]{3,2,1,0:T(8,128)}, f32[4,10,8,128]{3,2,1,0:T(8,128)S(1)}, u32[]{:S(2)}, u32[]{:S(2)}) collective-permute-start(f32[4,10,8,128]{3,2,1,0:T(8,128)} %get-tuple-element.11), channel_id=1, source_target_pairs={{0,8},{8,16},{16,24},{24,32},{32,40},{40,48},{48,56},{56,64},{64,7... | collective-permute-start | bytes 491528 | tf_op jit(solution)/shard_map/ppermute | solution.py:364
  6.0 4.8 %collective-permute-start.1 = (f32[4,10,8,128]{3,2,1,0:T(8,128)}, f32[4,10,8,128]{3,2,1,0:T(8,128)S(1)}, u32[]{:S(2)}, u32[]{:S(2)}) collective-permute-start(f32[4,10,8,128]{3,2,1,0:T(8,128)} %get-tuple-element.12), channel_id=1, source_target_pairs={{0,120},{8,0},{16,8},{24,16},{32,24},{40,32},{48,40},{56,48},{64,5... | collective-permute-start | bytes 491528 | tf_op jit(solution)/shard_map/ppermute | solution.py:364
  10.9 6.7 %all-to-all-start = ((f32[128,2,128]{2,1,0:T(2,128)}), f32[128,2,128]{2,1,0:T(2,128)S(1)}, u32[]{:S(2)}, u32[]{:S(2)}) async-start(f32[128,2,128]{2,1,0:T(2,128)} %bitcast.11), calls=%async_computation | async-start | bytes 262144 | tf_op jit(solution)/shard_map/all_to_all | solution.py:402
  17.5 0.0 collective-permute-done.low
  17.5 0.0 collective-permute-done.1.high
  17.6 0.0 copy-done.3
  17.6 0.0 copy-done.2
  17.6 0.0 copy-done.1
  17.6 0.0 copy-done
  17.6 0.5 %shard_map.132 = (f32[3,48,128]{2,1,0:T(8,128)S(1)}, f32[3,48,128]{2,1,0:T(8,128)S(1)}) custom-call(f32[10,32,128]{2,1,0:T(8,128)S(1)} %copy-done, f32[10,32,128]{2,1,0:T(8,128)S(1)} %copy-done.1, f32[10,32,128]{2,1,0:T(8,128)S(1)} %copy-done.2, f32[10,32,128]{2,1,0:T(8,128)S(1)} %copy-done.3, f32[4,10,8,128]{3,2,1,0:T(8,128)S(1)} %collective-permute-done.low, ...), custom_call_target="tpu_custom_call" | custom-call | bytes 3000000 | tf_op jit(solution)/shard_map/pallas_call | solution.py:404
  18.1 0.0 copy-start.4
  18.1 0.0 copy-start.7
  18.2 1.6 %collective-permute-start.2 = (f32[3,48,128]{2,1,0:T(8,128)S(1)}, f32[3,48,128]{2,1,0:T(8,128)S(1)}, u32[]{:S(2)}, u32[]{:S(2)}) collective-permute-start(f32[3,48,128]{2,1,0:T(8,128)S(1)} %get-tuple-element.13), channel_id=1, source_target_pairs={{0,1},{1,2},{2,3},{3,4},{4,5},{5,6},{6,7},{7,0},{8,9},{9,10},{10,1... | collective-permute-start | bytes 221192 | tf_op jit(solution)/shard_map/ppermute | solution.py:364
  19.8 0.0 collective-permute-start.3
  19.8 0.0 copy-done.5
  19.8 0.0 copy-done.6
  19.8 1.2 %shard_map.133.beds = f32[256,128]{1,0:T(8,128)S(1)} custom-call(s32[256,128]{1,0:T(8,128)S(1)} %bitcast.7, f32[32,128]{1,0:T(8,128)S(1)} %copy-done.6), custom_call_target="tpu_custom_call" | custom-call | bytes 6000000 | tf_op jit(solution)/shard_map/pallas_call | solution.py:403
  21.1 6.5 %all-to-all-done = f32[128,2,128]{2,1,0:T(2,128)S(1)} async-done(((f32[128,2,128]{2,1,0:T(2,128)}), f32[128,2,128]{2,1,0:T(2,128)S(1)}, u32[]{:S(2)}, u32[]{:S(2)}) %all-to-all-start) | async-done | bytes 131104 | tf_op jit(solution)/shard_map/all_to_all | solution.py:402
  27.6 0.0 collective-permute-done.2.left
  27.6 0.0 collective-permute-done.3.right
  27.6 7.1 %shard_map.134 = (f32[256,128]{1,0:T(8,128)}, f32[2,2,9,64,128]{4,3,2,1,0:T(8,128)S(1)}) custom-call(f32[10,32,128]{2,1,0:T(8,128)S(1)} %copy-done, f32[10,32,128]{2,1,0:T(8,128)S(1)} %copy-done.1, f32[10,32,128]{2,1,0:T(8,128)S(1)} %copy-done.2, f32[10,32,128]{2,1,0:T(8,128)S(1)} %copy-done.3, f32[4,10,8,128]{3,2,1,0:T(8,128)S(1)} %collective-permute-done.low, ...), custom_call_target="tpu_custom_call" | custom-call | bytes 15000000 | tf_op jit(solution)/shard_map/pallas_call | solution.py:408
  34.7 5.2 %all-to-all-start.1 = ((f32[128,2,128]{2,1,0:T(2,128)}), f32[128,2,128]{2,1,0:T(2,128)S(1)}, u32[]{:S(2)}, u32[]{:S(2)}) async-start(f32[128,2,128]{2,1,0:T(2,128)} %bitcast.4), calls=%async_computation.1 | async-start | bytes 262144 | tf_op jit(solution)/shard_map/all_to_all | solution.py:423
  39.9 3.1 %shard_map.135 = (f32[10,32,128]{2,1,0:T(8,128)}, f32[256,256]{1,0:T(8,128)S(1)}) custom-call(f32[10,32,128]{2,1,0:T(8,128)S(1)} %copy-done, f32[10,32,128]{2,1,0:T(8,128)S(1)} %copy-done.1, f32[10,32,128]{2,1,0:T(8,128)S(1)} %copy-done.2, f32[10,32,128]{2,1,0:T(8,128)S(1)} %copy-done.3, f32[4,10,8,128]{3,2,1,0:T(8,128)S(1)} %collective-permute-done.low, ...), custom_call_target="tpu_custom_call" | custom-call | bytes 15000000 | tf_op jit(solution)/shard_map/pallas_call | solution.py:424
  43.0 7.0 %all-to-all-done.1 = f32[128,2,128]{2,1,0:T(2,128)S(1)} async-done(((f32[128,2,128]{2,1,0:T(2,128)}), f32[128,2,128]{2,1,0:T(2,128)S(1)}, u32[]{:S(2)}, u32[]{:S(2)}) %all-to-all-start.1) | async-done | bytes 131104 | tf_op jit(solution)/shard_map/all_to_all | solution.py:423
  50.0 0.7 %shard_map.136 = f32[1,256]{1,0:T(1,128)} custom-call(f32[256,128]{1,0:T(8,128)S(1)} %bitcast.10, f32[256,256]{1,0:T(8,128)S(1)} %get-tuple-element.19.routed), custom_call_target="tpu_custom_call" | custom-call | bytes 3000000 | tf_op jit(solution)/shard_map/pallas_call | solution.py:436
  (2 shorter events, 0.0 us)
Async XLA Ops:
  0.6 16.9 %copy-start.3 = (f32[10,32,128]{2,1,0:T(8,128)S(1)}, f32[10,32,128]{2,1,0:T(8,128)}, u32[]{:S(2)}) copy-start(f32[10,32,128]{2,1,0:T(8,128)} %storage.7) | copy-start | bytes 491524
  0.6 16.9 %copy-start.2 = (f32[10,32,128]{2,1,0:T(8,128)S(1)}, f32[10,32,128]{2,1,0:T(8,128)}, u32[]{:S(2)}) copy-start(f32[10,32,128]{2,1,0:T(8,128)} %source.7) | copy-start | bytes 491524
  0.7 16.9 %copy-start.1 = (f32[10,32,128]{2,1,0:T(8,128)S(1)}, f32[10,32,128]{2,1,0:T(8,128)}, u32[]{:S(2)}) copy-start(f32[10,32,128]{2,1,0:T(8,128)} %cond.7) | copy-start | bytes 491524
  0.7 16.9 %copy-start = (f32[10,32,128]{2,1,0:T(8,128)S(1)}, f32[10,32,128]{2,1,0:T(8,128)}, u32[]{:S(2)}) copy-start(f32[10,32,128]{2,1,0:T(8,128)} %head.7) | copy-start | bytes 491524
  0.7 19.1 %copy-start.5 = (s32[1,256,128]{2,1,0:T(8,128)S(1)}, s32[1,256,128]{2,1,0:T(8,128)}, u32[]{:S(2)}) copy-start(s32[1,256,128]{2,1,0:T(8,128)} %param.17) | copy-start | bytes 393220
  0.7 19.1 %copy-start.6 = (f32[32,128]{1,0:T(8,128)S(1)}, f32[32,128]{1,0:T(8,128)}, u32[]{:S(2)}) copy-start(f32[32,128]{1,0:T(8,128)} %bed.1) | copy-start | bytes 49156
  3.9 13.6 %collective-permute-start = (f32[4,10,8,128]{3,2,1,0:T(8,128)}, f32[4,10,8,128]{3,2,1,0:T(8,128)S(1)}, u32[]{:S(2)}, u32[]{:S(2)}) collective-permute-start(f32[4,10,8,128]{3,2,1,0:T(8,128)} %get-tuple-element.11), channel_id=1, source_target_pairs={{0,8},{8,16},{16,24},{24,32},{32,40},{40,48},{48,56},{56,64},{64,7... | collective-permute-start | bytes 491528 | tf_op jit(solution)/shard_map/ppermute | solution.py:364
  6.0 11.5 %collective-permute-start.1 = (f32[4,10,8,128]{3,2,1,0:T(8,128)}, f32[4,10,8,128]{3,2,1,0:T(8,128)S(1)}, u32[]{:S(2)}, u32[]{:S(2)}) collective-permute-start(f32[4,10,8,128]{3,2,1,0:T(8,128)} %get-tuple-element.12), channel_id=1, source_target_pairs={{0,120},{8,0},{16,8},{24,16},{32,24},{40,32},{48,40},{56,48},{64,5... | collective-permute-start | bytes 491528 | tf_op jit(solution)/shard_map/ppermute | solution.py:364
  10.9 16.7 %all-to-all-start = ((f32[128,2,128]{2,1,0:T(2,128)}), f32[128,2,128]{2,1,0:T(2,128)S(1)}, u32[]{:S(2)}, u32[]{:S(2)}) async-start(f32[128,2,128]{2,1,0:T(2,128)} %bitcast.11), calls=%async_computation | async-start | bytes 262144 | tf_op jit(solution)/shard_map/all_to_all | solution.py:402
  18.1 21.7 %copy-start.4 = (f32[1,256,256]{2,1,0:T(8,128)S(1)}, f32[1,256,256]{2,1,0:T(8,128)}, u32[]{:S(2)}) copy-start(f32[1,256,256]{2,1,0:T(8,128)} %route.1) | copy-start | bytes 786436
  18.1 21.7 %copy-start.7 = (s32[1,256]{1,0:T(1,128)S(1)}, s32[1,256]{1,0:T(1,128)}, u32[]{:S(2)}) copy-start(s32[1,256]{1,0:T(1,128)} %reach.3) | copy-start | bytes 3076
  18.2 9.4 %collective-permute-start.2 = (f32[3,48,128]{2,1,0:T(8,128)S(1)}, f32[3,48,128]{2,1,0:T(8,128)S(1)}, u32[]{:S(2)}, u32[]{:S(2)}) collective-permute-start(f32[3,48,128]{2,1,0:T(8,128)S(1)} %get-tuple-element.13), channel_id=1, source_target_pairs={{0,1},{1,2},{2,3},{3,4},{4,5},{5,6},{6,7},{7,0},{8,9},{9,10},{10,1... | collective-permute-start | bytes 221192 | tf_op jit(solution)/shard_map/ppermute | solution.py:364
  19.8 7.8 %collective-permute-start.3 = (f32[3,48,128]{2,1,0:T(8,128)S(1)}, f32[3,48,128]{2,1,0:T(8,128)S(1)}, u32[]{:S(2)}, u32[]{:S(2)}) collective-permute-start(f32[3,48,128]{2,1,0:T(8,128)S(1)} %get-tuple-element.14), channel_id=1, source_target_pairs={{0,7},{1,0},{2,1},{3,2},{4,3},{5,4},{6,5},{7,6},{8,15},{9,8},{10,9... | collective-permute-start | bytes 221192 | tf_op jit(solution)/shard_map/ppermute | solution.py:364
  34.7 15.3 %all-to-all-start.1 = ((f32[128,2,128]{2,1,0:T(2,128)}), f32[128,2,128]{2,1,0:T(2,128)S(1)}, u32[]{:S(2)}, u32[]{:S(2)}) async-start(f32[128,2,128]{2,1,0:T(2,128)} %bitcast.4), calls=%async_computation.1 | async-start | bytes 262144 | tf_op jit(solution)/shard_map/all_to_all | solution.py:423

commit v4 on v2

v4 whole, which is shorter than its diff:
```python
import functools

import jax
import jax.numpy as jnp
from jax import lax
from jax.experimental import pallas as pl
from jax.experimental.pallas import tpu as pltpu
from jax.sharding import PartitionSpec as P

SWEEPS = 8
HALO = 8
LANES = 128
GROUPS = LANES // HALO
AXES = ("gx", "gy")
VMEM = pl.BlockSpec(memory_space=pltpu.VMEM)
ANY = pl.BlockSpec(memory_space=pl.ANY)
TOP, BOTTOM = HALO, 2 * HALO


def call(body, out, count, scratch=(), anywhere=False, mib=8, micros=1):
    return pl.pallas_call(
        body,
        out_shape=out,
        in_specs=[ANY if anywhere else VMEM] * count,
        out_specs=jax.tree.map(lambda _: VMEM, out),
        scratch_shapes=list(scratch),
        compiler_params=pltpu.CompilerParams(vmem_limit_bytes=mib * 1024 * 1024),
        cost_estimate=pl.CostEstimate(
            flops=0, transcendentals=0, bytes_accessed=micros * 3_000_000
        ),
    )


def f32(*shape):
    return jax.ShapeDtypeStruct(shape, jnp.float32)


def front(
    head, cond, source, storage, reach, section, depth, route, retention, heads,
    last_out, first_out, info_out,
    reach_here, section_here, depth_here, weight_here, retention_here, heads_here, sems,
):
    rows = head.shape[1]
    reaches = section.shape[1]
    edges = []
    for k, ref in enumerate((head, cond, source, storage)):
        edges.append((ref.at[:, rows - HALO :, :], last_out.at[k]))
        edges.append((ref.at[:, :HALO, :], first_out.at[k]))
    small = [
        (reach, reach_here),
        (section, section_here),
        (depth, depth_here),
        (route.at[0, reaches - 8 :, :], weight_here),
        (retention, retention_here),
        (heads, heads_here),
    ]
    copies = [pltpu.make_async_copy(a, b, sems.at[i]) for i, (a, b) in enumerate(small + edges)]
    for copy in copies:
        copy.start()
    for copy in copies[: len(small)]:
        copy.wait()
    carry = retention_here[0] * (1.0 - heads_here[0].astype(jnp.float32))
    sec = section_here[...]
    table = jnp.concatenate(
        [sec, sec - depth_here[...], weight_here[7:8, :], jnp.full((5, reaches), carry)], 0
    )
    count = reach.shape[1]
    for part in range(count // LANES):
        spots = jnp.broadcast_to(reach_here[:, part * LANES : (part + 1) * LANES], (8, LANES))
        picked = jnp.zeros((8, LANES), jnp.float32)
        for block in range(reaches // LANES):
            value = jnp.take_along_axis(
                table[:, block * LANES : (block + 1) * LANES],
                spots & (LANES - 1),
                axis=1,
                mode="promise_in_bounds",
            )
            picked = jnp.where(spots // LANES == block, value, picked)
        tall = jnp.concatenate([picked, jnp.zeros((LANES - 8, LANES), jnp.float32)], 0)
        info_out[part * LANES : (part + 1) * LANES, :] = jnp.transpose(tall)
    for copy in copies[len(small) :]:
        copy.wait()


def pack_y(head, cond, source, storage, low, high, last_out, first_out):
    layers, rows, width = head.shape
    lane = lax.broadcasted_iota(jnp.int32, (rows + 2 * HALO, LANES), 1)
    first_sum = [None] * last_out.shape[0]
    last_sum = [None] * last_out.shape[0]
    for k, ref in enumerate((head, cond, source, storage)):
        for l in range(layers):
            plane, group = divmod(k * layers + l, GROUPS)
            whole = jnp.concatenate([low[k, l], ref[l], high[k, l]], 0)
            mine = (lane >= group * HALO) & (lane < (group + 1) * HALO)
            first = pltpu.roll(whole, group * HALO, 1) if group else whole
            turn = (group + 1) * HALO % LANES
            last = pltpu.roll(whole, turn, 1) if turn else whole
            if first_sum[plane] is None:
                first_sum[plane], last_sum[plane] = first, last
            else:
                first_sum[plane] = jnp.where(mine, first, first_sum[plane])
                last_sum[plane] = jnp.where(mine, last, last_sum[plane])
    for plane in range(last_out.shape[0]):
        first_out[plane] = first_sum[plane]
        last_out[plane] = last_sum[plane]


def select_cells(cells_ref, table, finish):
    half = cells_ref.shape[0] // 16
    for b in range(2 * half):
        c, g = divmod(b, half)
        cells = cells_ref[pl.ds(g * 16 + c, 8, stride=2), :]
        column, line = cells & (LANES - 1), cells // LANES
        found = jnp.zeros((8, LANES), jnp.float32)
        for r, spread in enumerate(table):
            value = jnp.take_along_axis(spread, column, axis=1, mode="promise_in_bounds")
            found = jnp.where(line == r, value, found)
        finish(slice(b * 8, (b + 1) * 8), found)


def spread_rows(table):
    return [jnp.broadcast_to(table[r : r + 1, :], (8, LANES)) for r in range(table.shape[0])]


def tall_row(fields, low, high, k, l):
    return jnp.concatenate([low[k, l], fields[k][l], high[k, l]], 0)


def turned(value, by):
    return pltpu.roll(value, by % LANES, 1) if by % LANES else value


def side_tiles(fields, low, high, left, right):
    layers = fields[0].shape[0]

    def get(k, l):
        plane, group = divmod(k * layers + l, GROUPS)
        whole = tall_row(fields, low, high, k, l)
        lane = lax.broadcasted_iota(jnp.int32, whole.shape, 1)
        after = turned(right[plane], -group * HALO)
        ahead = turned(left[plane], LANES - HALO - group * HALO)
        side = jnp.where(lane < HALO, after, jnp.where(lane >= LANES - HALO, ahead, 0.0))
        return [whole, side]

    return get


def strip_tiles(strips, left, right, layers):
    def get(k, l):
        plane, group = divmod(k * layers + l, GROUPS)
        lane = lax.broadcasted_iota(jnp.int32, left.shape[1:], 1)
        after = turned(right[plane], 2 * HALO - group * HALO)
        ahead = turned(left[plane], 3 * HALO - group * HALO)
        own = strips[k, l]
        inner = jnp.where(lane < 3 * HALO, after, ahead)
        return [jnp.where((lane >= 2 * HALO) & (lane < 4 * HALO), inner, own)]

    return get


def inside_rows(row):
    at_x = lax.axis_index("gx")
    first_row = jnp.where(at_x == 0, HALO, 0)
    last_row = jnp.where(at_x == lax.axis_size("gx") - 1, row.shape[0] - HALO, row.shape[0])
    return (row >= first_row) & (row < last_row)


def beside(tiles):
    lane = lax.broadcasted_iota(jnp.int32, tiles[0].shape, 1)
    ahead = [pltpu.roll(one, LANES - 1, 1) for one in tiles]
    behind = [pltpu.roll(one, 1, 1) for one in tiles]
    if len(tiles) == 1:
        return ahead, behind
    east = [jnp.where(lane == LANES - 1, ahead[1 - t], ahead[t]) for t in range(2)]
    west = [jnp.where(lane == 0, behind[1 - t], behind[t]) for t in range(2)]
    return east, west


def set_coefs(get, conds, coef, l, bottom):
    tiles, rows = conds.shape[0], conds.shape[2]
    span = slice(TOP, rows - TOP)
    east, west = beside([conds[t, l, span, :] for t in range(tiles)])
    storage, source = get(3, l), get(2, l)
    for t in range(tiles):
        mid = conds[t, l, span, :]
        inside = mid > 0.0

        def face(near):
            return jnp.where(inside & (near > 0.0), 0.5 * (mid + near), 0.0)

        faces = [
            face(east[t]),
            face(west[t]),
            face(conds[t, l, TOP + 1 : rows - TOP + 1, :]),
            face(conds[t, l, TOP - 1 : rows - TOP - 1, :]),
            0.5 * (mid + conds[t, l - 1, span, :]) if l else None,
            None if bottom else 0.5 * (mid + conds[t, l + 1, span, :]),
        ]
        total = storage[t]
        for one in faces:
            if one is not None:
                total = total + one
        inverse = jnp.where(inside, 1.0 / jnp.where(inside, total, 1.0), 0.0)
        for k, one in enumerate(faces):
            if one is not None:
                coef[k, t, l] = one * inverse
        coef[6, t, l] = source[t] * inverse


def relax(get, masks, heads, coef, conds, layers, cone, final):
    tiles, held, rows = heads.shape[1:4]
    edge = jnp.zeros((TOP, LANES), jnp.float32)
    for l in range(held):
        for t, value in enumerate(get(0, l)):
            heads[0, t, l, TOP : rows - TOP, :] = value
        for t, value in enumerate(get(1, l)):
            conds[t, l, TOP : rows - TOP, :] = jnp.where(masks[t], value, 0.0)
            for span in (slice(0, TOP), slice(rows - TOP, rows)):
                conds[t, l, span, :] = edge
                heads[0, t, l, span, :] = edge
                heads[1, t, l, span, :] = edge
    for l in range(held - 1 if cone else held):
        set_coefs(get, conds, coef, l, l + 1 == layers)
    for time in range(SWEEPS):
        last_sweep = time == SWEEPS - 1
        margin = BOTTOM if last_sweep else TOP
        many = SWEEPS - time if cone else layers
        old = time % 2
        for start in range(margin, rows - margin, 8):
            span = slice(start, start + 8)
            mids = [
                [heads[old, t, l, span, :] for t in range(tiles)]
                for l in range(min(many + 1, layers))
            ]
            for l in range(many):
                east, west = beside(mids[l])
                at = slice(start - TOP, start - TOP + 8)
                for t in range(1 if last_sweep else tiles):
                    out = coef[6, t, l, at, :] + coef[0, t, l, at, :] * east[t]
                    out = out + coef[1, t, l, at, :] * west[t]
                    out = out + coef[2, t, l, at, :] * heads[old, t, l, start + 1 : start + 9, :]
                    out = out + coef[3, t, l, at, :] * heads[old, t, l, start - 1 : start + 7, :]
                    if l:
                        out = out + coef[4, t, l, at, :] * mids[l - 1][t]
                    if l + 1 < layers:
                        out = out + coef[5, t, l, at, :] * mids[l + 1][t]
                    if last_sweep:
                        final(l, start - BOTTOM, out)
                    else:
                        heads[1 - old, t, l, span, :] = out


def inner(
    head, cond, source, storage, low, high, cells, bed,
    beds_out, top_out, strips_out, heads, coef, conds,
):
    fields = (head, cond, source, storage)
    layers, rows, width = head.shape
    tall = rows + 2 * HALO
    lane = lax.broadcasted_iota(jnp.int32, (tall, LANES), 1)
    for k in range(4):
        for l in range(SWEEPS + 1 if k < 2 else SWEEPS):
            whole = tall_row(fields, low, high, k, l)
            strip = jnp.where(lane < 2 * HALO, turned(whole, 2 * HALO), turned(whole, 4 * HALO))
            strips_out[k, l] = jnp.where(lane < 6 * HALO, strip, 0.0)

    def keep(span, value):
        beds_out[span, :] = value

    select_cells(cells, spread_rows(bed[...]), keep)

    def final(l, start, value):
        top_out[start : start + 8, :] = value

    inside = inside_rows(lax.broadcasted_iota(jnp.int32, (tall, LANES), 0))
    relax(
        lambda k, l: [tall_row(fields, low, high, k, l)], [inside],
        heads, coef, conds, layers, True, final,
    )


def edges(layers, strips, left, right, top, table, heads, coef, conds):
    tall = top.shape[0] + 2 * HALO
    lane = lax.broadcasted_iota(jnp.int32, (tall, LANES), 1)
    at_y = lax.axis_index("gy")
    first = (at_y == 0) & (lane >= 3 * HALO) & (lane < 4 * HALO)
    last = (at_y == lax.axis_size("gy") - 1) & (lane >= 2 * HALO) & (lane < 3 * HALO)
    inside = inside_rows(lax.broadcasted_iota(jnp.int32, (tall, LANES), 0))
    mask = inside & ~first & ~last & (lane < 6 * HALO)

    def final(l, start, value):
        span = slice(start, start + 8)
        column = lax.broadcasted_iota(jnp.int32, value.shape, 1)
        ends = jnp.where(column < HALO, turned(value, -4 * HALO), turned(value, -2 * HALO))
        table[span, :] = jnp.where(
            (column < HALO) | (column >= LANES - HALO), ends, top[span, :]
        )

    relax(
        strip_tiles(strips, left, right, layers), [mask],
        heads, coef, conds, layers, True, final,
    )


def leak_rows(table, cells, beds, info, send_out, weights, levels, leaks):
    peers = info.shape[0] // 2
    groups = peers // 8
    for c in range(2):
        for g in range(groups):
            detail = info[pl.ds(g * 16 + c, 8, stride=2), :]
            span = slice((c * groups + g) * 8, (c * groups + g + 1) * 8)
            for k in range(2):
                levels[k, span, :] = jnp.broadcast_to(detail[:, k : k + 1], (8, LANES))

    sub = lax.broadcasted_iota(jnp.int32, (peers, LANES), 0)
    lane = lax.broadcasted_iota(jnp.int32, (peers, LANES), 1)
    details = [info[pl.ds(c, peers, stride=2), :] for c in range(2)]
    carry_row = jnp.sum(jnp.where(sub == lane, details[0][:, 3:4], 0.0), 0, keepdims=True)
    product = jnp.where(lane > sub, carry_row, 1.0)
    step = 1
    while step < LANES:
        product = product * jnp.where(lane >= step, pltpu.roll(product, step, 1), 1.0)
        step *= 2
    product = jnp.where(lane > sub, product, 0.0)
    for c in range(2):
        weights[c] = product * details[c][:, 2:3]

    def leak(span, value):
        leaks[span, :] = beds[span, :] * (
            jnp.maximum(value, levels[1, span, :]) - levels[0, span, :]
        )

    select_cells(cells, spread_rows(table[...]), leak)
    eight = lax.broadcasted_iota(jnp.int32, (8, LANES), 1)
    flow = jnp.zeros((8, LANES), jnp.float32)
    sums = []
    for g in range(groups):
        span = slice(g * 8, (g + 1) * 8)
        row_leak = [
            jnp.sum(leaks[c * peers + g * 8 : c * peers + (g + 1) * 8, :], 1, keepdims=True)
            for c in range(2)
        ]
        for c in range(2):
            flow = flow + weights[c, span, :] * row_leak[c]
        sums.append(jnp.where(eight == 0, row_leak[0], row_leak[1]))
    flow = jnp.sum(flow, 0, keepdims=True)
    for g in range(groups):
        mine = lax.broadcasted_iota(jnp.int32, (8, LANES), 0) + g * 8 == eight
        column = jnp.sum(jnp.where(mine, flow, 0.0), 1, keepdims=True)
        send_out[g * 8 : (g + 1) * 8, :] = jnp.where(eight == 2, column, sums[g])


def everywhere(
    head, cond, source, storage, low, high, left, right, reach, route,
    field_out, routed_out, heads, coef, conds, lines,
):
    fields = (head, cond, source, storage)
    layers, rows, width = head.shape
    tall = rows + 2 * HALO
    lane = lax.broadcasted_iota(jnp.int32, (tall, LANES), 1)
    inside = inside_rows(lax.broadcasted_iota(jnp.int32, (tall, LANES), 0))
    at_y = lax.axis_index("gy")
    after = jnp.where(at_y == lax.axis_size("gy") - 1, 0, HALO)
    ahead = jnp.where(at_y == 0, LANES, LANES - HALO)

    def final(l, start, value):
        field_out[l, start : start + 8, :] = value

    relax(
        side_tiles(fields, low, high, left, right),
        [inside, inside & ((lane < after) | (lane >= ahead))],
        heads, coef, conds, layers, False, final,
    )
    count, reaches = routed_out.shape
    line = lax.broadcasted_iota(jnp.int32, (reaches, count), 0)
    routed = lax.dot_general(
        (line == reach[...]).astype(jnp.float32),
        route[...],
        (((0,), (1,)), ((), ())),
        precision=lax.Precision.HIGHEST,
        preferred_element_type=jnp.float32,
    )
    for part in range(reaches // LANES):
        lines[part] = routed[:, part * LANES : (part + 1) * LANES]
    for part in range(reaches // LANES):
        for c in range(2):
            routed_out[c * (count // 2) : (c + 1) * (count // 2), part * LANES : (part + 1) * LANES] = (
                lines[part, pl.ds(c, count // 2, stride=2), :]
            )


def finish_flow(arrived, routed, out):
    half = arrived.shape[0]
    parts = arrived[...]
    flow = parts[:, 0:1] * routed[:half, :] + parts[:, 1:2] * routed[half:, :]
    out[...] = jnp.sum(flow + parts[:, 2:3], 0, keepdims=True)


def shifted(value, axis, by):
    count = lax.axis_size(axis)
    return lax.ppermute(value, axis, [(i, (i + by) % count) for i in range(count)])


def per_device(
    initial_head, conductivity, source_rate, storage_term, bed_conduct, row_cells, row_reach,
    river_section, bed_depth, route_inverse, retention, chain_heads,
):
    layers, rows, width = initial_head.shape
    fields = (initial_head, conductivity, source_rate, storage_term)
    edge = f32(4, layers, HALO, width)
    planes = -(-4 * layers // GROUPS)
    tall = rows + 2 * HALO
    side = f32(planes, tall, LANES)
    row_total = row_cells.shape[1]
    reaches = river_section.shape[1]
    cells = row_cells[0]

    def scratch(*shape):
        return pltpu.VMEM(shape, jnp.float32)

    last, first, info = call(
        front,
        (edge, edge, f32(row_total, LANES)),
        10,
        scratch=(
            pltpu.VMEM((1, row_total), jnp.int32),
            scratch(1, reaches),
            scratch(1, reaches),
            scratch(8, reaches),
            pltpu.SMEM((1,), jnp.float32),
            pltpu.SMEM((1,), jnp.int32),
            pltpu.SemaphoreType.DMA((14,)),
        ),
        anywhere=True,
        mib=60,
    )(*fields, row_reach, river_section, bed_depth, route_inverse, retention, chain_heads)
    low = shifted(last, "gx", 1)
    high = shifted(first, "gx", -1)
    info = lax.all_to_all(info, AXES, split_axis=0, concat_axis=0, tiled=True)
    last, first = call(pack_y, (side, side), 6)(*fields, low, high)
    left = shifted(last, "gy", 1)
    right = shifted(first, "gy", -1)
    pads = tall + 2 * TOP
    held = SWEEPS + 1
    own = (
        scratch(2, 1, held, pads, LANES),
        scratch(7, 1, SWEEPS, tall, LANES),
        scratch(1, held, pads, LANES),
    )
    beds, top, strips = call(
        inner,
        (f32(row_total, LANES), f32(rows, width), f32(4, held, tall, LANES)),
        8,
        scratch=own,
        mib=16,
        micros=3,
    )(*fields, low, high, cells, bed_conduct)
    table = call(
        functools.partial(edges, layers), f32(rows, width), 4, scratch=own, mib=16, micros=2
    )(strips, left, right, top)
    sent = call(
        leak_rows,
        f32(row_total // 2, LANES),
        4,
        scratch=(
            scratch(2, row_total // 2, LANES),
            scratch(2, row_total, LANES),
            scratch(row_total, LANES),
        ),
        micros=3,
    )(table, cells, beds, info)
    arrived = lax.all_to_all(sent, AXES, split_axis=0, concat_axis=0, tiled=True)
    head_field, routed = call(
        everywhere,
        (f32(layers, rows, width), f32(row_total, reaches)),
        10,
        scratch=(
            scratch(2, 2, layers, pads, LANES),
            scratch(7, 2, layers, tall, LANES),
            scratch(2, layers, pads, LANES),
            scratch(reaches // LANES, row_total, LANES),
        ),
        mib=20,
        micros=5,
    )(*fields, low, high, left, right, row_reach, route_inverse[0])
    reach_flow = call(finish_flow, f32(1, reaches), 2)(arrived, routed)
    return (head_field, reach_flow)


def solution(mesh):
    placed = (
        P(None, "gx", "gy"),
        P(None, "gx", "gy"),
        P(None, "gx", "gy"),
        P(None, "gx", "gy"),
        P("gx", "gy"),
        P(AXES, None, None),
        P(AXES, None),
        P(AXES, None),
        P(AXES, None),
        P(AXES, None, None),
        P(AXES),
        P(AXES),
    )
    return jax.shard_map(
        per_device,
        mesh=mesh,
        in_specs=placed,
        out_specs=(P(None, "gx", "gy"), P(AXES, None)),
        check_vma=False,
    )
```

time: 58.6 us -> 47.1 us (0.80)
  starting transfers between devices: 31.9 us -> 21.8 us
  waiting for transfers between devices: 9.63 us -> 8.41 us
  local copies, waits for them, and re-layouts: 0.04 us -> 0.7 us
  Pallas kernels: 14.4 us -> 13.8 us
    all_to_all x1, starting transfers between devices: 12.1 us -> 6.66 us  [per_device(): info = lax.all_to_all(info, AXES, split_axis=0, concat_axis=0, tiled=True)]
    all_to_all x1, waiting for transfers between devices: 7.03 us -> 4.57 us  [per_device(): lax.all_to_all(sent, AXES, split_axis=0, concat_axis=0, tiled=True)]
    all_to_all x1, starting transfers between devices: 8.96 us -> 6.59 us  [per_device(): lax.all_to_all(sent, AXES, split_axis=0, concat_axis=0, tiled=True)]
    ppermute x4, starting transfers between devices: 10.8 us -> 8.58 us  [shifted(): lax.ppermute(value, axis, [(i, (i + by) % count) for i in range(count)])]
    ppermute x4, waiting for transfers between devices: 0.09 us -> 1.62 us  [shifted(): lax.ppermute(value, axis, [(i, (i + by) % count) for i in range(count)])]
    pallas_call x3 -> x4, Pallas kernels: 11.3 us -> 10.6 us  [the longest x1 4.36 us: per_device(): call(everywhere, (f32(layers, rows, width), f32(row_total, reaches)), 10,...]
    unnamed x16, local copies, waits for them, and re-layouts: 0.04 us -> 0.7 us
  transfers between devices with their start and end apart: 6 -> 6, of which waited for: 3 -> 3; matrix products, arithmetic and copies ran while one was open for 0% -> 0% of each run, Pallas kernels for 8% -> 19%
where the time goes in v4:
time: 47.1 us; the launch traced here: 46.9 us
  starting transfers between devices  21.8 us (46%)
  Pallas kernels  13.8 us (29%)
  waiting for transfers between devices  8.41 us (18%)
  between operations  2.09 us (4%)
  local copies, waits for them, and re-layouts  0.7 us (1%)
    ppermute x4, starting transfers between devices, shifted(): lax.ppermute(value, axis, [(i, (i + by) % count) for i in range(count)])  8.58 us
    all_to_all x1, starting transfers between devices, per_device(): info = lax.all_to_all(info, AXES, split_axis=0, concat_axis=0, tiled=True)  6.66 us
    all_to_all x1, starting transfers between devices, per_device(): lax.all_to_all(sent, AXES, split_axis=0, concat_axis=0, tiled=True)  6.59 us
    all_to_all x1, waiting for transfers between devices, per_device(): lax.all_to_all(sent, AXES, split_axis=0, concat_axis=0, tiled=True)  4.57 us
    pallas_call x1, Pallas kernels, per_device(): call(everywhere, (f32(layers, rows, width), f32(row_total, reaches)), 10,...  4.36 us
    pallas_call x1, Pallas kernels, per_device(): call(inner, (f32(row_total, LANES), f32(rows, width), f32(4, held, tall,...  2.52 us
    pallas_call x1, Pallas kernels, per_device(): call(leak_rows, f32(row_total // 2, LANES), 4, scratch=(scratch(2, row_to...  2.41 us
    all_to_all x1, waiting for transfers between devices, per_device(): info = lax.all_to_all(info, AXES, split_axis=0, concat_axis=0, tiled=True)  2.23 us
  transfers between devices with their start and end apart: 6, of which 3 were waited for; matrix products, arithmetic and copies ran while one was open for 0% of the time, Pallas kernels for 19%

profile of v4, /device:TPU:1, one launch (start us, length us, event | category | flops | bytes accessed | tf_op | source)
XLA Modules:
  0.0 46.9 jit_solution(8669663589717558820)
XLA Ops:
  1.9 0.0 copy-start.1
  1.9 0.0 copy-start.2
  1.9 0.0 copy-start.3
  2.0 1.9 %shard_map.131 = (f32[4,10,8,128]{3,2,1,0:T(8,128)}, f32[4,10,8,128]{3,2,1,0:T(8,128)}, f32[256,128]{1,0:T(8,128)}) custom-call(f32[10,32,128]{2,1,0:T(8,128)} %head.7, f32[10,32,128]{2,1,0:T(8,128)} %cond.7, f32[10,32,128]{2,1,0:T(8,128)} %source.7, f32[10,32,128]{2,1,0:T(8,128)} %storage.7, s32[1,256]{1,0:T(1,128)} %reach.3, f32[1,256]{1,0:T(1,128)} %section.1, ...), custom_call_target="tpu_custom_call" | custom-call | bytes 3000000 | tf_op jit(solution)/shard_map/pallas_call | solution.py:421
  3.9 0.0 copy-start
  3.9 2.1 %collective-permute-start = (f32[4,10,8,128]{3,2,1,0:T(8,128)}, f32[4,10,8,128]{3,2,1,0:T(8,128)S(1)}, u32[]{:S(2)}, u32[]{:S(2)}) collective-permute-start(f32[4,10,8,128]{3,2,1,0:T(8,128)} %get-tuple-element.12), channel_id=1, source_target_pairs={{0,8},{8,16},{16,24},{24,32},{32,40},{40,48},{48,56},{56,64},{64,7... | collective-permute-start | bytes 491528 | tf_op jit(solution)/shard_map/ppermute | solution.py:401
  6.0 4.8 %collective-permute-start.1 = (f32[4,10,8,128]{3,2,1,0:T(8,128)}, f32[4,10,8,128]{3,2,1,0:T(8,128)S(1)}, u32[]{:S(2)}, u32[]{:S(2)}) collective-permute-start(f32[4,10,8,128]{3,2,1,0:T(8,128)} %get-tuple-element.13), channel_id=1, source_target_pairs={{0,120},{8,0},{16,8},{24,16},{32,24},{40,32},{48,40},{56,48},{64,5... | collective-permute-start | bytes 491528 | tf_op jit(solution)/shard_map/ppermute | solution.py:401
  10.8 6.7 %all-to-all-start = ((f32[128,2,128]{2,1,0:T(2,128)}), f32[128,2,128]{2,1,0:T(2,128)S(1)}, u32[]{:S(2)}, u32[]{:S(2)}) async-start(f32[128,2,128]{2,1,0:T(2,128)} %bitcast.13), calls=%async_computation | async-start | bytes 262144 | tf_op jit(solution)/shard_map/all_to_all | solution.py:439
  17.5 0.0 copy-start.5
  17.5 0.0 collective-permute-done.low
  17.5 0.0 collective-permute-done.1.high
  17.5 0.0 copy-done.1
  17.5 0.0 copy-done.2
  17.6 0.0 copy-done.3
  17.6 0.0 copy-done
  17.6 0.0 copy-start.6
  17.6 0.5 %shard_map.132 = (f32[3,48,128]{2,1,0:T(8,128)S(1)}, f32[3,48,128]{2,1,0:T(8,128)S(1)}) custom-call(f32[10,32,128]{2,1,0:T(8,128)S(1)} %copy-done, f32[10,32,128]{2,1,0:T(8,128)S(1)} %copy-done.1, f32[10,32,128]{2,1,0:T(8,128)S(1)} %copy-done.2, f32[10,32,128]{2,1,0:T(8,128)S(1)} %copy-done.3, f32[4,10,8,128]{3,2,1,0:T(8,128)S(1)} %collective-permute-done.low, ...), custom_call_target="tpu_custom_call" | custom-call | bytes 3000000 | tf_op jit(solution)/shard_map/pallas_call | solution.py:440
  18.1 1.6 %collective-permute-start.2 = (f32[3,48,128]{2,1,0:T(8,128)S(1)}, f32[3,48,128]{2,1,0:T(8,128)S(1)}, u32[]{:S(2)}, u32[]{:S(2)}) collective-permute-start(f32[3,48,128]{2,1,0:T(8,128)S(1)} %get-tuple-element.14), channel_id=1, source_target_pairs={{0,1},{1,2},{2,3},{3,4},{4,5},{5,6},{6,7},{7,0},{8,9},{9,10},{10,1... | collective-permute-start | bytes 221192 | tf_op jit(solution)/shard_map/ppermute | solution.py:401
  19.8 0.0 collective-permute-start.3
  19.8 0.0 copy-done.5
  19.8 2.5 %shard_map.134 = (f32[256,128]{1,0:T(8,128)S(1)}, f32[32,128]{1,0:T(8,128)S(1)}, f32[4,9,48,128]{3,2,1,0:T(8,128)S(1)}) custom-call(f32[10,32,128]{2,1,0:T(8,128)S(1)} %copy-done, f32[10,32,128]{2,1,0:T(8,128)S(1)} %copy-done.1, f32[10,32,128]{2,1,0:T(8,128)S(1)} %copy-done.2, f32[10,32,128]{2,1,0:T(8,128)S(1)} %copy-done.3, ...), custom_call_target="tpu_custom_call" | custom-call | bytes 9000000 | tf_op jit(solution)/shard_map/pallas_call | solution.py:450
  22.3 0.0 collective-permute-done.2.left
  22.3 1.6 %collective-permute-done.3.right = f32[3,48,128]{2,1,0:T(8,128)S(1)} collective-permute-done((f32[3,48,128]{2,1,0:T(8,128)S(1)}, f32[3,48,128]{2,1,0:T(8,128)S(1)}, u32[]{:S(2)}, u32[]{:S(2)}) %collective-permute-start.3) | collective-permute-done | bytes 73760 | tf_op jit(solution)/shard_map/ppermute | solution.py:401
  23.9 1.4 %shard_map.135.table = f32[32,128]{1,0:T(8,128)S(1)} custom-call(f32[4,9,48,128]{3,2,1,0:T(8,128)S(1)} %get-tuple-element.17.strips, f32[3,48,128]{2,1,0:T(8,128)S(1)} %collective-permute-done.2.left, f32[3,48,128]{2,1,0:T(8,128)S(1)} %collective-permute-done.3.right, f32[32,128]{1,0:T(8,128)S(1)} %get-tuple-element.18.top), custom_call_target="tpu_custom_call" | custom-call | bytes 6000000 | tf_op jit(solution)/shard_map/pallas_call | solution.py:458
  25.3 2.2 %all-to-all-done = f32[128,2,128]{2,1,0:T(2,128)S(1)} async-done(((f32[128,2,128]{2,1,0:T(2,128)}), f32[128,2,128]{2,1,0:T(2,128)S(1)}, u32[]{:S(2)}, u32[]{:S(2)}) %all-to-all-start) | async-done | bytes 131104 | tf_op jit(solution)/shard_map/all_to_all | solution.py:439
  27.5 2.4 %shard_map.136 = f32[128,128]{1,0:T(8,128)} custom-call(f32[32,128]{1,0:T(8,128)S(1)} %shard_map.135.table, s32[256,128]{1,0:T(8,128)S(1)} %bitcast.10, f32[256,128]{1,0:T(8,128)S(1)} %get-tuple-element.19.beds, f32[256,128]{1,0:T(8,128)S(1)} %bitcast.11), custom_call_target="tpu_custom_call" | custom-call | bytes 9000000 | tf_op jit(solution)/shard_map/pallas_call | solution.py:461
  29.9 6.6 %all-to-all-start.1 = ((f32[128,1,128]{2,1,0:T(1,128)}), f32[128,1,128]{2,1,0:T(1,128)S(1)}, u32[]{:S(2)}, u32[]{:S(2)}) async-start(f32[128,1,128]{2,1,0:T(1,128)} %bitcast.5), calls=%async_computation.1 | async-start | bytes 131072 | tf_op jit(solution)/shard_map/all_to_all | solution.py:472
  36.5 0.0 copy-start.7
  36.6 0.7 %copy-done.7 = s32[1,256]{1,0:T(1,128)S(1)} copy-done((s32[1,256]{1,0:T(1,128)S(1)}, s32[1,256]{1,0:T(1,128)}, u32[]{:S(2)}) %copy-start.7) | copy-done | bytes 1048
  37.2 4.4 %shard_map.133 = (f32[10,32,128]{2,1,0:T(8,128)}, f32[256,256]{1,0:T(8,128)S(1)}) custom-call(f32[10,32,128]{2,1,0:T(8,128)S(1)} %copy-done, f32[10,32,128]{2,1,0:T(8,128)S(1)} %copy-done.1, f32[10,32,128]{2,1,0:T(8,128)S(1)} %copy-done.2, f32[10,32,128]{2,1,0:T(8,128)S(1)} %copy-done.3, f32[4,10,8,128]{3,2,1,0:T(8,128)S(1)} %collective-permute-done.low, ...), custom_call_target="tpu_custom_call" | custom-call | bytes 15000000 | tf_op jit(solution)/shard_map/pallas_call | solution.py:473
  41.6 4.6 %all-to-all-done.1 = f32[128,1,128]{2,1,0:T(1,128)S(1)} async-done(((f32[128,1,128]{2,1,0:T(1,128)}), f32[128,1,128]{2,1,0:T(1,128)S(1)}, u32[]{:S(2)}, u32[]{:S(2)}) %all-to-all-start.1) | async-done | bytes 65568 | tf_op jit(solution)/shard_map/all_to_all | solution.py:472
  46.1 0.7 %shard_map.137 = f32[1,256]{1,0:T(1,128)} custom-call(f32[128,128]{1,0:T(8,128)S(1)} %bitcast.12, f32[256,256]{1,0:T(8,128)S(1)} %get-tuple-element.21.routed), custom_call_target="tpu_custom_call" | custom-call | bytes 3000000 | tf_op jit(solution)/shard_map/pallas_call | solution.py:486
  (3 shorter events, 0.0 us)
Async XLA Ops:
  1.9 15.6 %copy-start.1 = (f32[10,32,128]{2,1,0:T(8,128)S(1)}, f32[10,32,128]{2,1,0:T(8,128)}, u32[]{:S(2)}) copy-start(f32[10,32,128]{2,1,0:T(8,128)} %cond.7) | copy-start | bytes 491524
  1.9 15.6 %copy-start.2 = (f32[10,32,128]{2,1,0:T(8,128)S(1)}, f32[10,32,128]{2,1,0:T(8,128)}, u32[]{:S(2)}) copy-start(f32[10,32,128]{2,1,0:T(8,128)} %source.7) | copy-start | bytes 491524
  1.9 15.6 %copy-start.3 = (f32[10,32,128]{2,1,0:T(8,128)S(1)}, f32[10,32,128]{2,1,0:T(8,128)}, u32[]{:S(2)}) copy-start(f32[10,32,128]{2,1,0:T(8,128)} %storage.7) | copy-start | bytes 491524
  3.9 13.7 %copy-start = (f32[10,32,128]{2,1,0:T(8,128)S(1)}, f32[10,32,128]{2,1,0:T(8,128)}, u32[]{:S(2)}) copy-start(f32[10,32,128]{2,1,0:T(8,128)} %head.7) | copy-start | bytes 491524
  3.9 13.6 %collective-permute-start = (f32[4,10,8,128]{3,2,1,0:T(8,128)}, f32[4,10,8,128]{3,2,1,0:T(8,128)S(1)}, u32[]{:S(2)}, u32[]{:S(2)}) collective-permute-start(f32[4,10,8,128]{3,2,1,0:T(8,128)} %get-tuple-element.12), channel_id=1, source_target_pairs={{0,8},{8,16},{16,24},{24,32},{32,40},{40,48},{48,56},{56,64},{64,7... | collective-permute-start | bytes 491528 | tf_op jit(solution)/shard_map/ppermute | solution.py:401
  6.0 11.5 %collective-permute-start.1 = (f32[4,10,8,128]{3,2,1,0:T(8,128)}, f32[4,10,8,128]{3,2,1,0:T(8,128)S(1)}, u32[]{:S(2)}, u32[]{:S(2)}) collective-permute-start(f32[4,10,8,128]{3,2,1,0:T(8,128)} %get-tuple-element.13), channel_id=1, source_target_pairs={{0,120},{8,0},{16,8},{24,16},{32,24},{40,32},{48,40},{56,48},{64,5... | collective-permute-start | bytes 491528 | tf_op jit(solution)/shard_map/ppermute | solution.py:401
  10.8 16.7 %all-to-all-start = ((f32[128,2,128]{2,1,0:T(2,128)}), f32[128,2,128]{2,1,0:T(2,128)S(1)}, u32[]{:S(2)}, u32[]{:S(2)}) async-start(f32[128,2,128]{2,1,0:T(2,128)} %bitcast.13), calls=%async_computation | async-start | bytes 262144 | tf_op jit(solution)/shard_map/all_to_all | solution.py:439
  17.5 2.3 %copy-start.5 = (s32[1,256,128]{2,1,0:T(8,128)S(1)}, s32[1,256,128]{2,1,0:T(8,128)}, u32[]{:S(2)}) copy-start(s32[1,256,128]{2,1,0:T(8,128)} %param.17) | copy-start | bytes 393220
  17.6 2.2 %copy-start.6 = (f32[32,128]{1,0:T(8,128)S(1)}, f32[32,128]{1,0:T(8,128)}, u32[]{:S(2)}) copy-start(f32[32,128]{1,0:T(8,128)} %bed.1) | copy-start | bytes 49156
  18.1 4.2 %collective-permute-start.2 = (f32[3,48,128]{2,1,0:T(8,128)S(1)}, f32[3,48,128]{2,1,0:T(8,128)S(1)}, u32[]{:S(2)}, u32[]{:S(2)}) collective-permute-start(f32[3,48,128]{2,1,0:T(8,128)S(1)} %get-tuple-element.14), channel_id=1, source_target_pairs={{0,1},{1,2},{2,3},{3,4},{4,5},{5,6},{6,7},{7,0},{8,9},{9,10},{10,1... | collective-permute-start | bytes 221192 | tf_op jit(solution)/shard_map/ppermute | solution.py:401
  19.8 4.2 %collective-permute-start.3 = (f32[3,48,128]{2,1,0:T(8,128)S(1)}, f32[3,48,128]{2,1,0:T(8,128)S(1)}, u32[]{:S(2)}, u32[]{:S(2)}) collective-permute-start(f32[3,48,128]{2,1,0:T(8,128)S(1)} %get-tuple-element.15), channel_id=1, source_target_pairs={{0,7},{1,0},{2,1},{3,2},{4,3},{5,4},{6,5},{7,6},{8,15},{9,8},{10,9... | collective-permute-start | bytes 221192 | tf_op jit(solution)/shard_map/ppermute | solution.py:401
  27.5 9.0 %copy-start.4 = (f32[1,256,256]{2,1,0:T(8,128)S(1)}, f32[1,256,256]{2,1,0:T(8,128)}, u32[]{:S(2)}) copy-start(f32[1,256,256]{2,1,0:T(8,128)} %route.1) | copy-start | bytes 786436
  29.9 16.2 %all-to-all-start.1 = ((f32[128,1,128]{2,1,0:T(1,128)}), f32[128,1,128]{2,1,0:T(1,128)S(1)}, u32[]{:S(2)}, u32[]{:S(2)}) async-start(f32[128,1,128]{2,1,0:T(1,128)} %bitcast.5), calls=%async_computation.1 | async-start | bytes 131072 | tf_op jit(solution)/shard_map/all_to_all | solution.py:472
  36.5 0.7 %copy-start.7 = (s32[1,256]{1,0:T(1,128)S(1)}, s32[1,256]{1,0:T(1,128)}, u32[]{:S(2)}) copy-start(s32[1,256]{1,0:T(1,128)} %reach.3) | copy-start | bytes 3076

commit v5 on v4

--- a/solution.py
+++ b/solution.py
@@ -82,27 +82,30 @@
         copy.wait()
 
 
-def pack_y(head, cond, source, storage, low, high, last_out, first_out):
+def pack_y(head, cond, source, storage, low, high, even_out, odd_out):
+    fields = (head, cond, source, storage)
     layers, rows, width = head.shape
+    even_y = lax.axis_index("gy") % 2 == 0
     lane = lax.broadcasted_iota(jnp.int32, (rows + 2 * HALO, LANES), 1)
-    first_sum = [None] * last_out.shape[0]
-    last_sum = [None] * last_out.shape[0]
-    for k, ref in enumerate((head, cond, source, storage)):
+    first_sum = [None] * even_out.shape[0]
+    last_sum = [None] * even_out.shape[0]
+    for k in range(4):
         for l in range(layers):
             plane, group = divmod(k * layers + l, GROUPS)
-            whole = jnp.concatenate([low[k, l], ref[l], high[k, l]], 0)
-            mine = (lane >= group * HALO) & (lane < (group + 1) * HALO)
-            first = pltpu.roll(whole, group * HALO, 1) if group else whole
-            turn = (group + 1) * HALO % LANES
-            last = pltpu.roll(whole, turn, 1) if turn else whole
+            whole = tall_row(fields, (low, high), k, l)
+            spread = turned(whole, group * HALO)
             if first_sum[plane] is None:
-                first_sum[plane], last_sum[plane] = first, last
+                first_sum[plane], last_sum[plane] = spread, spread
             else:
-                first_sum[plane] = jnp.where(mine, first, first_sum[plane])
-                last_sum[plane] = jnp.where(mine, last, last_sum[plane])
-    for plane in range(last_out.shape[0]):
-        first_out[plane] = first_sum[plane]
-        last_out[plane] = last_sum[plane]
+                first_sum[plane] = jnp.where(
+                    lane // HALO == group, spread, first_sum[plane]
+                )
+                last_sum[plane] = jnp.where(
+                    lane // HALO == (group - 1) % GROUPS, spread, last_sum[plane]
+                )
+    for plane in range(even_out.shape[0]):
+        even_out[plane] = jnp.where(even_y, last_sum[plane], first_sum[plane])
+        odd_out[plane] = jnp.where(even_y, first_sum[plane], last_sum[plane])
 
 
 def select_cells(cells_ref, table, finish):
@@ -122,35 +125,43 @@
     return [jnp.broadcast_to(table[r : r + 1, :], (8, LANES)) for r in range(table.shape[0])]
 
 
-def tall_row(fields, low, high, k, l):
+def tall_row(fields, beside_x, k, l):
+    low, high = beside_x
     return jnp.concatenate([low[k, l], fields[k][l], high[k, l]], 0)
+
+
+def settle(one, other, sides):
+    even = lax.axis_index("gy") % 2 == 0
+    for plane in range(sides.shape[1]):
+        sides[0, plane] = jnp.where(even, other[plane], one[plane])
+        sides[1, plane] = jnp.where(even, one[plane], other[plane])
 
 
 def turned(value, by):
     return pltpu.roll(value, by % LANES, 1) if by % LANES else value
 
 
-def side_tiles(fields, low, high, left, right):
+def side_tiles(fields, beside_x, sides):
     layers = fields[0].shape[0]
 
     def get(k, l):
         plane, group = divmod(k * layers + l, GROUPS)
-        whole = tall_row(fields, low, high, k, l)
+        whole = tall_row(fields, beside_x, k, l)
         lane = lax.broadcasted_iota(jnp.int32, whole.shape, 1)
-        after = turned(right[plane], -group * HALO)
-        ahead = turned(left[plane], LANES - HALO - group * HALO)
-        side = jnp.where(lane < HALO, after, jnp.where(lane >= LANES - HALO, ahead, 0.0))
+        both = jnp.where(lane // HALO == group, sides[1, plane], sides[0, plane])
+        near = (lane < HALO) | (lane >= LANES - HALO)
+        side = jnp.where(near, turned(both, -group * HALO), 0.0)
         return [whole, side]
 
     return get
 
 
-def strip_tiles(strips, left, right, layers):
+def strip_tiles(strips, sides, layers):
     def get(k, l):
         plane, group = divmod(k * layers + l, GROUPS)
-        lane = lax.broadcasted_iota(jnp.int32, left.shape[1:], 1)
-        after = turned(right[plane], 2 * HALO - group * HALO)
-        ahead = turned(left[plane], 3 * HALO - group * HALO)
+        lane = lax.broadcasted_iota(jnp.int32, sides.shape[2:], 1)
+        after = turned(sides[1, plane], 2 * HALO - group * HALO)
+        ahead = turned(sides[0, plane], 3 * HALO - (group - 1) % GROUPS * HALO)
         own = strips[k, l]
         inner = jnp.where(lane < 3 * HALO, after, ahead)
         return [jnp.where((lane >= 2 * HALO) & (lane < 4 * HALO), inner, own)]
@@ -255,12 +266,13 @@
     beds_out, top_out, strips_out, heads, coef, conds,
 ):
     fields = (head, cond, source, storage)
+    beside_x = (low, high)
     layers, rows, width = head.shape
     tall = rows + 2 * HALO
     lane = lax.broadcasted_iota(jnp.int32, (tall, LANES), 1)
     for k in range(4):
         for l in range(SWEEPS + 1 if k < 2 else SWEEPS):
-            whole = tall_row(fields, low, high, k, l)
+            whole = tall_row(fields, beside_x, k, l)
             strip = jnp.where(lane < 2 * HALO, turned(whole, 2 * HALO), turned(whole, 4 * HALO))
             strips_out[k, l] = jnp.where(lane < 6 * HALO, strip, 0.0)
 
@@ -274,12 +286,13 @@
 
     inside = inside_rows(lax.broadcasted_iota(jnp.int32, (tall, LANES), 0))
     relax(
-        lambda k, l: [tall_row(fields, low, high, k, l)], [inside],
+        lambda k, l: [tall_row(fields, beside_x, k, l)], [inside],
         heads, coef, conds, layers, True, final,
     )
 
 
-def edges(layers, strips, left, right, top, table, heads, coef, conds):
+def edges(layers, strips, other_y, one_y, top, table, heads, coef, conds, sides):
+    settle(one_y, other_y, sides)
     tall = top.shape[0] + 2 * HALO
     lane = lax.broadcasted_iota(jnp.int32, (tall, LANES), 1)
     at_y = lax.axis_index("gy")
@@ -297,7 +310,7 @@
         )
 
     relax(
-        strip_tiles(strips, left, right, layers), [mask],
+        strip_tiles(strips, sides, layers), [mask],
         heads, coef, conds, layers, True, final,
     )
 
@@ -312,18 +325,28 @@
             for k in range(2):
                 levels[k, span, :] = jnp.broadcast_to(detail[:, k : k + 1], (8, LANES))
 
+    def running(value, lane, length):
+        step = 1
+        while step < length:
+            value = value * jnp.where(lane % length >= step, pltpu.roll(value, step, 1), 1.0)
+            step *= 2
+        return value
+
     sub = lax.broadcasted_iota(jnp.int32, (peers, LANES), 0)
     lane = lax.broadcasted_iota(jnp.int32, (peers, LANES), 1)
     details = [info[pl.ds(c, peers, stride=2), :] for c in range(2)]
     carry_row = jnp.sum(jnp.where(sub == lane, details[0][:, 3:4], 0.0), 0, keepdims=True)
-    product = jnp.where(lane > sub, carry_row, 1.0)
-    step = 1
-    while step < LANES:
-        product = product * jnp.where(lane >= step, pltpu.roll(product, step, 1), 1.0)
-        step *= 2
-    product = jnp.where(lane > sub, product, 0.0)
-    for c in range(2):
-        weights[c] = product * details[c][:, 2:3]
+    sub, lane = sub[:8], lane[:8]
+    within = running(jnp.where(lane % 8 > sub, carry_row, 1.0), lane, 8)
+    own = jnp.where(lane % 8 > sub, within, 0.0)
+    block = lax.broadcasted_iota(jnp.int32, (groups, LANES), 0)
+    wide = lax.broadcasted_iota(jnp.int32, (groups, LANES), 1)
+    beyond = running(jnp.where(wide > block * 8 + 7, carry_row, 1.0), wide, LANES)
+    for g in range(groups):
+        through = within[:, g * 8 + 7 : g * 8 + 8] * beyond[g : g + 1, :]
+        product = jnp.where(lane // 8 == g, own, jnp.where(lane // 8 > g, through, 0.0))
+        for c in range(2):
+            weights[c, g * 8 : (g + 1) * 8, :] = product * details[c][g * 8 : (g + 1) * 8, 2:3]
 
     def leak(span, value):
         leaks[span, :] = beds[span, :] * (
@@ -351,10 +374,12 @@
 
 
 def everywhere(
-    head, cond, source, storage, low, high, left, right, reach, route,
-    field_out, routed_out, heads, coef, conds, lines,
+    head, cond, source, storage, low, high, other_y, one_y, reach, route,
+    field_out, routed_out, heads, coef, conds, lines, sides,
 ):
     fields = (head, cond, source, storage)
+    beside_x = (low, high)
+    settle(one_y, other_y, sides)
     layers, rows, width = head.shape
     tall = rows + 2 * HALO
     lane = lax.broadcasted_iota(jnp.int32, (tall, LANES), 1)
@@ -367,7 +392,7 @@
         field_out[l, start : start + 8, :] = value
 
     relax(
-        side_tiles(fields, low, high, left, right),
+        side_tiles(fields, beside_x, sides),
         [inside, inside & ((lane < after) | (lane >= ahead))],
         heads, coef, conds, layers, False, final,
     )
@@ -399,6 +424,14 @@
 def shifted(value, axis, by):
     count = lax.axis_size(axis)
     return lax.ppermute(value, axis, [(i, (i + by) % count) for i in range(count)])
+
+
+def swapped(value, axis, first):
+    count = lax.axis_size(axis)
+    to = list(range(count))
+    for i in range(first, count, 2):
+        to[i], to[(i + 1) % count] = (i + 1) % count, i
+    return lax.ppermute(value, axis, list(enumerate(to)))
 
 
 def per_device(
@@ -434,14 +467,13 @@
         anywhere=True,
         mib=60,
     )(*fields, row_reach, river_section, bed_depth, route_inverse, retention, chain_heads)
-    low = shifted(last, "gx", 1)
-    high = shifted(first, "gx", -1)
+    pair_x = (shifted(last, "gx", 1), shifted(first, "gx", -1))
     info = lax.all_to_all(info, AXES, split_axis=0, concat_axis=0, tiled=True)
-    last, first = call(pack_y, (side, side), 6)(*fields, low, high)
-    left = shifted(last, "gy", 1)
-    right = shifted(first, "gy", -1)
+    for_even, for_odd = call(pack_y, (side, side), 6)(*fields, *pair_x)
+    pair_y = (swapped(for_odd, "gy", 1), swapped(for_even, "gy", 0))
     pads = tall + 2 * TOP
     held = SWEEPS + 1
+    sides = scratch(2, planes, tall, LANES)
     own = (
         scratch(2, 1, held, pads, LANES),
         scratch(7, 1, SWEEPS, tall, LANES),
@@ -454,10 +486,10 @@
         scratch=own,
         mib=16,
         micros=3,
-    )(*fields, low, high, cells, bed_conduct)
+    )(*fields, *pair_x, cells, bed_conduct)
     table = call(
-        functools.partial(edges, layers), f32(rows, width), 4, scratch=own, mib=16, micros=2
-    )(strips, left, right, top)
+        functools.partial(edges, layers), f32(rows, width), 4, scratch=(*own, sides), mib=16, micros=2
+    )(strips, *pair_y, top)
     sent = call(
         leak_rows,
         f32(row_total // 2, LANES),
@@ -479,10 +511,11 @@
             scratch(7, 2, layers, tall, LANES),
             scratch(2, layers, pads, LANES),
             scratch(reaches // LANES, row_total, LANES),
+            sides,
         ),
         mib=20,
         micros=5,
-    )(*fields, low, high, left, right, row_reach, route_inverse[0])
+    )(*fields, *pair_x, *pair_y, row_reach, route_inverse[0])
     reach_flow = call(finish_flow, f32(1, reaches), 2)(arrived, routed)
     return (head_field, reach_flow)
 

time: 47.1 us -> 46.5 us (0.987)
  waiting for transfers between devices: 8.41 us -> 7.35 us
  starting transfers between devices: 21.8 us -> 22.8 us
    ppermute x0 -> x2, starting transfers between devices: none -> 3.12 us  [swapped(): return lax.ppermute(value, axis, list(enumerate(to)))]
    ppermute x4 -> x2, starting transfers between devices: 8.58 us -> 6.93 us  [shifted(): lax.ppermute(value, axis, [(i, (i + by) % count) for i in range(count)])]
    ppermute x4 -> x2, waiting for transfers between devices: 1.62 us -> 0.01 us  [shifted(): lax.ppermute(value, axis, [(i, (i + by) % count) for i in range(count)])]
    all_to_all x1, starting transfers between devices: 6.59 us -> 6.1 us  [per_device(): lax.all_to_all(sent, AXES, split_axis=0, concat_axis=0, tiled=True)]
  transfers between devices with their start and end apart: 6 -> 6, of which waited for: 3 -> 2; matrix products, arithmetic and copies ran while one was open for 0% -> 0% of each run, Pallas kernels for 19% -> 18%
where the time goes in v5:
time: 46.5 us; the launch traced here: 46.3 us
  starting transfers between devices  22.8 us (49%)
  Pallas kernels  13.4 us (29%)
  waiting for transfers between devices  7.35 us (16%)
  between operations  2.09 us (4%)
  local copies, waits for them, and re-layouts  0.7 us (2%)
    ppermute x2, starting transfers between devices, shifted(): lax.ppermute(value, axis, [(i, (i + by) % count) for i in range(count)])  6.93 us
    all_to_all x1, starting transfers between devices, per_device(): info = lax.all_to_all(info, AXES, split_axis=0, concat_axis=0, tiled=True)  6.66 us
    all_to_all x1, starting transfers between devices, per_device(): lax.all_to_all(sent, AXES, split_axis=0, concat_axis=0, tiled=True)  6.1 us
    all_to_all x1, waiting for transfers between devices, per_device(): lax.all_to_all(sent, AXES, split_axis=0, concat_axis=0, tiled=True)  4.75 us
    pallas_call x1, Pallas kernels, per_device(): call(everywhere, (f32(layers, rows, width), f32(row_total, reaches)), 10,...  4.18 us
    ppermute x2, starting transfers between devices, swapped(): return lax.ppermute(value, axis, list(enumerate(to)))  3.12 us
    all_to_all x1, waiting for transfers between devices, per_device(): info = lax.all_to_all(info, AXES, split_axis=0, concat_axis=0, tiled=True)  2.6 us
    pallas_call x1, Pallas kernels, per_device(): call(inner, (f32(row_total, LANES), f32(rows, width), f32(4, held, tall,...  2.52 us
  transfers between devices with their start and end apart: 6, of which 2 were waited for; matrix products, arithmetic and copies ran while one was open for 0% of the time, Pallas kernels for 18%

profile of v5, /device:TPU:1, one launch (start us, length us, event | category | flops | bytes accessed | tf_op | source)
XLA Modules:
  0.0 46.3 jit_solution(7819481096715142869)
XLA Ops:
  1.9 0.0 copy-start.1
  1.9 0.0 copy-start.2
  1.9 0.0 copy-start.3
  2.0 1.9 %shard_map.131 = (f32[4,10,8,128]{3,2,1,0:T(8,128)}, f32[4,10,8,128]{3,2,1,0:T(8,128)}, f32[256,128]{1,0:T(8,128)}) custom-call(f32[10,32,128]{2,1,0:T(8,128)} %head.7, f32[10,32,128]{2,1,0:T(8,128)} %cond.7, f32[10,32,128]{2,1,0:T(8,128)} %source.7, f32[10,32,128]{2,1,0:T(8,128)} %storage.7, s32[1,256]{1,0:T(1,128)} %reach.3, f32[1,256]{1,0:T(1,128)} %section.1, ...), custom_call_target="tpu_custom_call" | custom-call | bytes 3000000 | tf_op jit(solution)/shard_map/pallas_call | solution.py:454
  3.9 0.0 copy-start
  3.9 2.1 %collective-permute-start = (f32[4,10,8,128]{3,2,1,0:T(8,128)}, f32[4,10,8,128]{3,2,1,0:T(8,128)S(1)}, u32[]{:S(2)}, u32[]{:S(2)}) collective-permute-start(f32[4,10,8,128]{3,2,1,0:T(8,128)} %get-tuple-element.12), channel_id=1, source_target_pairs={{0,8},{8,16},{16,24},{24,32},{32,40},{40,48},{48,56},{56,64},{64,7... | collective-permute-start | bytes 491528 | tf_op jit(solution)/shard_map/ppermute | solution.py:426
  6.0 4.8 %collective-permute-start.1 = (f32[4,10,8,128]{3,2,1,0:T(8,128)}, f32[4,10,8,128]{3,2,1,0:T(8,128)S(1)}, u32[]{:S(2)}, u32[]{:S(2)}) collective-permute-start(f32[4,10,8,128]{3,2,1,0:T(8,128)} %get-tuple-element.13), channel_id=1, source_target_pairs={{0,120},{8,0},{16,8},{24,16},{32,24},{40,32},{48,40},{56,48},{64,5... | collective-permute-start | bytes 491528 | tf_op jit(solution)/shard_map/ppermute | solution.py:426
  10.8 6.7 %all-to-all-start = ((f32[128,2,128]{2,1,0:T(2,128)}), f32[128,2,128]{2,1,0:T(2,128)S(1)}, u32[]{:S(2)}, u32[]{:S(2)}) async-start(f32[128,2,128]{2,1,0:T(2,128)} %bitcast.13), calls=%async_computation | async-start | bytes 262144 | tf_op jit(solution)/shard_map/all_to_all | solution.py:471
  17.5 0.0 copy-start.5
  17.5 0.0 collective-permute-done.low
  17.5 0.0 collective-permute-done.1.high
  17.5 0.0 copy-done.1
  17.5 0.0 copy-done.2
  17.6 0.0 copy-done.3
  17.6 0.0 copy-done
  17.6 0.0 copy-start.6
  17.6 0.3 shard_map.132
  17.9 1.7 %collective-permute-start.2 = (f32[3,48,128]{2,1,0:T(8,128)S(1)}, f32[3,48,128]{2,1,0:T(8,128)S(1)}, u32[]{:S(2)}, u32[]{:S(2)}) collective-permute-start(f32[3,48,128]{2,1,0:T(8,128)S(1)} %get-tuple-element.14), channel_id=1, source_target_pairs={{0,7},{1,2},{2,1},{3,4},{4,3},{5,6},{6,5},{7,0},{8,15},{9,10},{10,... | collective-permute-start | bytes 221192 | tf_op jit(solution)/shard_map/ppermute | solution.py:434
  19.6 1.4 %collective-permute-start.3 = (f32[3,48,128]{2,1,0:T(8,128)S(1)}, f32[3,48,128]{2,1,0:T(8,128)S(1)}, u32[]{:S(2)}, u32[]{:S(2)}) collective-permute-start(f32[3,48,128]{2,1,0:T(8,128)S(1)} %get-tuple-element.15), channel_id=1, source_target_pairs={{0,1},{1,0},{2,3},{3,2},{4,5},{5,4},{6,7},{7,6},{8,9},{9,8},{10,11... | collective-permute-start | bytes 221192 | tf_op jit(solution)/shard_map/ppermute | solution.py:434
  21.0 0.0 copy-done.5
  21.0 2.5 %shard_map.134 = (f32[256,128]{1,0:T(8,128)S(1)}, f32[32,128]{1,0:T(8,128)S(1)}, f32[4,9,48,128]{3,2,1,0:T(8,128)S(1)}) custom-call(f32[10,32,128]{2,1,0:T(8,128)S(1)} %copy-done, f32[10,32,128]{2,1,0:T(8,128)S(1)} %copy-done.1, f32[10,32,128]{2,1,0:T(8,128)S(1)} %copy-done.2, f32[10,32,128]{2,1,0:T(8,128)S(1)} %copy-done.3, ...), custom_call_target="tpu_custom_call" | custom-call | bytes 9000000 | tf_op jit(solution)/shard_map/pallas_call | solution.py:482
  23.6 0.0 collective-permute-done.2.other_y
  23.6 0.0 collective-permute-done.3.one_y
  23.6 1.4 %shard_map.135.table = f32[32,128]{1,0:T(8,128)S(1)} custom-call(f32[4,9,48,128]{3,2,1,0:T(8,128)S(1)} %get-tuple-element.17.strips, f32[3,48,128]{2,1,0:T(8,128)S(1)} %collective-permute-done.2.other_y, f32[3,48,128]{2,1,0:T(8,128)S(1)} %collective-permute-done.3.one_y, f32[32,128]{1,0:T(8,128)S(1)} %get-tuple-element.18.top), custom_call_target="tpu_custom_call" | custom-call | bytes 6000000 | tf_op jit(solution)/shard_map/pallas_call | solution.py:490
  24.9 2.6 %all-to-all-done = f32[128,2,128]{2,1,0:T(2,128)S(1)} async-done(((f32[128,2,128]{2,1,0:T(2,128)}), f32[128,2,128]{2,1,0:T(2,128)S(1)}, u32[]{:S(2)}, u32[]{:S(2)}) %all-to-all-start) | async-done | bytes 131104 | tf_op jit(solution)/shard_map/all_to_all | solution.py:471
  27.5 2.4 %shard_map.136 = f32[128,128]{1,0:T(8,128)} custom-call(f32[32,128]{1,0:T(8,128)S(1)} %shard_map.135.table, s32[256,128]{1,0:T(8,128)S(1)} %bitcast.10, f32[256,128]{1,0:T(8,128)S(1)} %get-tuple-element.19.beds, f32[256,128]{1,0:T(8,128)S(1)} %bitcast.11), custom_call_target="tpu_custom_call" | custom-call | bytes 9000000 | tf_op jit(solution)/shard_map/pallas_call | solution.py:493
  29.9 6.1 %all-to-all-start.1 = ((f32[128,1,128]{2,1,0:T(1,128)}), f32[128,1,128]{2,1,0:T(1,128)S(1)}, u32[]{:S(2)}, u32[]{:S(2)}) async-start(f32[128,1,128]{2,1,0:T(1,128)} %bitcast.5), calls=%async_computation.1 | async-start | bytes 131072 | tf_op jit(solution)/shard_map/all_to_all | solution.py:504
  36.0 0.0 copy-start.7
  36.0 0.7 %copy-done.7 = s32[1,256]{1,0:T(1,128)S(1)} copy-done((s32[1,256]{1,0:T(1,128)S(1)}, s32[1,256]{1,0:T(1,128)}, u32[]{:S(2)}) %copy-start.7) | copy-done | bytes 1048
  36.7 4.2 %shard_map.133 = (f32[10,32,128]{2,1,0:T(8,128)}, f32[256,256]{1,0:T(8,128)S(1)}) custom-call(f32[10,32,128]{2,1,0:T(8,128)S(1)} %copy-done, f32[10,32,128]{2,1,0:T(8,128)S(1)} %copy-done.1, f32[10,32,128]{2,1,0:T(8,128)S(1)} %copy-done.2, f32[10,32,128]{2,1,0:T(8,128)S(1)} %copy-done.3, f32[4,10,8,128]{3,2,1,0:T(8,128)S(1)} %collective-permute-done.low, ...), custom_call_target="tpu_custom_call" | custom-call | bytes 15000000 | tf_op jit(solution)/shard_map/pallas_call | solution.py:505
  40.9 4.7 %all-to-all-done.1 = f32[128,1,128]{2,1,0:T(1,128)S(1)} async-done(((f32[128,1,128]{2,1,0:T(1,128)}), f32[128,1,128]{2,1,0:T(1,128)S(1)}, u32[]{:S(2)}, u32[]{:S(2)}) %all-to-all-start.1) | async-done | bytes 65568 | tf_op jit(solution)/shard_map/all_to_all | solution.py:504
  45.6 0.7 %shard_map.137 = f32[1,256]{1,0:T(1,128)} custom-call(f32[128,128]{1,0:T(8,128)S(1)} %bitcast.12, f32[256,256]{1,0:T(8,128)S(1)} %get-tuple-element.21.routed), custom_call_target="tpu_custom_call" | custom-call | bytes 3000000 | tf_op jit(solution)/shard_map/pallas_call | solution.py:519
  (3 shorter events, 0.0 us)
Async XLA Ops:
  1.9 15.6 %copy-start.1 = (f32[10,32,128]{2,1,0:T(8,128)S(1)}, f32[10,32,128]{2,1,0:T(8,128)}, u32[]{:S(2)}) copy-start(f32[10,32,128]{2,1,0:T(8,128)} %cond.7) | copy-start | bytes 491524
  1.9 15.6 %copy-start.2 = (f32[10,32,128]{2,1,0:T(8,128)S(1)}, f32[10,32,128]{2,1,0:T(8,128)}, u32[]{:S(2)}) copy-start(f32[10,32,128]{2,1,0:T(8,128)} %source.7) | copy-start | bytes 491524
  1.9 15.6 %copy-start.3 = (f32[10,32,128]{2,1,0:T(8,128)S(1)}, f32[10,32,128]{2,1,0:T(8,128)}, u32[]{:S(2)}) copy-start(f32[10,32,128]{2,1,0:T(8,128)} %storage.7) | copy-start | bytes 491524
  3.9 13.7 %copy-start = (f32[10,32,128]{2,1,0:T(8,128)S(1)}, f32[10,32,128]{2,1,0:T(8,128)}, u32[]{:S(2)}) copy-start(f32[10,32,128]{2,1,0:T(8,128)} %head.7) | copy-start | bytes 491524
  3.9 13.6 %collective-permute-start = (f32[4,10,8,128]{3,2,1,0:T(8,128)}, f32[4,10,8,128]{3,2,1,0:T(8,128)S(1)}, u32[]{:S(2)}, u32[]{:S(2)}) collective-permute-start(f32[4,10,8,128]{3,2,1,0:T(8,128)} %get-tuple-element.12), channel_id=1, source_target_pairs={{0,8},{8,16},{16,24},{24,32},{32,40},{40,48},{48,56},{56,64},{64,7... | collective-permute-start | bytes 491528 | tf_op jit(solution)/shard_map/ppermute | solution.py:426
  6.0 11.5 %collective-permute-start.1 = (f32[4,10,8,128]{3,2,1,0:T(8,128)}, f32[4,10,8,128]{3,2,1,0:T(8,128)S(1)}, u32[]{:S(2)}, u32[]{:S(2)}) collective-permute-start(f32[4,10,8,128]{3,2,1,0:T(8,128)} %get-tuple-element.13), channel_id=1, source_target_pairs={{0,120},{8,0},{16,8},{24,16},{32,24},{40,32},{48,40},{56,48},{64,5... | collective-permute-start | bytes 491528 | tf_op jit(solution)/shard_map/ppermute | solution.py:426
  10.8 16.7 %all-to-all-start = ((f32[128,2,128]{2,1,0:T(2,128)}), f32[128,2,128]{2,1,0:T(2,128)S(1)}, u32[]{:S(2)}, u32[]{:S(2)}) async-start(f32[128,2,128]{2,1,0:T(2,128)} %bitcast.13), calls=%async_computation | async-start | bytes 262144 | tf_op jit(solution)/shard_map/all_to_all | solution.py:471
  17.5 3.5 %copy-start.5 = (s32[1,256,128]{2,1,0:T(8,128)S(1)}, s32[1,256,128]{2,1,0:T(8,128)}, u32[]{:S(2)}) copy-start(s32[1,256,128]{2,1,0:T(8,128)} %param.17) | copy-start | bytes 393220
  17.6 3.4 %copy-start.6 = (f32[32,128]{1,0:T(8,128)S(1)}, f32[32,128]{1,0:T(8,128)}, u32[]{:S(2)}) copy-start(f32[32,128]{1,0:T(8,128)} %bed.1) | copy-start | bytes 49156
  17.9 5.7 %collective-permute-start.2 = (f32[3,48,128]{2,1,0:T(8,128)S(1)}, f32[3,48,128]{2,1,0:T(8,128)S(1)}, u32[]{:S(2)}, u32[]{:S(2)}) collective-permute-start(f32[3,48,128]{2,1,0:T(8,128)S(1)} %get-tuple-element.14), channel_id=1, source_target_pairs={{0,7},{1,2},{2,1},{3,4},{4,3},{5,6},{6,5},{7,0},{8,15},{9,10},{10,... | collective-permute-start | bytes 221192 | tf_op jit(solution)/shard_map/ppermute | solution.py:434
  19.6 4.0 %collective-permute-start.3 = (f32[3,48,128]{2,1,0:T(8,128)S(1)}, f32[3,48,128]{2,1,0:T(8,128)S(1)}, u32[]{:S(2)}, u32[]{:S(2)}) collective-permute-start(f32[3,48,128]{2,1,0:T(8,128)S(1)} %get-tuple-element.15), channel_id=1, source_target_pairs={{0,1},{1,0},{2,3},{3,2},{4,5},{5,4},{6,7},{7,6},{8,9},{9,8},{10,11... | collective-permute-start | bytes 221192 | tf_op jit(solution)/shard_map/ppermute | solution.py:434
  27.5 8.5 %copy-start.4 = (f32[1,256,256]{2,1,0:T(8,128)S(1)}, f32[1,256,256]{2,1,0:T(8,128)}, u32[]{:S(2)}) copy-start(f32[1,256,256]{2,1,0:T(8,128)} %route.1) | copy-start | bytes 786436
  29.9 15.7 %all-to-all-start.1 = ((f32[128,1,128]{2,1,0:T(1,128)}), f32[128,1,128]{2,1,0:T(1,128)S(1)}, u32[]{:S(2)}, u32[]{:S(2)}) async-start(f32[128,1,128]{2,1,0:T(1,128)} %bitcast.5), calls=%async_computation.1 | async-start | bytes 131072 | tf_op jit(solution)/shard_map/all_to_all | solution.py:504
  36.0 0.7 %copy-start.7 = (s32[1,256]{1,0:T(1,128)S(1)}, s32[1,256]{1,0:T(1,128)}, u32[]{:S(2)}) copy-start(s32[1,256]{1,0:T(1,128)} %reach.3) | copy-start | bytes 3076

commit v6 on v5

--- a/solution.py
+++ b/solution.py
@@ -108,17 +108,17 @@
         odd_out[plane] = jnp.where(even_y, first_sum[plane], last_sum[plane])
 
 
-def select_cells(cells_ref, table, finish):
-    half = cells_ref.shape[0] // 16
-    for b in range(2 * half):
-        c, g = divmod(b, half)
-        cells = cells_ref[pl.ds(g * 16 + c, 8, stride=2), :]
-        column, line = cells & (LANES - 1), cells // LANES
-        found = jnp.zeros((8, LANES), jnp.float32)
-        for r, spread in enumerate(table):
-            value = jnp.take_along_axis(spread, column, axis=1, mode="promise_in_bounds")
-            found = jnp.where(line == r, value, found)
-        finish(slice(b * 8, (b + 1) * 8), found)
+def cell_block(cells_ref, b):
+    c, g = divmod(b, cells_ref.shape[0] // 16)
+    cells = cells_ref[pl.ds(g * 16 + c, 8, stride=2), :]
+    return cells & (LANES - 1), cells // LANES
+
+
+def select(found, column, line, table):
+    for r, spread in enumerate(table):
+        value = jnp.take_along_axis(spread, column, axis=1, mode="promise_in_bounds")
+        found = jnp.where(line == r, value, found)
+    return found
 
 
 def spread_rows(table):
@@ -263,7 +263,7 @@
 
 def inner(
     head, cond, source, storage, low, high, cells, bed,
-    beds_out, top_out, strips_out, heads, coef, conds,
+    beds_out, found_out, strips_out, heads, coef, conds, top,
 ):
     fields = (head, cond, source, storage)
     beside_x = (low, high)
@@ -276,24 +276,26 @@
             strip = jnp.where(lane < 2 * HALO, turned(whole, 2 * HALO), turned(whole, 4 * HALO))
             strips_out[k, l] = jnp.where(lane < 6 * HALO, strip, 0.0)
 
-    def keep(span, value):
-        beds_out[span, :] = value
-
-    select_cells(cells, spread_rows(bed[...]), keep)
-
     def final(l, start, value):
-        top_out[start : start + 8, :] = value
+        top[start : start + 8, :] = value
 
     inside = inside_rows(lax.broadcasted_iota(jnp.int32, (tall, LANES), 0))
     relax(
         lambda k, l: [tall_row(fields, beside_x, k, l)], [inside],
         heads, coef, conds, layers, True, final,
     )
-
-
-def edges(layers, strips, other_y, one_y, top, table, heads, coef, conds, sides):
+    bed_table, head_table = spread_rows(bed[...]), spread_rows(top[...])
+    for b in range(cells.shape[0] // 8):
+        column, line = cell_block(cells, b)
+        span = slice(b * 8, (b + 1) * 8)
+        nothing = jnp.zeros((8, LANES), jnp.float32)
+        beds_out[span, :] = select(nothing, column, line, bed_table)
+        found_out[span, :] = select(nothing, column, line, head_table)
+
+
+def edges(layers, strips, other_y, one_y, ends_out, heads, coef, conds, sides):
     settle(one_y, other_y, sides)
-    tall = top.shape[0] + 2 * HALO
+    tall = strips.shape[2]
     lane = lax.broadcasted_iota(jnp.int32, (tall, LANES), 1)
     at_y = lax.axis_index("gy")
     first = (at_y == 0) & (lane >= 3 * HALO) & (lane < 4 * HALO)
@@ -302,12 +304,14 @@
     mask = inside & ~first & ~last & (lane < 6 * HALO)
 
     def final(l, start, value):
-        span = slice(start, start + 8)
         column = lax.broadcasted_iota(jnp.int32, value.shape, 1)
-        ends = jnp.where(column < HALO, turned(value, -4 * HALO), turned(value, -2 * HALO))
-        table[span, :] = jnp.where(
-            (column < HALO) | (column >= LANES - HALO), ends, top[span, :]
-        )
+        row = lax.broadcasted_iota(jnp.int32, value.shape, 0)
+        ends = jnp.where(column < HALO, turned(value, -4 * HALO), value)
+        ends = jnp.where(column < 2 * HALO, ends, 0.0)
+        line = jnp.zeros_like(value)
+        for r in range(8):
+            line = line + jnp.where(row == r, turned(ends, r * 2 * HALO), 0.0)
+        ends_out[start // 8 : start // 8 + 1, :] = jnp.sum(line, 0, keepdims=True)
 
     relax(
         strip_tiles(strips, sides, layers), [mask],
@@ -315,7 +319,7 @@
     )
 
 
-def leak_rows(table, cells, beds, info, send_out, weights, levels, leaks):
+def leak_rows(found, ends, cells, beds, info, send_out, weights, levels, leaks):
     peers = info.shape[0] // 2
     groups = peers // 8
     for c in range(2):
@@ -348,12 +352,18 @@
         for c in range(2):
             weights[c, g * 8 : (g + 1) * 8, :] = product * details[c][g * 8 : (g + 1) * 8, 2:3]
 
-    def leak(span, value):
+    table = spread_rows(ends[...])
+    for b in range(2 * groups):
+        column, line = cell_block(cells, b)
+        span = slice(b * 8, (b + 1) * 8)
+        near = (column < HALO) | (column >= LANES - HALO)
+        at = line * (2 * HALO) + jnp.where(column < HALO, column, column - (LANES - 2 * HALO))
+        value = select(
+            found[span, :], at & (LANES - 1), jnp.where(near, at // LANES, -1), table
+        )
         leaks[span, :] = beds[span, :] * (
             jnp.maximum(value, levels[1, span, :]) - levels[0, span, :]
         )
-
-    select_cells(cells, spread_rows(table[...]), leak)
     eight = lax.broadcasted_iota(jnp.int32, (8, LANES), 1)
     flow = jnp.zeros((8, LANES), jnp.float32)
     sums = []
@@ -479,28 +489,33 @@
         scratch(7, 1, SWEEPS, tall, LANES),
         scratch(1, held, pads, LANES),
     )
-    beds, top, strips = call(
+    beds, found, strips = call(
         inner,
-        (f32(row_total, LANES), f32(rows, width), f32(4, held, tall, LANES)),
+        (f32(row_total, LANES), f32(row_total, LANES), f32(4, held, tall, LANES)),
         8,
-        scratch=own,
+        scratch=(*own, scratch(rows, LANES)),
         mib=16,
         micros=3,
     )(*fields, *pair_x, cells, bed_conduct)
-    table = call(
-        functools.partial(edges, layers), f32(rows, width), 4, scratch=(*own, sides), mib=16, micros=2
-    )(strips, *pair_y, top)
+    ends = call(
+        functools.partial(edges, layers),
+        f32(rows // 8, LANES),
+        3,
+        scratch=(*own, sides),
+        mib=16,
+        micros=2,
+    )(strips, *pair_y)
     sent = call(
         leak_rows,
         f32(row_total // 2, LANES),
-        4,
+        5,
         scratch=(
             scratch(2, row_total // 2, LANES),
             scratch(2, row_total, LANES),
             scratch(row_total, LANES),
         ),
         micros=3,
-    )(table, cells, beds, info)
+    )(found, ends, cells, beds, info)
     arrived = lax.all_to_all(sent, AXES, split_axis=0, concat_axis=0, tiled=True)
     head_field, routed = call(
         everywhere,

time: 46.5 us -> 46.2 us (level)
  waiting for transfers between devices: 7.35 us -> 6.14 us
  starting transfers between devices: 22.8 us -> 23.4 us
    all_to_all x1, waiting for transfers between devices: 2.6 us -> 1.39 us  [per_device(): info = lax.all_to_all(info, AXES, split_axis=0, concat_axis=0, tiled=True)]
    all_to_all x1, starting transfers between devices: 6.1 us -> 6.7 us  [per_device(): lax.all_to_all(sent, AXES, split_axis=0, concat_axis=0, tiled=True)]
  transfers between devices with their start and end apart: 6 -> 6, of which waited for: 2 -> 2; matrix products, arithmetic and copies ran while one was open for 0% -> 0% of each run, Pallas kernels for 18% -> 21%
where the time goes in v6:
time: 46.2 us; the launch traced here: 46 us
  starting transfers between devices  23.4 us (51%)
  Pallas kernels  13.7 us (30%)
  waiting for transfers between devices  6.14 us (13%)
  between operations  2.1 us (5%)
  local copies, waits for them, and re-layouts  0.7 us (2%)
    ppermute x2, starting transfers between devices, shifted(): lax.ppermute(value, axis, [(i, (i + by) % count) for i in range(count)])  6.93 us
    all_to_all x1, starting transfers between devices, per_device(): lax.all_to_all(sent, AXES, split_axis=0, concat_axis=0, tiled=True)  6.7 us
    all_to_all x1, starting transfers between devices, per_device(): info = lax.all_to_all(info, AXES, split_axis=0, concat_axis=0, tiled=True)  6.66 us
    all_to_all x1, waiting for transfers between devices, per_device(): lax.all_to_all(sent, AXES, split_axis=0, concat_axis=0, tiled=True)  4.74 us
    pallas_call x1, Pallas kernels, per_device(): call(everywhere, (f32(layers, rows, width), f32(row_total, reaches)), 10,...  4.18 us
    pallas_call x1, Pallas kernels, per_device(): call(inner, (f32(row_total, LANES), f32(row_total, LANES), f32(4, held, t...  3.65 us
    ppermute x2, starting transfers between devices, swapped(): return lax.ppermute(value, axis, list(enumerate(to)))  3.12 us
    pallas_call x1, Pallas kernels, per_device(): call(front, (edge, edge, f32(row_total, LANES)), 10, scratch=(pltpu.VMEM(...  1.93 us
  transfers between devices with their start and end apart: 6, of which 2 were waited for; matrix products, arithmetic and copies ran while one was open for 0% of the time, Pallas kernels for 21%

profile of v6, /device:TPU:1, one launch (start us, length us, event | category | flops | bytes accessed | tf_op | source)
XLA Modules:
  0.0 46.0 jit_solution(15548497421498964711)
XLA Ops:
  1.9 0.0 copy-start.1
  1.9 0.0 copy-start.2
  1.9 0.0 copy-start.3
  2.0 1.9 %shard_map.131 = (f32[4,10,8,128]{3,2,1,0:T(8,128)}, f32[4,10,8,128]{3,2,1,0:T(8,128)}, f32[256,128]{1,0:T(8,128)}) custom-call(f32[10,32,128]{2,1,0:T(8,128)} %head.7, f32[10,32,128]{2,1,0:T(8,128)} %cond.7, f32[10,32,128]{2,1,0:T(8,128)} %source.7, f32[10,32,128]{2,1,0:T(8,128)} %storage.7, s32[1,256]{1,0:T(1,128)} %reach.3, f32[1,256]{1,0:T(1,128)} %section.1, ...), custom_call_target="tpu_custom_call" | custom-call | bytes 3000000 | tf_op jit(solution)/shard_map/pallas_call | solution.py:464
  3.9 0.0 copy-start
  3.9 2.1 %collective-permute-start = (f32[4,10,8,128]{3,2,1,0:T(8,128)}, f32[4,10,8,128]{3,2,1,0:T(8,128)S(1)}, u32[]{:S(2)}, u32[]{:S(2)}) collective-permute-start(f32[4,10,8,128]{3,2,1,0:T(8,128)} %get-tuple-element.12), channel_id=1, source_target_pairs={{0,8},{8,16},{16,24},{24,32},{32,40},{40,48},{48,56},{56,64},{64,7... | collective-permute-start | bytes 491528 | tf_op jit(solution)/shard_map/ppermute | solution.py:436
  6.0 4.8 %collective-permute-start.1 = (f32[4,10,8,128]{3,2,1,0:T(8,128)}, f32[4,10,8,128]{3,2,1,0:T(8,128)S(1)}, u32[]{:S(2)}, u32[]{:S(2)}) collective-permute-start(f32[4,10,8,128]{3,2,1,0:T(8,128)} %get-tuple-element.13), channel_id=1, source_target_pairs={{0,120},{8,0},{16,8},{24,16},{32,24},{40,32},{48,40},{56,48},{64,5... | collective-permute-start | bytes 491528 | tf_op jit(solution)/shard_map/ppermute | solution.py:436
  10.8 6.7 %all-to-all-start = ((f32[128,2,128]{2,1,0:T(2,128)}), f32[128,2,128]{2,1,0:T(2,128)S(1)}, u32[]{:S(2)}, u32[]{:S(2)}) async-start(f32[128,2,128]{2,1,0:T(2,128)} %bitcast.13), calls=%async_computation | async-start | bytes 262144 | tf_op jit(solution)/shard_map/all_to_all | solution.py:481
  17.5 0.0 copy-start.5
  17.5 0.0 collective-permute-done.low
  17.5 0.0 collective-permute-done.1.high
  17.5 0.0 copy-done.1
  17.5 0.0 copy-done.2
  17.6 0.0 copy-done.3
  17.6 0.0 copy-done
  17.6 0.0 copy-start.6
  17.6 0.3 shard_map.132
  17.9 1.7 %collective-permute-start.2 = (f32[3,48,128]{2,1,0:T(8,128)S(1)}, f32[3,48,128]{2,1,0:T(8,128)S(1)}, u32[]{:S(2)}, u32[]{:S(2)}) collective-permute-start(f32[3,48,128]{2,1,0:T(8,128)S(1)} %get-tuple-element.14), channel_id=1, source_target_pairs={{0,7},{1,2},{2,1},{3,4},{4,3},{5,6},{6,5},{7,0},{8,15},{9,10},{10,... | collective-permute-start | bytes 221192 | tf_op jit(solution)/shard_map/ppermute | solution.py:444
  19.6 1.4 %collective-permute-start.3 = (f32[3,48,128]{2,1,0:T(8,128)S(1)}, f32[3,48,128]{2,1,0:T(8,128)S(1)}, u32[]{:S(2)}, u32[]{:S(2)}) collective-permute-start(f32[3,48,128]{2,1,0:T(8,128)S(1)} %get-tuple-element.15), channel_id=1, source_target_pairs={{0,1},{1,0},{2,3},{3,2},{4,5},{5,4},{6,7},{7,6},{8,9},{9,8},{10,11... | collective-permute-start | bytes 221192 | tf_op jit(solution)/shard_map/ppermute | solution.py:444
  21.0 0.0 copy-done.5
  21.0 3.6 %shard_map.134 = (f32[256,128]{1,0:T(8,128)S(1)}, f32[256,128]{1,0:T(8,128)S(1)}, f32[4,9,48,128]{3,2,1,0:T(8,128)S(1)}) custom-call(f32[10,32,128]{2,1,0:T(8,128)S(1)} %copy-done, f32[10,32,128]{2,1,0:T(8,128)S(1)} %copy-done.1, f32[10,32,128]{2,1,0:T(8,128)S(1)} %copy-done.2, f32[10,32,128]{2,1,0:T(8,128)S(1)} %copy-done.3, ...), custom_call_target="tpu_custom_call" | custom-call | bytes 9000000 | tf_op jit(solution)/shard_map/pallas_call | solution.py:492
  24.7 0.0 collective-permute-done.2.other_y
  24.7 0.0 collective-permute-done.3.one_y
  24.7 1.4 %shard_map.135.ends = f32[4,128]{1,0:T(4,128)S(1)} custom-call(f32[4,9,48,128]{3,2,1,0:T(8,128)S(1)} %get-tuple-element.18.strips, f32[3,48,128]{2,1,0:T(8,128)S(1)} %collective-permute-done.2.other_y, f32[3,48,128]{2,1,0:T(8,128)S(1)} %collective-permute-done.3.one_y), custom_call_target="tpu_custom_call" | custom-call | bytes 6000000 | tf_op jit(solution)/shard_map/pallas_call | solution.py:500
  26.1 1.4 %all-to-all-done = f32[128,2,128]{2,1,0:T(2,128)S(1)} async-done(((f32[128,2,128]{2,1,0:T(2,128)}), f32[128,2,128]{2,1,0:T(2,128)S(1)}, u32[]{:S(2)}, u32[]{:S(2)}) %all-to-all-start) | async-done | bytes 131104 | tf_op jit(solution)/shard_map/all_to_all | solution.py:481
  27.5 1.5 %shard_map.136 = f32[128,128]{1,0:T(8,128)} custom-call(f32[256,128]{1,0:T(8,128)S(1)} %get-tuple-element.17.found, f32[4,128]{1,0:T(4,128)S(1)} %shard_map.135.ends, s32[256,128]{1,0:T(8,128)S(1)} %bitcast.10, f32[256,128]{1,0:T(8,128)S(1)} %get-tuple-element.19.beds, f32[256,128]{1,0:T(8,128)S(1)} %bitcast.11), custom_call_target="tpu_custom_call" | custom-call | bytes 9000000 | tf_op jit(solution)/shard_map/pallas_call | solution.py:508
  29.0 6.7 %all-to-all-start.1 = ((f32[128,1,128]{2,1,0:T(1,128)}), f32[128,1,128]{2,1,0:T(1,128)S(1)}, u32[]{:S(2)}, u32[]{:S(2)}) async-start(f32[128,1,128]{2,1,0:T(1,128)} %bitcast.5), calls=%async_computation.1 | async-start | bytes 131072 | tf_op jit(solution)/shard_map/all_to_all | solution.py:519
  35.7 0.0 copy-start.7
  35.7 0.7 %copy-done.7 = s32[1,256]{1,0:T(1,128)S(1)} copy-done((s32[1,256]{1,0:T(1,128)S(1)}, s32[1,256]{1,0:T(1,128)}, u32[]{:S(2)}) %copy-start.7) | copy-done | bytes 1048
  36.4 4.2 %shard_map.133 = (f32[10,32,128]{2,1,0:T(8,128)}, f32[256,256]{1,0:T(8,128)S(1)}) custom-call(f32[10,32,128]{2,1,0:T(8,128)S(1)} %copy-done, f32[10,32,128]{2,1,0:T(8,128)S(1)} %copy-done.1, f32[10,32,128]{2,1,0:T(8,128)S(1)} %copy-done.2, f32[10,32,128]{2,1,0:T(8,128)S(1)} %copy-done.3, f32[4,10,8,128]{3,2,1,0:T(8,128)S(1)} %collective-permute-done.low, ...), custom_call_target="tpu_custom_call" | custom-call | bytes 15000000 | tf_op jit(solution)/shard_map/pallas_call | solution.py:520
  40.6 4.7 %all-to-all-done.1 = f32[128,1,128]{2,1,0:T(1,128)S(1)} async-done(((f32[128,1,128]{2,1,0:T(1,128)}), f32[128,1,128]{2,1,0:T(1,128)S(1)}, u32[]{:S(2)}, u32[]{:S(2)}) %all-to-all-start.1) | async-done | bytes 65568 | tf_op jit(solution)/shard_map/all_to_all | solution.py:519
  45.3 0.7 %shard_map.137 = f32[1,256]{1,0:T(1,128)} custom-call(f32[128,128]{1,0:T(8,128)S(1)} %bitcast.12, f32[256,256]{1,0:T(8,128)S(1)} %get-tuple-element.21.routed), custom_call_target="tpu_custom_call" | custom-call | bytes 3000000 | tf_op jit(solution)/shard_map/pallas_call | solution.py:534
  (3 shorter events, 0.0 us)
Async XLA Ops:
  1.9 15.6 %copy-start.1 = (f32[10,32,128]{2,1,0:T(8,128)S(1)}, f32[10,32,128]{2,1,0:T(8,128)}, u32[]{:S(2)}) copy-start(f32[10,32,128]{2,1,0:T(8,128)} %cond.7) | copy-start | bytes 491524
  1.9 15.6 %copy-start.2 = (f32[10,32,128]{2,1,0:T(8,128)S(1)}, f32[10,32,128]{2,1,0:T(8,128)}, u32[]{:S(2)}) copy-start(f32[10,32,128]{2,1,0:T(8,128)} %source.7) | copy-start | bytes 491524
  1.9 15.6 %copy-start.3 = (f32[10,32,128]{2,1,0:T(8,128)S(1)}, f32[10,32,128]{2,1,0:T(8,128)}, u32[]{:S(2)}) copy-start(f32[10,32,128]{2,1,0:T(8,128)} %storage.7) | copy-start | bytes 491524
  3.9 13.7 %copy-start = (f32[10,32,128]{2,1,0:T(8,128)S(1)}, f32[10,32,128]{2,1,0:T(8,128)}, u32[]{:S(2)}) copy-start(f32[10,32,128]{2,1,0:T(8,128)} %head.7) | copy-start | bytes 491524
  3.9 13.6 %collective-permute-start = (f32[4,10,8,128]{3,2,1,0:T(8,128)}, f32[4,10,8,128]{3,2,1,0:T(8,128)S(1)}, u32[]{:S(2)}, u32[]{:S(2)}) collective-permute-start(f32[4,10,8,128]{3,2,1,0:T(8,128)} %get-tuple-element.12), channel_id=1, source_target_pairs={{0,8},{8,16},{16,24},{24,32},{32,40},{40,48},{48,56},{56,64},{64,7... | collective-permute-start | bytes 491528 | tf_op jit(solution)/shard_map/ppermute | solution.py:436
  6.0 11.5 %collective-permute-start.1 = (f32[4,10,8,128]{3,2,1,0:T(8,128)}, f32[4,10,8,128]{3,2,1,0:T(8,128)S(1)}, u32[]{:S(2)}, u32[]{:S(2)}) collective-permute-start(f32[4,10,8,128]{3,2,1,0:T(8,128)} %get-tuple-element.13), channel_id=1, source_target_pairs={{0,120},{8,0},{16,8},{24,16},{32,24},{40,32},{48,40},{56,48},{64,5... | collective-permute-start | bytes 491528 | tf_op jit(solution)/shard_map/ppermute | solution.py:436
  10.8 16.7 %all-to-all-start = ((f32[128,2,128]{2,1,0:T(2,128)}), f32[128,2,128]{2,1,0:T(2,128)S(1)}, u32[]{:S(2)}, u32[]{:S(2)}) async-start(f32[128,2,128]{2,1,0:T(2,128)} %bitcast.13), calls=%async_computation | async-start | bytes 262144 | tf_op jit(solution)/shard_map/all_to_all | solution.py:481
  17.5 3.5 %copy-start.5 = (s32[1,256,128]{2,1,0:T(8,128)S(1)}, s32[1,256,128]{2,1,0:T(8,128)}, u32[]{:S(2)}) copy-start(s32[1,256,128]{2,1,0:T(8,128)} %param.17) | copy-start | bytes 393220
  17.6 3.4 %copy-start.6 = (f32[32,128]{1,0:T(8,128)S(1)}, f32[32,128]{1,0:T(8,128)}, u32[]{:S(2)}) copy-start(f32[32,128]{1,0:T(8,128)} %bed.1) | copy-start | bytes 49156
  17.9 6.8 %collective-permute-start.2 = (f32[3,48,128]{2,1,0:T(8,128)S(1)}, f32[3,48,128]{2,1,0:T(8,128)S(1)}, u32[]{:S(2)}, u32[]{:S(2)}) collective-permute-start(f32[3,48,128]{2,1,0:T(8,128)S(1)} %get-tuple-element.14), channel_id=1, source_target_pairs={{0,7},{1,2},{2,1},{3,4},{4,3},{5,6},{6,5},{7,0},{8,15},{9,10},{10,... | collective-permute-start | bytes 221192 | tf_op jit(solution)/shard_map/ppermute | solution.py:444
  19.6 5.1 %collective-permute-start.3 = (f32[3,48,128]{2,1,0:T(8,128)S(1)}, f32[3,48,128]{2,1,0:T(8,128)S(1)}, u32[]{:S(2)}, u32[]{:S(2)}) collective-permute-start(f32[3,48,128]{2,1,0:T(8,128)S(1)} %get-tuple-element.15), channel_id=1, source_target_pairs={{0,1},{1,0},{2,3},{3,2},{4,5},{5,4},{6,7},{7,6},{8,9},{9,8},{10,11... | collective-permute-start | bytes 221192 | tf_op jit(solution)/shard_map/ppermute | solution.py:444
  27.5 8.2 %copy-start.4 = (f32[1,256,256]{2,1,0:T(8,128)S(1)}, f32[1,256,256]{2,1,0:T(8,128)}, u32[]{:S(2)}) copy-start(f32[1,256,256]{2,1,0:T(8,128)} %route.1) | copy-start | bytes 786436
  29.0 16.3 %all-to-all-start.1 = ((f32[128,1,128]{2,1,0:T(1,128)}), f32[128,1,128]{2,1,0:T(1,128)S(1)}, u32[]{:S(2)}, u32[]{:S(2)}) async-start(f32[128,1,128]{2,1,0:T(1,128)} %bitcast.5), calls=%async_computation.1 | async-start | bytes 131072 | tf_op jit(solution)/shard_map/all_to_all | solution.py:519
  35.7 0.7 %copy-start.7 = (s32[1,256]{1,0:T(1,128)S(1)}, s32[1,256]{1,0:T(1,128)}, u32[]{:S(2)}) copy-start(s32[1,256]{1,0:T(1,128)} %reach.3) | copy-start | bytes 3076

commit v7 on v6

--- a/solution.py
+++ b/solution.py
@@ -243,7 +243,8 @@
                 [heads[old, t, l, span, :] for t in range(tiles)]
                 for l in range(min(many + 1, layers))
             ]
-            for l in range(many):
+            main_rows = BOTTOM <= start < rows - BOTTOM
+            for l in range(many if main_rows or not cone else many - 1):
                 east, west = beside(mids[l])
                 at = slice(start - TOP, start - TOP + 8)
                 for t in range(1 if last_sweep else tiles):
@@ -288,9 +289,13 @@
     for b in range(cells.shape[0] // 8):
         column, line = cell_block(cells, b)
         span = slice(b * 8, (b + 1) * 8)
-        nothing = jnp.zeros((8, LANES), jnp.float32)
-        beds_out[span, :] = select(nothing, column, line, bed_table)
-        found_out[span, :] = select(nothing, column, line, head_table)
+        picked = [jnp.zeros((8, LANES), jnp.float32)] * 2
+        for r in range(rows):
+            mine = line == r
+            for k, spread in enumerate((bed_table[r], head_table[r])):
+                value = jnp.take_along_axis(spread, column, axis=1, mode="promise_in_bounds")
+                picked[k] = jnp.where(mine, value, picked[k])
+        beds_out[span, :], found_out[span, :] = picked
 
 
 def edges(layers, strips, other_y, one_y, ends_out, heads, coef, conds, sides):

time: 46.2 us -> 46.2 us (level)
  no operation moved by 1% of the time
where the time goes in v7:
time: 46.2 us; the launch traced here: 45.9 us
  starting transfers between devices  23.3 us (50%)
  Pallas kernels  13.6 us (29%)
  waiting for transfers between devices  6.22 us (13%)
  between operations  2.09 us (5%)
  local copies, waits for them, and re-layouts  0.7 us (2%)
    ppermute x2, starting transfers between devices, shifted(): lax.ppermute(value, axis, [(i, (i + by) % count) for i in range(count)])  6.93 us
    all_to_all x1, starting transfers between devices, per_device(): info = lax.all_to_all(info, AXES, split_axis=0, concat_axis=0, tiled=True)  6.66 us
    all_to_all x1, starting transfers between devices, per_device(): lax.all_to_all(sent, AXES, split_axis=0, concat_axis=0, tiled=True)  6.63 us
    all_to_all x1, waiting for transfers between devices, per_device(): lax.all_to_all(sent, AXES, split_axis=0, concat_axis=0, tiled=True)  4.74 us
    pallas_call x1, Pallas kernels, per_device(): call(everywhere, (f32(layers, rows, width), f32(row_total, reaches)), 10,...  4.18 us
    pallas_call x1, Pallas kernels, per_device(): call(inner, (f32(row_total, LANES), f32(row_total, LANES), f32(4, held, t...  3.64 us
    ppermute x2, starting transfers between devices, swapped(): return lax.ppermute(value, axis, list(enumerate(to)))  3.12 us
    pallas_call x1, Pallas kernels, per_device(): call(front, (edge, edge, f32(row_total, LANES)), 10, scratch=(pltpu.VMEM(...  1.93 us
  transfers between devices with their start and end apart: 6, of which 2 were waited for; matrix products, arithmetic and copies ran while one was open for 0% of the time, Pallas kernels for 21%

profile of v7, /device:TPU:1, one launch (start us, length us, event | category | flops | bytes accessed | tf_op | source)
XLA Modules:
  0.0 45.9 jit_solution(11618524011942708117)
XLA Ops:
  1.9 0.0 copy-start.1
  1.9 0.0 copy-start.2
  1.9 0.0 copy-start.3
  2.0 1.9 %shard_map.131 = (f32[4,10,8,128]{3,2,1,0:T(8,128)}, f32[4,10,8,128]{3,2,1,0:T(8,128)}, f32[256,128]{1,0:T(8,128)}) custom-call(f32[10,32,128]{2,1,0:T(8,128)} %head.7, f32[10,32,128]{2,1,0:T(8,128)} %cond.7, f32[10,32,128]{2,1,0:T(8,128)} %source.7, f32[10,32,128]{2,1,0:T(8,128)} %storage.7, s32[1,256]{1,0:T(1,128)} %reach.3, f32[1,256]{1,0:T(1,128)} %section.1, ...), custom_call_target="tpu_custom_call" | custom-call | bytes 3000000 | tf_op jit(solution)/shard_map/pallas_call | solution.py:469
  3.9 0.0 copy-start
  3.9 2.1 %collective-permute-start = (f32[4,10,8,128]{3,2,1,0:T(8,128)}, f32[4,10,8,128]{3,2,1,0:T(8,128)S(1)}, u32[]{:S(2)}, u32[]{:S(2)}) collective-permute-start(f32[4,10,8,128]{3,2,1,0:T(8,128)} %get-tuple-element.12), channel_id=1, source_target_pairs={{0,8},{8,16},{16,24},{24,32},{32,40},{40,48},{48,56},{56,64},{64,7... | collective-permute-start | bytes 491528 | tf_op jit(solution)/shard_map/ppermute | solution.py:441
  6.0 4.8 %collective-permute-start.1 = (f32[4,10,8,128]{3,2,1,0:T(8,128)}, f32[4,10,8,128]{3,2,1,0:T(8,128)S(1)}, u32[]{:S(2)}, u32[]{:S(2)}) collective-permute-start(f32[4,10,8,128]{3,2,1,0:T(8,128)} %get-tuple-element.13), channel_id=1, source_target_pairs={{0,120},{8,0},{16,8},{24,16},{32,24},{40,32},{48,40},{56,48},{64,5... | collective-permute-start | bytes 491528 | tf_op jit(solution)/shard_map/ppermute | solution.py:441
  10.8 6.7 %all-to-all-start = ((f32[128,2,128]{2,1,0:T(2,128)}), f32[128,2,128]{2,1,0:T(2,128)S(1)}, u32[]{:S(2)}, u32[]{:S(2)}) async-start(f32[128,2,128]{2,1,0:T(2,128)} %bitcast.13), calls=%async_computation | async-start | bytes 262144 | tf_op jit(solution)/shard_map/all_to_all | solution.py:486
  17.5 0.0 copy-start.5
  17.5 0.0 collective-permute-done.low
  17.5 0.0 collective-permute-done.1.high
  17.5 0.0 copy-done.1
  17.5 0.0 copy-done.2
  17.6 0.0 copy-done.3
  17.6 0.0 copy-done
  17.6 0.0 copy-start.6
  17.6 0.3 shard_map.132
  17.9 1.7 %collective-permute-start.2 = (f32[3,48,128]{2,1,0:T(8,128)S(1)}, f32[3,48,128]{2,1,0:T(8,128)S(1)}, u32[]{:S(2)}, u32[]{:S(2)}) collective-permute-start(f32[3,48,128]{2,1,0:T(8,128)S(1)} %get-tuple-element.14), channel_id=1, source_target_pairs={{0,7},{1,2},{2,1},{3,4},{4,3},{5,6},{6,5},{7,0},{8,15},{9,10},{10,... | collective-permute-start | bytes 221192 | tf_op jit(solution)/shard_map/ppermute | solution.py:449
  19.6 1.4 %collective-permute-start.3 = (f32[3,48,128]{2,1,0:T(8,128)S(1)}, f32[3,48,128]{2,1,0:T(8,128)S(1)}, u32[]{:S(2)}, u32[]{:S(2)}) collective-permute-start(f32[3,48,128]{2,1,0:T(8,128)S(1)} %get-tuple-element.15), channel_id=1, source_target_pairs={{0,1},{1,0},{2,3},{3,2},{4,5},{5,4},{6,7},{7,6},{8,9},{9,8},{10,11... | collective-permute-start | bytes 221192 | tf_op jit(solution)/shard_map/ppermute | solution.py:449
  21.0 0.0 copy-done.5
  21.0 3.6 %shard_map.134 = (f32[256,128]{1,0:T(8,128)S(1)}, f32[256,128]{1,0:T(8,128)S(1)}, f32[4,9,48,128]{3,2,1,0:T(8,128)S(1)}) custom-call(f32[10,32,128]{2,1,0:T(8,128)S(1)} %copy-done, f32[10,32,128]{2,1,0:T(8,128)S(1)} %copy-done.1, f32[10,32,128]{2,1,0:T(8,128)S(1)} %copy-done.2, f32[10,32,128]{2,1,0:T(8,128)S(1)} %copy-done.3, ...), custom_call_target="tpu_custom_call" | custom-call | bytes 9000000 | tf_op jit(solution)/shard_map/pallas_call | solution.py:497
  24.7 0.0 collective-permute-done.2.other_y
  24.7 0.0 collective-permute-done.3.one_y
  24.7 1.4 %shard_map.135.ends = f32[4,128]{1,0:T(4,128)S(1)} custom-call(f32[4,9,48,128]{3,2,1,0:T(8,128)S(1)} %get-tuple-element.18.strips, f32[3,48,128]{2,1,0:T(8,128)S(1)} %collective-permute-done.2.other_y, f32[3,48,128]{2,1,0:T(8,128)S(1)} %collective-permute-done.3.one_y), custom_call_target="tpu_custom_call" | custom-call | bytes 6000000 | tf_op jit(solution)/shard_map/pallas_call | solution.py:505
  26.1 1.5 %all-to-all-done = f32[128,2,128]{2,1,0:T(2,128)S(1)} async-done(((f32[128,2,128]{2,1,0:T(2,128)}), f32[128,2,128]{2,1,0:T(2,128)S(1)}, u32[]{:S(2)}, u32[]{:S(2)}) %all-to-all-start) | async-done | bytes 131104 | tf_op jit(solution)/shard_map/all_to_all | solution.py:486
  27.5 1.5 %shard_map.136 = f32[128,128]{1,0:T(8,128)} custom-call(f32[256,128]{1,0:T(8,128)S(1)} %get-tuple-element.17.found, f32[4,128]{1,0:T(4,128)S(1)} %shard_map.135.ends, s32[256,128]{1,0:T(8,128)S(1)} %bitcast.10, f32[256,128]{1,0:T(8,128)S(1)} %get-tuple-element.19.beds, f32[256,128]{1,0:T(8,128)S(1)} %bitcast.11), custom_call_target="tpu_custom_call" | custom-call | bytes 9000000 | tf_op jit(solution)/shard_map/pallas_call | solution.py:513
  29.0 6.6 %all-to-all-start.1 = ((f32[128,1,128]{2,1,0:T(1,128)}), f32[128,1,128]{2,1,0:T(1,128)S(1)}, u32[]{:S(2)}, u32[]{:S(2)}) async-start(f32[128,1,128]{2,1,0:T(1,128)} %bitcast.5), calls=%async_computation.1 | async-start | bytes 131072 | tf_op jit(solution)/shard_map/all_to_all | solution.py:524
  35.6 0.0 copy-start.7
  35.6 0.7 %copy-done.7 = s32[1,256]{1,0:T(1,128)S(1)} copy-done((s32[1,256]{1,0:T(1,128)S(1)}, s32[1,256]{1,0:T(1,128)}, u32[]{:S(2)}) %copy-start.7) | copy-done | bytes 1048
  36.3 4.2 %shard_map.133 = (f32[10,32,128]{2,1,0:T(8,128)}, f32[256,256]{1,0:T(8,128)S(1)}) custom-call(f32[10,32,128]{2,1,0:T(8,128)S(1)} %copy-done, f32[10,32,128]{2,1,0:T(8,128)S(1)} %copy-done.1, f32[10,32,128]{2,1,0:T(8,128)S(1)} %copy-done.2, f32[10,32,128]{2,1,0:T(8,128)S(1)} %copy-done.3, f32[4,10,8,128]{3,2,1,0:T(8,128)S(1)} %collective-permute-done.low, ...), custom_call_target="tpu_custom_call" | custom-call | bytes 15000000 | tf_op jit(solution)/shard_map/pallas_call | solution.py:525
  40.5 4.7 %all-to-all-done.1 = f32[128,1,128]{2,1,0:T(1,128)S(1)} async-done(((f32[128,1,128]{2,1,0:T(1,128)}), f32[128,1,128]{2,1,0:T(1,128)S(1)}, u32[]{:S(2)}, u32[]{:S(2)}) %all-to-all-start.1) | async-done | bytes 65568 | tf_op jit(solution)/shard_map/all_to_all | solution.py:524
  45.2 0.7 %shard_map.137 = f32[1,256]{1,0:T(1,128)} custom-call(f32[128,128]{1,0:T(8,128)S(1)} %bitcast.12, f32[256,256]{1,0:T(8,128)S(1)} %get-tuple-element.21.routed), custom_call_target="tpu_custom_call" | custom-call | bytes 3000000 | tf_op jit(solution)/shard_map/pallas_call | solution.py:539
  (3 shorter events, 0.0 us)
Async XLA Ops:
  1.9 15.6 %copy-start.1 = (f32[10,32,128]{2,1,0:T(8,128)S(1)}, f32[10,32,128]{2,1,0:T(8,128)}, u32[]{:S(2)}) copy-start(f32[10,32,128]{2,1,0:T(8,128)} %cond.7) | copy-start | bytes 491524
  1.9 15.6 %copy-start.2 = (f32[10,32,128]{2,1,0:T(8,128)S(1)}, f32[10,32,128]{2,1,0:T(8,128)}, u32[]{:S(2)}) copy-start(f32[10,32,128]{2,1,0:T(8,128)} %source.7) | copy-start | bytes 491524
  1.9 15.6 %copy-start.3 = (f32[10,32,128]{2,1,0:T(8,128)S(1)}, f32[10,32,128]{2,1,0:T(8,128)}, u32[]{:S(2)}) copy-start(f32[10,32,128]{2,1,0:T(8,128)} %storage.7) | copy-start | bytes 491524
  3.9 13.7 %copy-start = (f32[10,32,128]{2,1,0:T(8,128)S(1)}, f32[10,32,128]{2,1,0:T(8,128)}, u32[]{:S(2)}) copy-start(f32[10,32,128]{2,1,0:T(8,128)} %head.7) | copy-start | bytes 491524
  3.9 13.6 %collective-permute-start = (f32[4,10,8,128]{3,2,1,0:T(8,128)}, f32[4,10,8,128]{3,2,1,0:T(8,128)S(1)}, u32[]{:S(2)}, u32[]{:S(2)}) collective-permute-start(f32[4,10,8,128]{3,2,1,0:T(8,128)} %get-tuple-element.12), channel_id=1, source_target_pairs={{0,8},{8,16},{16,24},{24,32},{32,40},{40,48},{48,56},{56,64},{64,7... | collective-permute-start | bytes 491528 | tf_op jit(solution)/shard_map/ppermute | solution.py:441
  6.0 11.5 %collective-permute-start.1 = (f32[4,10,8,128]{3,2,1,0:T(8,128)}, f32[4,10,8,128]{3,2,1,0:T(8,128)S(1)}, u32[]{:S(2)}, u32[]{:S(2)}) collective-permute-start(f32[4,10,8,128]{3,2,1,0:T(8,128)} %get-tuple-element.13), channel_id=1, source_target_pairs={{0,120},{8,0},{16,8},{24,16},{32,24},{40,32},{48,40},{56,48},{64,5... | collective-permute-start | bytes 491528 | tf_op jit(solution)/shard_map/ppermute | solution.py:441
  10.8 16.7 %all-to-all-start = ((f32[128,2,128]{2,1,0:T(2,128)}), f32[128,2,128]{2,1,0:T(2,128)S(1)}, u32[]{:S(2)}, u32[]{:S(2)}) async-start(f32[128,2,128]{2,1,0:T(2,128)} %bitcast.13), calls=%async_computation | async-start | bytes 262144 | tf_op jit(solution)/shard_map/all_to_all | solution.py:486
  17.5 3.5 %copy-start.5 = (s32[1,256,128]{2,1,0:T(8,128)S(1)}, s32[1,256,128]{2,1,0:T(8,128)}, u32[]{:S(2)}) copy-start(s32[1,256,128]{2,1,0:T(8,128)} %param.17) | copy-start | bytes 393220
  17.6 3.4 %copy-start.6 = (f32[32,128]{1,0:T(8,128)S(1)}, f32[32,128]{1,0:T(8,128)}, u32[]{:S(2)}) copy-start(f32[32,128]{1,0:T(8,128)} %bed.1) | copy-start | bytes 49156
  17.9 6.8 %collective-permute-start.2 = (f32[3,48,128]{2,1,0:T(8,128)S(1)}, f32[3,48,128]{2,1,0:T(8,128)S(1)}, u32[]{:S(2)}, u32[]{:S(2)}) collective-permute-start(f32[3,48,128]{2,1,0:T(8,128)S(1)} %get-tuple-element.14), channel_id=1, source_target_pairs={{0,7},{1,2},{2,1},{3,4},{4,3},{5,6},{6,5},{7,0},{8,15},{9,10},{10,... | collective-permute-start | bytes 221192 | tf_op jit(solution)/shard_map/ppermute | solution.py:449
  19.6 5.1 %collective-permute-start.3 = (f32[3,48,128]{2,1,0:T(8,128)S(1)}, f32[3,48,128]{2,1,0:T(8,128)S(1)}, u32[]{:S(2)}, u32[]{:S(2)}) collective-permute-start(f32[3,48,128]{2,1,0:T(8,128)S(1)} %get-tuple-element.15), channel_id=1, source_target_pairs={{0,1},{1,0},{2,3},{3,2},{4,5},{5,4},{6,7},{7,6},{8,9},{9,8},{10,11... | collective-permute-start | bytes 221192 | tf_op jit(solution)/shard_map/ppermute | solution.py:449
  27.5 8.1 %copy-start.4 = (f32[1,256,256]{2,1,0:T(8,128)S(1)}, f32[1,256,256]{2,1,0:T(8,128)}, u32[]{:S(2)}) copy-start(f32[1,256,256]{2,1,0:T(8,128)} %route.1) | copy-start | bytes 786436
  29.0 16.2 %all-to-all-start.1 = ((f32[128,1,128]{2,1,0:T(1,128)}), f32[128,1,128]{2,1,0:T(1,128)S(1)}, u32[]{:S(2)}, u32[]{:S(2)}) async-start(f32[128,1,128]{2,1,0:T(1,128)} %bitcast.5), calls=%async_computation.1 | async-start | bytes 131072 | tf_op jit(solution)/shard_map/all_to_all | solution.py:524
  35.6 0.7 %copy-start.7 = (s32[1,256]{1,0:T(1,128)S(1)}, s32[1,256]{1,0:T(1,128)}, u32[]{:S(2)}) copy-start(s32[1,256]{1,0:T(1,128)} %reach.3) | copy-start | bytes 3076

commit v8 on v6

--- a/solution.py
+++ b/solution.py
@@ -383,6 +383,14 @@
         send_out[g * 8 : (g + 1) * 8, :] = jnp.where(eight == 2, column, sums[g])
 
 
+def edge_leaks(
+    layers, strips, other_y, one_y, found, cells, beds, info,
+    send_out, heads, coef, conds, sides, ends, weights, levels, leaks,
+):
+    edges(layers, strips, other_y, one_y, ends, heads, coef, conds, sides)
+    leak_rows(found, ends, cells, beds, info, send_out, weights, levels, leaks)
+
+
 def everywhere(
     head, cond, source, storage, low, high, other_y, one_y, reach, route,
     field_out, routed_out, heads, coef, conds, lines, sides,
@@ -497,25 +505,21 @@
         mib=16,
         micros=3,
     )(*fields, *pair_x, cells, bed_conduct)
-    ends = call(
-        functools.partial(edges, layers),
-        f32(rows // 8, LANES),
-        3,
-        scratch=(*own, sides),
-        mib=16,
-        micros=2,
-    )(strips, *pair_y)
     sent = call(
-        leak_rows,
+        functools.partial(edge_leaks, layers),
         f32(row_total // 2, LANES),
-        5,
+        7,
         scratch=(
+            *own,
+            sides,
+            scratch(rows // 8, LANES),
             scratch(2, row_total // 2, LANES),
             scratch(2, row_total, LANES),
             scratch(row_total, LANES),
         ),
-        micros=3,
-    )(found, ends, cells, beds, info)
+        mib=16,
+        micros=5,
+    )(strips, *pair_y, found, cells, beds, info)
     arrived = lax.all_to_all(sent, AXES, split_axis=0, concat_axis=0, tiled=True)
     head_field, routed = call(
         everywhere,

time: 46.2 us -> 47.1 us (1.019)
  waiting for transfers between devices: 6.14 us -> 7.58 us
  starting transfers between devices: 23.4 us -> 22 us
  Pallas kernels: 13.7 us -> 14.6 us
    all_to_all x1, waiting for transfers between devices: 1.39 us -> 2.84 us  [per_device(): info = lax.all_to_all(info, AXES, split_axis=0, concat_axis=0, tiled=True)]
    all_to_all x1, starting transfers between devices: 6.7 us -> 5.26 us  [per_device(): lax.all_to_all(sent, AXES, split_axis=0, concat_axis=0, tiled=True)]
    pallas_call x2 -> x1, Pallas kernels: 2.88 us -> 3.77 us  [per_device(): call(functools.partial(edge_leaks, layers), f32(row_total // 2, LANES), 7...]
  transfers between devices with their start and end apart: 6 -> 6, of which waited for: 2 -> 2; matrix products, arithmetic and copies ran while one was open for 0% -> 0% of each run, Pallas kernels for 21% -> 17%
where the time goes in v8:
time: 47.1 us; the launch traced here: 46.9 us
  starting transfers between devices  22 us (47%)
  Pallas kernels  14.6 us (31%)
  waiting for transfers between devices  7.58 us (16%)
  between operations  2.08 us (4%)
  local copies, waits for them, and re-layouts  0.7 us (1%)
    ppermute x2, starting transfers between devices, shifted(): lax.ppermute(value, axis, [(i, (i + by) % count) for i in range(count)])  6.93 us
    all_to_all x1, starting transfers between devices, per_device(): info = lax.all_to_all(info, AXES, split_axis=0, concat_axis=0, tiled=True)  6.66 us
    all_to_all x1, starting transfers between devices, per_device(): lax.all_to_all(sent, AXES, split_axis=0, concat_axis=0, tiled=True)  5.26 us
    all_to_all x1, waiting for transfers between devices, per_device(): lax.all_to_all(sent, AXES, split_axis=0, concat_axis=0, tiled=True)  4.73 us
    pallas_call x1, Pallas kernels, per_device(): call(everywhere, (f32(layers, rows, width), f32(row_total, reaches)), 10,...  4.2 us
    pallas_call x1, Pallas kernels, per_device(): call(functools.partial(edge_leaks, layers), f32(row_total // 2, LANES), 7...  3.77 us
    pallas_call x1, Pallas kernels, per_device(): call(inner, (f32(row_total, LANES), f32(row_total, LANES), f32(4, held, t...  3.65 us
    ppermute x2, starting transfers between devices, swapped(): return lax.ppermute(value, axis, list(enumerate(to)))  3.12 us
  transfers between devices with their start and end apart: 6, of which 2 were waited for; matrix products, arithmetic and copies ran while one was open for 0% of the time, Pallas kernels for 17%

profile of v8, /device:TPU:1, one launch (start us, length us, event | category | flops | bytes accessed | tf_op | source)
XLA Modules:
  0.0 46.9 jit_solution(5525740605511660088)
XLA Ops:
  1.9 0.0 copy-start.1
  1.9 0.0 copy-start.2
  1.9 0.0 copy-start.3
  2.0 1.9 %shard_map.131 = (f32[4,10,8,128]{3,2,1,0:T(8,128)}, f32[4,10,8,128]{3,2,1,0:T(8,128)}, f32[256,128]{1,0:T(8,128)}) custom-call(f32[10,32,128]{2,1,0:T(8,128)} %head.7, f32[10,32,128]{2,1,0:T(8,128)} %cond.7, f32[10,32,128]{2,1,0:T(8,128)} %source.7, f32[10,32,128]{2,1,0:T(8,128)} %storage.7, s32[1,256]{1,0:T(1,128)} %reach.3, f32[1,256]{1,0:T(1,128)} %section.1, ...), custom_call_target="tpu_custom_call" | custom-call | bytes 3000000 | tf_op jit(solution)/shard_map/pallas_call | solution.py:472
  3.9 0.0 copy-start
  3.9 2.1 %collective-permute-start = (f32[4,10,8,128]{3,2,1,0:T(8,128)}, f32[4,10,8,128]{3,2,1,0:T(8,128)S(1)}, u32[]{:S(2)}, u32[]{:S(2)}) collective-permute-start(f32[4,10,8,128]{3,2,1,0:T(8,128)} %get-tuple-element.12), channel_id=1, source_target_pairs={{0,8},{8,16},{16,24},{24,32},{32,40},{40,48},{48,56},{56,64},{64,7... | collective-permute-start | bytes 491528 | tf_op jit(solution)/shard_map/ppermute | solution.py:444
  6.0 4.8 %collective-permute-start.1 = (f32[4,10,8,128]{3,2,1,0:T(8,128)}, f32[4,10,8,128]{3,2,1,0:T(8,128)S(1)}, u32[]{:S(2)}, u32[]{:S(2)}) collective-permute-start(f32[4,10,8,128]{3,2,1,0:T(8,128)} %get-tuple-element.13), channel_id=1, source_target_pairs={{0,120},{8,0},{16,8},{24,16},{32,24},{40,32},{48,40},{56,48},{64,5... | collective-permute-start | bytes 491528 | tf_op jit(solution)/shard_map/ppermute | solution.py:444
  10.8 6.7 %all-to-all-start = ((f32[128,2,128]{2,1,0:T(2,128)}), f32[128,2,128]{2,1,0:T(2,128)S(1)}, u32[]{:S(2)}, u32[]{:S(2)}) async-start(f32[128,2,128]{2,1,0:T(2,128)} %bitcast.13), calls=%async_computation | async-start | bytes 262144 | tf_op jit(solution)/shard_map/all_to_all | solution.py:489
  17.5 0.0 copy-start.5
  17.5 0.0 collective-permute-done.low
  17.5 0.0 collective-permute-done.1.high
  17.5 0.0 copy-done.1
  17.5 0.0 copy-done.2
  17.6 0.0 copy-done.3
  17.6 0.0 copy-done
  17.6 0.0 copy-start.6
  17.6 0.3 shard_map.132
  17.9 1.7 %collective-permute-start.2 = (f32[3,48,128]{2,1,0:T(8,128)S(1)}, f32[3,48,128]{2,1,0:T(8,128)S(1)}, u32[]{:S(2)}, u32[]{:S(2)}) collective-permute-start(f32[3,48,128]{2,1,0:T(8,128)S(1)} %get-tuple-element.14), channel_id=1, source_target_pairs={{0,7},{1,2},{2,1},{3,4},{4,3},{5,6},{6,5},{7,0},{8,15},{9,10},{10,... | collective-permute-start | bytes 221192 | tf_op jit(solution)/shard_map/ppermute | solution.py:452
  19.6 1.4 %collective-permute-start.3 = (f32[3,48,128]{2,1,0:T(8,128)S(1)}, f32[3,48,128]{2,1,0:T(8,128)S(1)}, u32[]{:S(2)}, u32[]{:S(2)}) collective-permute-start(f32[3,48,128]{2,1,0:T(8,128)S(1)} %get-tuple-element.15), channel_id=1, source_target_pairs={{0,1},{1,0},{2,3},{3,2},{4,5},{5,4},{6,7},{7,6},{8,9},{9,8},{10,11... | collective-permute-start | bytes 221192 | tf_op jit(solution)/shard_map/ppermute | solution.py:452
  21.0 0.0 copy-done.5
  21.0 0.0 copy-done.6
  21.0 3.6 %shard_map.134 = (f32[256,128]{1,0:T(8,128)S(1)}, f32[256,128]{1,0:T(8,128)S(1)}, f32[4,9,48,128]{3,2,1,0:T(8,128)S(1)}) custom-call(f32[10,32,128]{2,1,0:T(8,128)S(1)} %copy-done, f32[10,32,128]{2,1,0:T(8,128)S(1)} %copy-done.1, f32[10,32,128]{2,1,0:T(8,128)S(1)} %copy-done.2, f32[10,32,128]{2,1,0:T(8,128)S(1)} %copy-done.3, ...), custom_call_target="tpu_custom_call" | custom-call | bytes 9000000 | tf_op jit(solution)/shard_map/pallas_call | solution.py:500
  24.7 2.8 %all-to-all-done = f32[128,2,128]{2,1,0:T(2,128)S(1)} async-done(((f32[128,2,128]{2,1,0:T(2,128)}), f32[128,2,128]{2,1,0:T(2,128)S(1)}, u32[]{:S(2)}, u32[]{:S(2)}) %all-to-all-start) | async-done | bytes 131104 | tf_op jit(solution)/shard_map/all_to_all | solution.py:489
  27.5 0.0 collective-permute-done.2.other_y
  27.5 0.0 collective-permute-done.3.one_y
  27.5 3.8 %shard_map.135 = f32[128,128]{1,0:T(8,128)} custom-call(f32[4,9,48,128]{3,2,1,0:T(8,128)S(1)} %get-tuple-element.17.strips, f32[3,48,128]{2,1,0:T(8,128)S(1)} %collective-permute-done.2.other_y, f32[3,48,128]{2,1,0:T(8,128)S(1)} %collective-permute-done.3.one_y, f32[256,128]{1,0:T(8,128)S(1)} %get-tuple-element.18.found, s32[256,128]{1,0:T(8,128)S(1)} %bitcast.10, ...), custom_call_target="tpu_custom_call" | custom-call | bytes 15000000 | tf_op jit(solution)/shard_map/pallas_call | solution.py:508
  31.3 5.3 %all-to-all-start.1 = ((f32[128,1,128]{2,1,0:T(1,128)}), f32[128,1,128]{2,1,0:T(1,128)S(1)}, u32[]{:S(2)}, u32[]{:S(2)}) async-start(f32[128,1,128]{2,1,0:T(1,128)} %bitcast.5), calls=%async_computation.1 | async-start | bytes 131072 | tf_op jit(solution)/shard_map/all_to_all | solution.py:523
  36.6 0.0 copy-start.7
  36.6 0.7 %copy-done.7 = s32[1,256]{1,0:T(1,128)S(1)} copy-done((s32[1,256]{1,0:T(1,128)S(1)}, s32[1,256]{1,0:T(1,128)}, u32[]{:S(2)}) %copy-start.7) | copy-done | bytes 1048
  37.3 4.2 %shard_map.133 = (f32[10,32,128]{2,1,0:T(8,128)}, f32[256,256]{1,0:T(8,128)S(1)}) custom-call(f32[10,32,128]{2,1,0:T(8,128)S(1)} %copy-done, f32[10,32,128]{2,1,0:T(8,128)S(1)} %copy-done.1, f32[10,32,128]{2,1,0:T(8,128)S(1)} %copy-done.2, f32[10,32,128]{2,1,0:T(8,128)S(1)} %copy-done.3, f32[4,10,8,128]{3,2,1,0:T(8,128)S(1)} %collective-permute-done.low, ...), custom_call_target="tpu_custom_call" | custom-call | bytes 15000000 | tf_op jit(solution)/shard_map/pallas_call | solution.py:524
  41.4 4.7 %all-to-all-done.1 = f32[128,1,128]{2,1,0:T(1,128)S(1)} async-done(((f32[128,1,128]{2,1,0:T(1,128)}), f32[128,1,128]{2,1,0:T(1,128)S(1)}, u32[]{:S(2)}, u32[]{:S(2)}) %all-to-all-start.1) | async-done | bytes 65568 | tf_op jit(solution)/shard_map/all_to_all | solution.py:523
  46.2 0.7 %shard_map.136 = f32[1,256]{1,0:T(1,128)} custom-call(f32[128,128]{1,0:T(8,128)S(1)} %bitcast.12, f32[256,256]{1,0:T(8,128)S(1)} %get-tuple-element.21.routed), custom_call_target="tpu_custom_call" | custom-call | bytes 3000000 | tf_op jit(solution)/shard_map/pallas_call | solution.py:538
  (2 shorter events, 0.0 us)
Async XLA Ops:
  1.9 15.6 %copy-start.1 = (f32[10,32,128]{2,1,0:T(8,128)S(1)}, f32[10,32,128]{2,1,0:T(8,128)}, u32[]{:S(2)}) copy-start(f32[10,32,128]{2,1,0:T(8,128)} %cond.7) | copy-start | bytes 491524
  1.9 15.6 %copy-start.2 = (f32[10,32,128]{2,1,0:T(8,128)S(1)}, f32[10,32,128]{2,1,0:T(8,128)}, u32[]{:S(2)}) copy-start(f32[10,32,128]{2,1,0:T(8,128)} %source.7) | copy-start | bytes 491524
  1.9 15.6 %copy-start.3 = (f32[10,32,128]{2,1,0:T(8,128)S(1)}, f32[10,32,128]{2,1,0:T(8,128)}, u32[]{:S(2)}) copy-start(f32[10,32,128]{2,1,0:T(8,128)} %storage.7) | copy-start | bytes 491524
  3.9 13.7 %copy-start = (f32[10,32,128]{2,1,0:T(8,128)S(1)}, f32[10,32,128]{2,1,0:T(8,128)}, u32[]{:S(2)}) copy-start(f32[10,32,128]{2,1,0:T(8,128)} %head.7) | copy-start | bytes 491524
  3.9 13.6 %collective-permute-start = (f32[4,10,8,128]{3,2,1,0:T(8,128)}, f32[4,10,8,128]{3,2,1,0:T(8,128)S(1)}, u32[]{:S(2)}, u32[]{:S(2)}) collective-permute-start(f32[4,10,8,128]{3,2,1,0:T(8,128)} %get-tuple-element.12), channel_id=1, source_target_pairs={{0,8},{8,16},{16,24},{24,32},{32,40},{40,48},{48,56},{56,64},{64,7... | collective-permute-start | bytes 491528 | tf_op jit(solution)/shard_map/ppermute | solution.py:444
  6.0 11.5 %collective-permute-start.1 = (f32[4,10,8,128]{3,2,1,0:T(8,128)}, f32[4,10,8,128]{3,2,1,0:T(8,128)S(1)}, u32[]{:S(2)}, u32[]{:S(2)}) collective-permute-start(f32[4,10,8,128]{3,2,1,0:T(8,128)} %get-tuple-element.13), channel_id=1, source_target_pairs={{0,120},{8,0},{16,8},{24,16},{32,24},{40,32},{48,40},{56,48},{64,5... | collective-permute-start | bytes 491528 | tf_op jit(solution)/shard_map/ppermute | solution.py:444
  10.8 16.7 %all-to-all-start = ((f32[128,2,128]{2,1,0:T(2,128)}), f32[128,2,128]{2,1,0:T(2,128)S(1)}, u32[]{:S(2)}, u32[]{:S(2)}) async-start(f32[128,2,128]{2,1,0:T(2,128)} %bitcast.13), calls=%async_computation | async-start | bytes 262144 | tf_op jit(solution)/shard_map/all_to_all | solution.py:489
  17.5 3.5 %copy-start.5 = (s32[1,256,128]{2,1,0:T(8,128)S(1)}, s32[1,256,128]{2,1,0:T(8,128)}, u32[]{:S(2)}) copy-start(s32[1,256,128]{2,1,0:T(8,128)} %param.17) | copy-start | bytes 393220
  17.6 3.4 %copy-start.6 = (f32[32,128]{1,0:T(8,128)S(1)}, f32[32,128]{1,0:T(8,128)}, u32[]{:S(2)}) copy-start(f32[32,128]{1,0:T(8,128)} %bed.1) | copy-start | bytes 49156
  17.9 9.6 %collective-permute-start.2 = (f32[3,48,128]{2,1,0:T(8,128)S(1)}, f32[3,48,128]{2,1,0:T(8,128)S(1)}, u32[]{:S(2)}, u32[]{:S(2)}) collective-permute-start(f32[3,48,128]{2,1,0:T(8,128)S(1)} %get-tuple-element.14), channel_id=1, source_target_pairs={{0,7},{1,2},{2,1},{3,4},{4,3},{5,6},{6,5},{7,0},{8,15},{9,10},{10,... | collective-permute-start | bytes 221192 | tf_op jit(solution)/shard_map/ppermute | solution.py:452
  19.6 7.9 %collective-permute-start.3 = (f32[3,48,128]{2,1,0:T(8,128)S(1)}, f32[3,48,128]{2,1,0:T(8,128)S(1)}, u32[]{:S(2)}, u32[]{:S(2)}) collective-permute-start(f32[3,48,128]{2,1,0:T(8,128)S(1)} %get-tuple-element.15), channel_id=1, source_target_pairs={{0,1},{1,0},{2,3},{3,2},{4,5},{5,4},{6,7},{7,6},{8,9},{9,8},{10,11... | collective-permute-start | bytes 221192 | tf_op jit(solution)/shard_map/ppermute | solution.py:452
  27.5 9.1 %copy-start.4 = (f32[1,256,256]{2,1,0:T(8,128)S(1)}, f32[1,256,256]{2,1,0:T(8,128)}, u32[]{:S(2)}) copy-start(f32[1,256,256]{2,1,0:T(8,128)} %route.1) | copy-start | bytes 786436
  31.3 14.9 %all-to-all-start.1 = ((f32[128,1,128]{2,1,0:T(1,128)}), f32[128,1,128]{2,1,0:T(1,128)S(1)}, u32[]{:S(2)}, u32[]{:S(2)}) async-start(f32[128,1,128]{2,1,0:T(1,128)} %bitcast.5), calls=%async_computation.1 | async-start | bytes 131072 | tf_op jit(solution)/shard_map/all_to_all | solution.py:523
  36.6 0.7 %copy-start.7 = (s32[1,256]{1,0:T(1,128)S(1)}, s32[1,256]{1,0:T(1,128)}, u32[]{:S(2)}) copy-start(s32[1,256]{1,0:T(1,128)} %reach.3) | copy-start | bytes 3076
